TPU v7x, 512 devices: a whole 4x4x16 slice. The times are simulated.
512 devices in a mesh: sec: 2 (over core), dp: 64 (over x, z_hi, y), mp: 4 (over z_lo).
Axes of the slice: x: 4, y: 4, z: 16 (z_hi: 4, z_lo: 4; z = z_hi * 4 + z_lo), core: 2. Of those that a mesh axis runs over, the one named last changes fastest.
Arguments:
- states: bfloat16 [2, 32768, 896], P('sec', 'dp'), may hold values from -16 to 16
- proj_weights: bfloat16 [2, 896, 2, 2048], P('sec', None, None, 'mp'), may hold values from -0.1875 to 0.1875
- queries: bfloat16 [8192, 2048], P('dp', 'mp'), may hold values from -6 to 6
- out_grad: bfloat16 [8192, 2048], P('dp', 'mp'), may hold values from -24 to 24
- logsumexp: float32 [16, 8192], P('mp', 'dp'), may hold values from 3 to 5
- delta: float32 [16, 8192], P('mp', 'dp'), may hold values from -96 to 96
- span_blocks: int32 [128, 2], P('dp'), may hold values from 0 to 3, all different within a row
Outputs:
- row_grads: bfloat16 [2, 32768, 896], P('sec', ('dp', 'mp'))
- weight_grads: float32 [2, 896, 2, 2048], P('sec', 'dp', None, 'mp')
Inputs may be any that keep to these rules, and one draw needn't show every extreme that they name: `span_blocks`: the two blocks of a span differ, and each block number occurs in some row.
All inputs are finite; a program needn't handle non-finite values.
Results may differ from a plain program's by a relative error of at most 0.022.
Values may be sent and summed in bfloat16 or wider, within the bound.
No kernel may reach another device: no remote copies, remote signals or barrier semaphores. Data moves between devices by JAX's collectives and lax.ppermute only.
A program may use at most 64 MiB of HBM per device.

v0:
```python
import jax
import jax.numpy as jnp
from jax import lax
from jax.sharding import PartitionSpec as P

HEAD_DIM = 128
SPAN = 64
NEIGH_LEN = 128


def shifted(value, axis, steps):
    count = lax.axis_size(axis)
    first, last = (max(0, -steps), min(count, count - steps))
    return lax.ppermute(value, axis, [(source, source + steps) for source in range(first, last)])


def gelu_value(pre_act):
    inner = 0.7978845608 * (pre_act + 0.044715 * pre_act * pre_act * pre_act)
    return 0.5 * pre_act * (1.0 + jnp.tanh(inner))


def gelu_slope(pre_act):
    inner = 0.7978845608 * (pre_act + 0.044715 * pre_act * pre_act * pre_act)
    tangent = jnp.tanh(inner)
    return 0.5 * (1.0 + tangent) + 0.5 * pre_act * (1.0 - tangent * tangent) * 0.7978845608 * (
        1.0 + 0.134145 * pre_act * pre_act
    )


def shards(states, proj_weights, queries, out_grad, logsumexp, delta, span_blocks):
    mp_parts = lax.axis_size("mp")
    layer_rows = states[0]
    local_rows = layer_rows.shape[0]
    half_cols = proj_weights.shape[3]
    weights = proj_weights[0].reshape(proj_weights.shape[1], 2 * half_cols)
    spans = span_blocks.shape[0]
    blocks = 2 * spans
    heads_here = half_cols // HEAD_DIM
    score_scale = HEAD_DIM ** (-0.5)
    is_decoder = lax.axis_index("sec") == 0
    select = span_blocks.reshape(-1)[:, None] == jnp.arange(blocks, dtype=jnp.int32)[None, :]

    def decoder_branch():
        key_values = jnp.dot(layer_rows, weights, preferred_element_type=jnp.float32).astype(
            jnp.bfloat16
        )
        kv_blocks = key_values.reshape(blocks, NEIGH_LEN * 2 * half_cols)
        kv_slots = jnp.dot(
            select.astype(jnp.bfloat16), kv_blocks, preferred_element_type=jnp.float32
        ).astype(jnp.bfloat16)
        kv_slots = kv_slots.reshape(spans, 2 * NEIGH_LEN, 2, heads_here, HEAD_DIM)
        key_rows = kv_slots[:, :, 0]
        value_rows = kv_slots[:, :, 1]
        query_rows = queries.reshape(spans, SPAN, heads_here, HEAD_DIM)
        grad_rows = out_grad.reshape(spans, SPAN, heads_here, HEAD_DIM)
        row_stats = logsumexp.reshape(heads_here, spans, SPAN).transpose(1, 0, 2)
        row_delta = delta.reshape(heads_here, spans, SPAN).transpose(1, 0, 2)
        scores = (
            jnp.einsum("cqhd,ckhd->chqk", query_rows, key_rows, preferred_element_type=jnp.float32)
            * score_scale
        )
        attn_probs = jnp.exp(scores - row_stats[..., None])
        probs_low = attn_probs.astype(jnp.bfloat16)
        slot_vgrad = jnp.einsum(
            "chqk,cqhd->ckhd", probs_low, grad_rows, preferred_element_type=jnp.float32
        )
        grad_probs = jnp.einsum(
            "cqhd,ckhd->chqk", grad_rows, value_rows, preferred_element_type=jnp.float32
        )
        grad_scores = (attn_probs * (grad_probs - row_delta[..., None])).astype(jnp.bfloat16)
        slot_kgrad = score_scale * jnp.einsum(
            "chqk,cqhd->ckhd", grad_scores, query_rows, preferred_element_type=jnp.float32
        )
        slot_grads = jnp.stack([slot_kgrad, slot_vgrad], axis=2).reshape(
            blocks, NEIGH_LEN * 2 * half_cols
        )
        block_grads = jnp.einsum(
            "sb,sx->bx", select.astype(jnp.float32), slot_grads, precision=lax.Precision.HIGHEST
        )
        block_grads = block_grads.astype(jnp.bfloat16).reshape(local_rows, 2 * half_cols)
        enc_part = jnp.einsum("rc,ec->re", block_grads, weights, preferred_element_type=jnp.float32)
        return (block_grads, enc_part)

    def decoder_spare():
        return (
            jnp.zeros((local_rows, 2 * half_cols), jnp.bfloat16),
            jnp.zeros((local_rows, layer_rows.shape[1]), jnp.float32),
        )

    block_grads, enc_part = lax.cond(is_decoder, decoder_branch, decoder_spare)
    quarter = local_rows // mp_parts
    row_start = lax.axis_index("mp") * quarter
    enc_grads = lax.psum(enc_part.astype(jnp.bfloat16), "mp")
    enc_share = lax.dynamic_slice_in_dim(enc_grads, row_start, quarter, 0)
    arrived = shifted(enc_grads, "sec", 1)

    def encoder_branch():
        up_piece = weights[:, :half_cols]
        pre_act = jnp.dot(layer_rows, up_piece, preferred_element_type=jnp.float32)
        hidden = gelu_value(pre_act).astype(jnp.bfloat16)
        grad_hidden = jnp.dot(arrived, weights[:, half_cols:], preferred_element_type=jnp.float32)
        grad_pre = (grad_hidden * gelu_slope(pre_act)).astype(jnp.bfloat16)
        input_part = jnp.einsum("rf,ef->re", grad_pre, up_piece, preferred_element_type=jnp.float32)
        return (grad_pre, hidden, input_part)

    def encoder_spare():
        empty_cols = jnp.zeros((local_rows, half_cols), jnp.bfloat16)
        return (empty_cols, empty_cols, jnp.zeros((local_rows, layer_rows.shape[1]), jnp.float32))

    grad_pre, hidden, input_part = lax.cond(is_decoder, encoder_spare, encoder_branch)
    input_whole = lax.psum(input_part.astype(jnp.bfloat16), "mp")
    input_share = lax.dynamic_slice_in_dim(input_whole, row_start, quarter, 0)
    row_part = jnp.where(is_decoder, enc_share, input_share)[None]
    right_one = jnp.where(is_decoder, block_grads[:, :half_cols], grad_pre)
    left_two = jnp.where(is_decoder, layer_rows, arrived)
    right_two = jnp.where(is_decoder, block_grads[:, half_cols:], hidden)
    first_term = jnp.einsum("rk,rf->kf", layer_rows, right_one, preferred_element_type=jnp.float32)
    second_term = jnp.einsum("rk,rf->kf", left_two, right_two, preferred_element_type=jnp.float32)
    summed = lax.psum_scatter(
        jnp.concatenate([first_term, second_term], axis=1), "dp", scatter_dimension=0, tiled=True
    )
    weight_part = (summed / lax.axis_size("dp")).reshape(1, summed.shape[0], 2, half_cols)
    return (row_part, weight_part)


def solution(mesh):
    in_specs = (
        P("sec", "dp", None),
        P("sec", None, None, "mp"),
        P("dp", "mp"),
        P("dp", "mp"),
        P("mp", "dp"),
        P("mp", "dp"),
        P("dp", None),
    )
    out_specs = (P("sec", ("dp", "mp"), None), P("sec", "dp", None, "mp"))
    return jax.shard_map(shards, mesh=mesh, in_specs=in_specs, out_specs=out_specs, check_vma=False)
```

profile of v0, /device:TPU:32, one launch (start us, length us, event | category | flops | bytes accessed | tf_op | source)
XLA Modules:
  0.0 1063.6 jit_solution(7626560260171648171)
XLA Ops:
  7.2 0.0 all-reduce.5.cloned.1.call-start
  7.2 0.0 copy-start
  7.2 0.0 copy-start.3
  7.2 0.0 copy-start.4
  7.3 0.0 copy-start.5
  7.3 0.0 copy-start.6
  7.3 0.0 copy-start.7
  7.3 3.3 copy.43
  10.6 21.7 %conditional.2 = (bf16[512,896]{1,0:T(8,128)(2,1)}, bf16[512,512]{1,0:T(8,128)(2,1)}, bf16[512,512]{1,0:T(8,128)(2,1)}) conditional(s32[]{:T(128)} %convert_element_type.37, () %tuple.30, (s32[2,2]{1,0:T(2,128)S(1)}, s32[4,4]{1,0:T(4,128)S(1)}, bf16[512,896]{1,0:T(8,128)(2,1)S(1)}, bf16[896,1024]{1,0:T(8,128)(2,1)}, bf16[128,512]{1,0:T(8,128)(2,1)S(1)}, ...), branch_computations={%region_0.0_spmd, %region_1.0_spmd} | conditional | flops 2045771776 | bytes 41701592 | solution.py:90
  10.7 2.8 convolution_convert_fusion.2
  13.4 0.8 reshape.33
  14.2 0.1 eq.19
  14.3 0.8 convolution_convert_fusion.1
  15.1 1.1 reshape.34
  16.1 0.4 fusion.33
  16.5 0.1 reshape.36
  16.6 0.3 fusion.3
  17.0 0.3 convolution_bitcast_fusion
  17.3 0.1 reshape.38
  17.4 0.6 fusion
  18.0 0.1 pad_maximum_fusion
  18.1 2.7 copy.37
  20.8 3.0 reshape.39
  23.8 2.8 convolution_convert_fusion
  26.6 0.9 reshape.40
  27.5 3.7 fusion.34
  31.2 1.1 fusion.32
  32.3 0.0 all-reduce.5.cloned.1.call-update
  32.3 0.0 all-reduce.7.cloned.1.call-start
  32.4 73.1 %all-reduce.5.cloned.1.call-done = bf16[512,896]{1,0:T(8,128)(2,1)} async-done(((bf16[512,896]{1,0:T(8,128)(2,1)}), bf16[512,896]{1,0:T(8,128)(2,1)}) %all-reduce.5.cloned.1.call-update) | async-done | bytes 917520 | tf_op jit(solution)/shard_map/psum | solution.py:93
  105.5 1.8 collective-permute-start
  107.3 2.2 collective-permute-done
  109.6 0.2 conditional.3
  109.7 0.1 broadcast.49
  109.8 0.9 copy-done.2
  110.7 0.0 all-reduce.7.cloned.1.call-update
  110.7 0.0 all-reduce.9.cloned.1.call-start
  110.7 0.0 copy-start.1
  110.7 2.2 convolution_bitcast_fusion.1
  112.9 1.8 fusion.23
  114.7 2.1 pad_maximum_fusion.1
  116.8 0.0 all-reduce.9.cloned.1.call-update
  116.9 1.3 dynamic-slice
  118.8 68.0 %all-reduce.7.cloned.1.call-done = bf16[512,896]{1,0:T(8,128)(2,1)} async-done(((bf16[512,896]{1,0:T(8,128)(2,1)}), bf16[512,896]{1,0:T(8,128)(2,1)}) %all-reduce.7.cloned.1.call-update) | async-done | bytes 917520 | tf_op jit(solution)/shard_map/psum | solution.py:111
  186.7 1.8 select_bitcast_fusion
  188.5 866.3 %all-reduce.9.cloned.1.call-done = f32[896,1024]{0,1:T(8,128)} async-done(((f32[896,1024]{0,1:T(8,128)}), f32[896,1024]{0,1:T(8,128)}) %all-reduce.9.cloned.1.call-update) | async-done | bytes 3670032
  1054.9 1.4 dynamic-slice_multiply_fusion
  1056.3 0.8 copy.38
  (15 shorter events, 0.2 us)
Async XLA Ops:
  7.2 98.3 %all-reduce.5.cloned.1.call-start = ((), (), s32[]{:S(2)}) async-start(), calls=%async_computation | async-start | bytes 1835008 | tf_op jit(solution)/shard_map/psum | solution.py:93
  7.2 3.4 copy-start
  7.2 3.4 copy-start.3
  7.2 3.4 copy-start.4
  7.3 3.4 copy-start.5
  7.3 3.4 copy-start.6
  7.3 3.4 copy-start.7
  32.3 154.4 %all-reduce.7.cloned.1.call-start = ((), (), s32[]{:S(2)}) async-start(), calls=%async_computation.1 | async-start | bytes 1835008 | tf_op jit(solution)/shard_map/psum | solution.py:111
  105.5 4.1 collective-permute-start
  109.7 0.9 copy-start.2
  110.7 944.2 %all-reduce.9.cloned.1.call-start = ((), (), s32[]{:S(2)}) async-start(), calls=%async_computation.2 | async-start | bytes 7340032
  110.7 2.2 copy-start.1
Sparse Core Ops, SparseCore 0:
  32.5 72.9 all-reduce.4
  110.8 75.8 all-reduce.6
  189.6 865.1 all-reduce.8
where the time goes:
time: 1060 us
  waiting for transfers between devices  1010 us (95%)
  local copies, waits for them, and re-layouts  16.6 us (2%)
  matrix products  15.3 us (1%)
  between operations  14.6 us (1%)
    unnamed x4, waiting for transfers between devices  866 us
    psum x1, waiting for transfers between devices, shards(): enc_grads = lax.psum(enc_part.astype(jnp.bfloat16), 'mp')  73.1 us
    psum x1, waiting for transfers between devices, shards(): input_whole = lax.psum(input_part.astype(jnp.bfloat16), 'mp')  68 us
  transfers between devices with their start and end apart: 4, of which 4 were waited for; matrix products, arithmetic and copies ran while one was open for 1% of the time, Pallas kernels for 0%

commit v1 on v0

v1 whole, which is shorter than its diff:
```python
import jax
import jax.numpy as jnp
from jax import lax
from jax.experimental import pallas as pl
from jax.experimental.pallas import tpu as pltpu
from jax.sharding import Mesh
from jax.sharding import PartitionSpec as P

HEAD_DIM = 128
SPAN = 64
NEIGH = 128
BLOCKS = 4
N_MP = 4
SIDE = 4
SCALE = HEAD_DIM ** (-0.5)
F32 = jnp.float32
BF16 = jnp.bfloat16
NT = (((1,), (1,)), ((), ()))
TN = (((0,), (0,)), ((), ()))
VMEM_LIMIT = 48 * 1024 * 1024


def mm(left, right, dims=(((1,), (0,)), ((), ()))):
    return lax.dot_general(left, right, dims, preferred_element_type=F32)


def block_rows(index):
    return pl.ds(pl.multiple_of(index * NEIGH, NEIGH), NEIGH)


def decoder_kernel(mp_ref, span_ref, rows_ref, weight_ref, query_ref, grad_ref, lse_ref, delta_ref,
                   kv_grad_ref, part0, part1, part2, part3, kv_ref):
    half = weight_ref.shape[1] // 2
    kv_ref[...] = mm(rows_ref[...], weight_ref[...]).astype(BF16)
    lane = lax.broadcasted_iota(jnp.int32, (1, 2 * SPAN), 1)
    used = []
    for block in range(BLOCKS):
        flags = [
            jnp.where((span_ref[c, 0] == block) | (span_ref[c, 1] == block), 1, 0) for c in range(2)
        ]
        used.append(jnp.where(lane < SPAN, flags[0], flags[1]) > 0)
    for head in range(half // HEAD_DIM):
        lo = head * HEAD_DIM
        query = query_ref[:, lo:lo + HEAD_DIM]
        grad = grad_ref[:, lo:lo + HEAD_DIM]
        lse = lse_ref[head:head + 1, :]
        delta = delta_ref[head:head + 1, :]
        for block in range(BLOCKS):
            r0 = block * NEIGH
            key = kv_ref[r0:r0 + NEIGH, lo:lo + HEAD_DIM]
            value = kv_ref[r0:r0 + NEIGH, half + lo:half + lo + HEAD_DIM]
            shift = jnp.where(used[block], lse, jnp.inf)
            probs = jnp.exp(mm(key, query, NT) * SCALE - shift)
            value_grad = mm(probs.astype(BF16), grad)
            score_grad = probs * (mm(value, grad, NT) - delta)
            key_grad = mm(score_grad.astype(BF16), query) * SCALE
            kv_grad_ref[r0:r0 + NEIGH, lo:lo + HEAD_DIM] = key_grad.astype(BF16)
            kv_grad_ref[r0:r0 + NEIGH, half + lo:half + lo + HEAD_DIM] = value_grad.astype(BF16)
    mp = mp_ref[0]
    for step, part in enumerate((part0, part1, part2, part3)):
        rows = kv_grad_ref[block_rows(lax.rem(mp + step, N_MP)), :]
        part[...] = mm(rows, weight_ref[...], NT).astype(BF16)


def prepare_kernel(rows_ref, weight_ref, hidden_ref, slope_ref):
    half = weight_ref.shape[1] // 2
    pre = mm(rows_ref[...], weight_ref[:, :half])
    square = pre * pre
    tangent = jnp.tanh(0.7978845608 * (pre + 0.044715 * square * pre))
    hidden_ref[...] = (0.5 * pre * (1.0 + tangent)).astype(BF16)
    slope_ref[...] = 0.5 * (1.0 + tangent) + 0.5 * pre * (1.0 - tangent * tangent) * 0.7978845608 * (
        1.0 + 0.134145 * square
    )


def encoder_kernel(mp_ref, rows_ref, weight_ref, hidden_ref, slope_ref, got0, got1, got2, got3,
                   partial_ref, part0, part1, part2, part3, pre_grad_ref, arrived_ref):
    half = weight_ref.shape[1] // 2
    mp = mp_ref[0]
    up = weight_ref[:, :half]
    for step, (got, part) in enumerate(zip((got0, got3, got2, got1), (part0, part1, part2, part3))):
        rows = block_rows(lax.rem(mp + step, N_MP))
        arrived_ref[rows, :] = got[...]
        hidden_grad = mm(got[...], weight_ref[:, half:])
        pre_grad = (hidden_grad * slope_ref[rows, :]).astype(BF16)
        pre_grad_ref[rows, :] = pre_grad
        part[...] = mm(pre_grad, up, NT).astype(BF16)
    partial_ref[:, half:] = mm(arrived_ref[...], hidden_ref[...], TN).astype(BF16)
    partial_ref[:, :half] = mm(rows_ref[...], pre_grad_ref[...], TN).astype(BF16)


def weight_kernel(rows_ref, kv_grad_ref, partial_ref):
    partial_ref[...] = mm(rows_ref[...], kv_grad_ref[...], TN).astype(BF16)


def sum_kernel(piece_ref, out0, out1, out2, out3, total_ref):
    total = piece_ref[0].astype(F32)
    for source in range(1, piece_ref.shape[0]):
        total = total + piece_ref[source].astype(F32)
    count = total.shape[0]
    share = count // SIDE
    total_ref[:count, :] = total
    total_ref[count:, :] = jnp.zeros((total_ref.shape[0] - count, total_ref.shape[1]), F32)
    for index, out in enumerate((out0, out1, out2, out3)):
        first = index * share
        out[...] = total_ref[first:first + out.shape[0], :].astype(BF16)


def vmem():
    return pl.BlockSpec(memory_space=pltpu.VMEM)


def smem():
    return pl.BlockSpec(memory_space=pltpu.SMEM)


def call(kernel, outs, args, scalars=0, scratch=(), flops=0):
    return pl.pallas_call(
        kernel,
        out_shape=[jax.ShapeDtypeStruct(shape, kind) for shape, kind in outs],
        in_specs=[smem()] * scalars + [vmem()] * (len(args) - scalars),
        out_specs=[vmem()] * len(outs),
        scratch_shapes=list(scratch),
        compiler_params=pltpu.CompilerParams(vmem_limit_bytes=VMEM_LIMIT),
        cost_estimate=pl.CostEstimate(flops=flops, bytes_accessed=4 << 20, transcendentals=0),
    )(*args)


def mp_move(value, source, target, step):
    pairs = [(source * N_MP + m, target * N_MP + (m + step) % N_MP) for m in range(N_MP)]
    return lax.ppermute(value, ("sec", "mp"), pairs)


def mp_sum(parts, section):
    total = parts[0].astype(F32)
    for step in (2, 1, 3):
        total = total + mp_move(parts[step], section, section, step).astype(F32)
    return total.astype(BF16)


def shards(states, proj_weights, queries, out_grad, logsumexp, delta, span_blocks):
    rows = states[0]
    local_rows, width = rows.shape
    half = proj_weights.shape[3]
    weights = proj_weights[0].reshape(width, 2 * half)
    quarter = local_rows // N_MP
    is_decoder = lax.axis_index("sec") == 0
    mp = lax.axis_index("mp").astype(jnp.int32).reshape(1)
    part_outs = [((quarter, width), BF16)] * N_MP

    def decoder_branch():
        kv_grad, *parts = call(
            decoder_kernel,
            [((local_rows, 2 * half), BF16)] + part_outs,
            (mp, span_blocks, rows, weights, queries, out_grad, logsumexp, delta),
            scalars=2,
            scratch=[pltpu.VMEM((local_rows, 2 * half), BF16)],
            flops=4 * local_rows * width * 2 * half,
        )
        return (kv_grad, jnp.zeros((local_rows, half), F32), *parts)

    def prepare_branch():
        hidden, slope = call(
            prepare_kernel,
            [((local_rows, half), BF16), ((local_rows, half), F32)],
            (rows, weights),
            flops=2 * local_rows * width * half,
        )
        empty = jnp.zeros((quarter, width), BF16)
        return (jnp.concatenate([hidden, hidden], axis=1), slope, empty, empty, empty, empty)

    mixed, slope, *enc_parts = lax.cond(is_decoder, decoder_branch, prepare_branch)
    enc_share = mp_sum(enc_parts, 0)
    got = [mp_move(enc_share, 0, 1, step) for step in range(N_MP)]

    def decoder_weights():
        (partial,) = call(
            weight_kernel, [((width, 2 * half), BF16)], (rows, mixed), flops=4 * local_rows * width * half
        )
        empty = jnp.zeros((quarter, width), BF16)
        return (partial, empty, empty, empty, empty)

    def encoder_branch():
        return tuple(
            call(
                encoder_kernel,
                [((width, 2 * half), BF16)] + part_outs,
                (mp, rows, weights, mixed[:, :half], slope, *got),
                scalars=1,
                scratch=[pltpu.VMEM((local_rows, half), BF16), pltpu.VMEM((local_rows, width), BF16)],
                flops=8 * local_rows * width * half,
            )
        )

    partial, *in_parts = lax.cond(is_decoder, decoder_weights, encoder_branch)
    in_share = mp_sum(in_parts, 1)
    pieces = lax.all_to_all(partial, ("x", "y"), 0, 0, tiled=True)
    chunk = width // (SIDE * SIDE)
    padded = 16
    blocks = call(
        sum_kernel,
        [((padded, 2 * half), BF16)] * SIDE,
        (pieces.reshape(SIDE * SIDE, chunk, 2 * half),),
        scratch=[pltpu.VMEM((SIDE * padded, 2 * half), F32)],
    )
    zh = lax.axis_index("zh")
    total = jnp.zeros((padded, 2 * half), F32)
    for step in range(SIDE):
        target = lax.rem(zh + step, SIDE)
        block = blocks[0]
        for index in range(1, SIDE):
            block = jnp.where(target == index, blocks[index], block)
        pairs = [
            (b * SIDE + a, a * SIDE + (b + step) % SIDE) for b in range(SIDE) for a in range(SIDE)
        ]
        total = total + lax.ppermute(block, ("zh", "y"), pairs).astype(F32)
    share = chunk // SIDE
    weight_part = (total[:share] / (SIDE * SIDE * SIDE)).reshape(1, share, 2, half)
    return (jnp.where(is_decoder, enc_share, in_share)[None], weight_part)


def solution(mesh):
    split = Mesh(mesh.devices.reshape(2, SIDE, SIDE, SIDE, N_MP), ("sec", "x", "zh", "y", "mp"))
    dp = ("x", "zh", "y")
    in_specs = (
        P("sec", dp, None),
        P("sec", None, None, "mp"),
        P(dp, "mp"),
        P(dp, "mp"),
        P("mp", dp),
        P("mp", dp),
        P(dp, None),
    )
    out_specs = (P("sec", (*dp, "mp"), None), P("sec", dp, None, "mp"))
    return jax.shard_map(shards, mesh=split, in_specs=in_specs, out_specs=out_specs, check_vma=False)
```

time: 1060 us -> 124 us (0.12)
  the two profiles are of different devices: /device:TPU:32 before, /device:TPU:1 now
where the time goes in v1:
time: 124 us
  waiting for transfers between devices  65.4 us (53%)
  starting transfers between devices  45.2 us (36%)
  Pallas kernels  7.01 us (6%)
  local copies, waits for them, and re-layouts  4.15 us (3%)
    ppermute x10, waiting for transfers between devices, mp_move(): return lax.ppermute(value, ('sec', 'mp'), pairs)  35.6 us
    ppermute x4, starting transfers between devices, shards(): total = total + lax.ppermute(block, ('zh', 'y'), pairs).astype(F32)  22.5 us
    ppermute x10, starting transfers between devices, mp_move(): return lax.ppermute(value, ('sec', 'mp'), pairs)  18.1 us
    all_to_all x1, waiting for transfers between devices, shards(): pieces = lax.all_to_all(partial, ('x', 'y'), 0, 0, tiled=True)  16.2 us
    ppermute x4, waiting for transfers between devices, shards(): total = total + lax.ppermute(block, ('zh', 'y'), pairs).astype(F32)  13.6 us
    pallas_call x3, Pallas kernels, call(): pl.pallas_call(kernel, out_shape=[jax.ShapeDtypeStruct(shape, kind) for s...  7.01 us
    all_to_all x1, starting transfers between devices, shards(): pieces = lax.all_to_all(partial, ('x', 'y'), 0, 0, tiled=True)  4.62 us
    unnamed x17, local copies, waits for them, and re-layouts  3.35 us
  transfers between devices with their start and end apart: 15, of which 6 were waited for; matrix products, arithmetic and copies ran while one was open for 1% of the time, Pallas kernels for 0%

profile of v1, /device:TPU:1, one launch (start us, length us, event | category | flops | bytes accessed | tf_op | source)
XLA Modules:
  0.0 123.9 jit_solution(1262814639278743139)
XLA Ops:
  0.6 0.0 copy-start
  0.6 0.0 copy-start.5
  0.7 0.0 copy-start.6
  0.7 0.0 copy-start.7
  0.7 2.1 %copy.14 = bf16[112,8,2,512]{3,1,2,0:T(8,128)(2,1)S(1)} copy(bf16[112,8,2,512]{3,2,1,0:T(2,128)(2,1)} %bitcast.15) | data formatting | bytes 3670016
  2.8 2.4 %conditional.2 = (bf16[512,1024]{1,0:T(8,128)(2,1)S(1)}, f32[512,512]{1,0:T(8,128)}, bf16[128,896]{1,0:T(8,128)(2,1)S(1)}, bf16[128,896]{1,0:T(8,128)(2,1)S(1)},...) conditional(s32[]{:T(128)} %convert_element_type.52, (bf16[512,896]{1,0:T(8,128)(2,1)S(1)}, ...), branch_computations={%region_0.0_spmd, %region_1.0_spmd} | conditional | flops 1879162880 | bytes 9601104 | solution.py:172
  2.8 2.2 %branch_0_fun.2 = (bf16[512,512]{1,0:T(8,128)(2,1)S(1)}, f32[512,512]{1,0:T(8,128)}) custom-call(bf16[512,896]{1,0:T(8,128)(2,1)S(1)} %get-tuple-element.49.rows_ref, bf16[896,1024]{1,0:T(8,128)(2,1)S(1)} %get-tuple-element.50.weight_ref), custom_call_target="tpu_custom_call" | custom-call | flops 469762048 | bytes 4194304 | tf_op jit(solution)/shard_map/cond/branch_0_fun/pallas_call | solution.py:118
  5.0 0.1 pad_maximum_fusion
  5.2 0.7 collective-permute-start
  5.9 0.7 collective-permute-start.1
  6.6 0.7 collective-permute-start.2
  7.3 0.0 collective-permute-done
  7.3 0.0 collective-permute-done.1
  7.3 0.0 collective-permute-done.2
  7.3 0.1 add_convert_fusion.1
  7.4 0.0 copy-start.3
  7.4 1.3 %collective-permute-start.3 = (bf16[128,896]{1,0:T(8,128)(2,1)S(1)}, bf16[128,896]{1,0:T(8,128)(2,1)S(1)}, u32[]{:S(2)}, u32[]{:S(2)}) collective-permute-start(bf16[128,896]{1,0:T(8,128)(2,1)S(1)} %add_convert_fusion.1), channel_id=1, source_target_pairs={{0,256},{1,257},{2,258},{3,259},{4,260},{5,261},{6,262},{7,263},{8... | collective-permute-start | bytes 688136 | tf_op jit(solution)/shard_map/ppermute | solution.py:131
  8.7 1.3 %collective-permute-start.4 = (bf16[128,896]{1,0:T(8,128)(2,1)S(1)}, bf16[128,896]{1,0:T(8,128)(2,1)S(1)}, u32[]{:S(2)}, u32[]{:S(2)}) collective-permute-start(bf16[128,896]{1,0:T(8,128)(2,1)S(1)} %add_convert_fusion.1), channel_id=1, source_target_pairs={{0,257},{1,258},{2,259},{3,256},{4,261},{5,262},{6,263},{7,260},{8... | collective-permute-start | bytes 688136 | tf_op jit(solution)/shard_map/ppermute | solution.py:131
  10.0 1.3 %collective-permute-start.5 = (bf16[128,896]{1,0:T(8,128)(2,1)S(1)}, bf16[128,896]{1,0:T(8,128)(2,1)S(1)}, u32[]{:S(2)}, u32[]{:S(2)}) collective-permute-start(bf16[128,896]{1,0:T(8,128)(2,1)S(1)} %add_convert_fusion.1), channel_id=1, source_target_pairs={{0,258},{1,259},{2,256},{3,257},{4,262},{5,263},{6,260},{7,261},{8... | collective-permute-start | bytes 688136 | tf_op jit(solution)/shard_map/ppermute | solution.py:131
  11.3 1.3 %collective-permute-start.6 = (bf16[128,896]{1,0:T(8,128)(2,1)S(1)}, bf16[128,896]{1,0:T(8,128)(2,1)S(1)}, u32[]{:S(2)}, u32[]{:S(2)}) collective-permute-start(bf16[128,896]{1,0:T(8,128)(2,1)S(1)} %add_convert_fusion.1), channel_id=1, source_target_pairs={{0,259},{1,256},{2,257},{3,258},{4,263},{5,260},{6,261},{7,262},{8... | collective-permute-start | bytes 688136 | tf_op jit(solution)/shard_map/ppermute | solution.py:131
  12.6 25.1 %collective-permute-done.3 = bf16[128,896]{1,0:T(8,128)(2,1)S(1)} collective-permute-done((bf16[128,896]{1,0:T(8,128)(2,1)S(1)}, bf16[128,896]{1,0:T(8,128)(2,1)S(1)}, u32[]{:S(2)}, u32[]{:S(2)}) %collective-permute-start.3) | collective-permute-done | bytes 229408 | tf_op jit(solution)/shard_map/ppermute | solution.py:131
  37.7 7.1 %collective-permute-done.4 = bf16[128,896]{1,0:T(8,128)(2,1)S(1)} collective-permute-done((bf16[128,896]{1,0:T(8,128)(2,1)S(1)}, bf16[128,896]{1,0:T(8,128)(2,1)S(1)}, u32[]{:S(2)}, u32[]{:S(2)}) %collective-permute-start.4) | collective-permute-done | bytes 229408 | tf_op jit(solution)/shard_map/ppermute | solution.py:131
  44.8 3.4 %collective-permute-done.5 = bf16[128,896]{1,0:T(8,128)(2,1)S(1)} collective-permute-done((bf16[128,896]{1,0:T(8,128)(2,1)S(1)}, bf16[128,896]{1,0:T(8,128)(2,1)S(1)}, u32[]{:S(2)}, u32[]{:S(2)}) %collective-permute-start.5) | collective-permute-done | bytes 229408 | tf_op jit(solution)/shard_map/ppermute | solution.py:131
  48.2 0.0 collective-permute-done.6
  48.2 4.5 %conditional.3 = (bf16[896,1024]{1,0:T(8,128)(2,1)S(1)}, bf16[128,896]{1,0:T(8,128)(2,1)}, bf16[128,896]{1,0:T(8,128)(2,1)}, bf16[128,896]{1,0:T(8,128)(2,1)}, f32[128,896]{1,0:T(8,128)S(1)}) conditional(s32[]{:T(128)} %convert_element_type.52, (bf16[512,1024]{1,0:T(8,128)(2,1)S(1)}, s32[1]{0:T(128)}, bf16[512,896]{1,0:T(8,128)(2,1)}, ...), branch_computations={%region_2.0_spmd, %region_3.0_spmd} | conditional | flops 1879162880 | bytes 5931048 | solution.py:195
  48.2 4.5 %branch_0_fun.3 = (bf16[896,1024]{1,0:T(8,128)(2,1)S(1)}, bf16[128,896]{1,0:T(8,128)(2,1)S(1)}, bf16[128,896]{1,0:T(8,128)(2,1)}, bf16[128,896]{1,0:T(8,128)(2,1)}, bf16[128,896]{1,0:T(8,128)(2,1)}) custom-call(s32[1]{0:T(128)} %get-tuple-element.66.mp_ref, bf16[512,896]{1,0:T(8,128)(2,1)} %get-tuple-element.67.rows_ref, ...), custom_call_target="tpu_custom_call" | custom-call | flops 1879048192 | bytes 4194304 | tf_op jit(solution)/shard_map/cond/branch_0_fun/pallas_call | solution.py:118
  52.8 1.2 %copy-done.2 = bf16[896,1024]{1,0:T(8,128)(2,1)} copy-done((bf16[896,1024]{1,0:T(8,128)(2,1)}, bf16[896,1024]{1,0:T(8,128)(2,1)S(1)}, u32[]{:S(2)}) %copy-start.2) | copy-done | bytes 1835032
  54.0 4.6 %all-to-all-start = ((bf16[16,56,1024]{2,1,0:T(8,128)(2,1)}), bf16[16,56,1024]{2,1,0:T(8,128)(2,1)S(1)}, u32[]{:S(2)}, u32[]{:S(2)}) async-start(bf16[16,56,1024]{2,1,0:T(8,128)(2,1)} %bitcast.16), calls=%async_computation | async-start | bytes 3670016 | tf_op jit(solution)/shard_map/all_to_all | solution.py:197
  58.6 0.0 copy-start.4
  58.7 3.8 %collective-permute-start.7 = (bf16[128,896]{1,0:T(8,128)(2,1)}, bf16[128,896]{1,0:T(8,128)(2,1)S(1)}, u32[]{:S(2)}, u32[]{:S(2)}) collective-permute-start(bf16[128,896]{1,0:T(8,128)(2,1)} %get-tuple-element.106), channel_id=1, source_target_pairs={{256,258},{257,259},{258,256},{259,257},{260,262},{261,263},{262,2... | collective-permute-start | bytes 688136 | tf_op jit(solution)/shard_map/ppermute | solution.py:131
  62.5 3.6 %collective-permute-start.8 = (bf16[128,896]{1,0:T(8,128)(2,1)}, bf16[128,896]{1,0:T(8,128)(2,1)S(1)}, u32[]{:S(2)}, u32[]{:S(2)}) collective-permute-start(bf16[128,896]{1,0:T(8,128)(2,1)} %get-tuple-element.107), channel_id=1, source_target_pairs={{256,257},{257,258},{258,259},{259,256},{260,261},{261,262},{262,2... | collective-permute-start | bytes 688136 | tf_op jit(solution)/shard_map/ppermute | solution.py:131
  66.1 3.4 %collective-permute-start.9 = (bf16[128,896]{1,0:T(8,128)(2,1)}, bf16[128,896]{1,0:T(8,128)(2,1)S(1)}, u32[]{:S(2)}, u32[]{:S(2)}) collective-permute-start(bf16[128,896]{1,0:T(8,128)(2,1)} %get-tuple-element.108), channel_id=1, source_target_pairs={{256,259},{257,256},{258,257},{259,258},{260,263},{261,260},{262,2... | collective-permute-start | bytes 688136 | tf_op jit(solution)/shard_map/ppermute | solution.py:131
  69.6 16.2 %all-to-all-done.piece_ref = bf16[16,56,1024]{2,1,0:T(8,128)(2,1)S(1)} async-done(((bf16[16,56,1024]{2,1,0:T(8,128)(2,1)}), bf16[16,56,1024]{2,1,0:T(8,128)(2,1)S(1)}, u32[]{:S(2)}, u32[]{:S(2)}) %all-to-all-start) | async-done | bytes 1835040 | tf_op jit(solution)/shard_map/all_to_all | solution.py:197
  85.8 0.4 shard_map.91
  86.2 0.7 collective-permute-start.10
  86.8 11.3 %collective-permute-start.11 = (bf16[16,1024]{1,0:T(8,128)(2,1)S(1)}, bf16[16,1024]{1,0:T(8,128)(2,1)S(1)}, u32[]{:S(2)}, u32[]{:S(2)}) collective-permute-start(bf16[16,1024]{1,0:T(8,128)(2,1)S(1)} %get-tuple-element.127), channel_id=1, source_target_pairs={{0,4},{4,20},{8,36},{12,52},{16,8},{20,24},{24,40},{28,56},{32,12}... | collective-permute-start | bytes 98312 | tf_op jit(solution)/shard_map/ppermute | solution.py:216
  98.1 0.0 collective-permute-done.7
  98.1 7.8 %collective-permute-start.12 = (bf16[16,1024]{1,0:T(8,128)(2,1)S(1)}, bf16[16,1024]{1,0:T(8,128)(2,1)S(1)}, u32[]{:S(2)}, u32[]{:S(2)}) collective-permute-start(bf16[16,1024]{1,0:T(8,128)(2,1)S(1)} %get-tuple-element.126), channel_id=1, source_target_pairs={{0,8},{4,24},{8,40},{12,56},{16,12},{20,28},{24,44},{28,60},{32,0}... | collective-permute-start | bytes 98312 | tf_op jit(solution)/shard_map/ppermute | solution.py:216
  105.9 0.0 collective-permute-done.8
  105.9 2.8 %collective-permute-start.13 = (bf16[16,1024]{1,0:T(8,128)(2,1)S(1)}, bf16[16,1024]{1,0:T(8,128)(2,1)S(1)}, u32[]{:S(2)}, u32[]{:S(2)}) collective-permute-start(bf16[16,1024]{1,0:T(8,128)(2,1)S(1)} %get-tuple-element.125), channel_id=1, source_target_pairs={{0,12},{4,28},{8,44},{12,60},{16,0},{20,16},{24,32},{28,48},{32,4}... | collective-permute-start | bytes 98312 | tf_op jit(solution)/shard_map/ppermute | solution.py:216
  108.7 0.0 collective-permute-done.9
  108.7 0.0 copy-done.4
  108.7 0.8 fusion.1
  109.6 0.0 collective-permute-done.10
  109.6 0.0 collective-permute-done.11
  109.6 4.5 %collective-permute-done.12 = bf16[16,1024]{1,0:T(8,128)(2,1)S(1)} collective-permute-done((bf16[16,1024]{1,0:T(8,128)(2,1)S(1)}, bf16[16,1024]{1,0:T(8,128)(2,1)S(1)}, u32[]{:S(2)}, u32[]{:S(2)}) %collective-permute-start.12) | collective-permute-done | bytes 32800 | tf_op jit(solution)/shard_map/ppermute | solution.py:216
  114.0 9.1 %collective-permute-done.13 = bf16[16,1024]{1,0:T(8,128)(2,1)S(1)} collective-permute-done((bf16[16,1024]{1,0:T(8,128)(2,1)S(1)}, bf16[16,1024]{1,0:T(8,128)(2,1)S(1)}, u32[]{:S(2)}, u32[]{:S(2)}) %collective-permute-start.13) | collective-permute-done | bytes 32800 | tf_op jit(solution)/shard_map/ppermute | solution.py:216
  123.2 0.7 reshape.15
  (16 shorter events, 0.2 us)
Async XLA Ops:
  0.6 2.1 %copy-start = (bf16[1,512,896]{2,1,0:T(8,128)(2,1)S(1)}, bf16[1,512,896]{2,1,0:T(8,128)(2,1)}, u32[]{:S(2)}) copy-start(bf16[1,512,896]{2,1,0:T(8,128)(2,1)} %param.11) | copy-start | bytes 2752516
  0.6 2.1 %copy-start.5 = (bf16[128,512]{1,0:T(8,128)(2,1)S(1)}, bf16[128,512]{1,0:T(8,128)(2,1)}, u32[]{:S(2)}) copy-start(bf16[128,512]{1,0:T(8,128)(2,1)} %param.13) | copy-start | bytes 393220
  0.7 2.1 %copy-start.6 = (f32[4,128]{1,0:T(4,128)S(1)}, f32[4,128]{1,0:T(4,128)}, u32[]{:S(2)}) copy-start(f32[4,128]{1,0:T(4,128)} %param.15) | copy-start | bytes 6148
  0.7 2.1 %copy-start.7 = (f32[4,128]{1,0:T(4,128)S(1)}, f32[4,128]{1,0:T(4,128)}, u32[]{:S(2)}) copy-start(f32[4,128]{1,0:T(4,128)} %param.16) | copy-start | bytes 6148
  0.7 2.1 %copy-start.8 = (s32[2,2]{1,0:T(2,128)S(1)}, s32[2,2]{1,0:T(2,128)}, u32[]{:S(2)}) copy-start(s32[2,2]{1,0:T(2,128)} %param.17) | copy-start | bytes 52
  5.2 2.1 %collective-permute-start = (bf16[128,896]{1,0:T(8,128)(2,1)S(1)}, bf16[128,896]{1,0:T(8,128)(2,1)S(1)}, u32[]{:S(2)}, u32[]{:S(2)}) collective-permute-start(bf16[128,896]{1,0:T(8,128)(2,1)S(1)} %get-tuple-element.100), channel_id=1, source_target_pairs={{0,2},{1,3},{2,0},{3,1},{4,6},{5,7},{6,4},{7,5},{8,10},{9,11},{10,... | collective-permute-start | bytes 688136 | tf_op jit(solution)/shard_map/ppermute | solution.py:131
  5.9 1.4 %collective-permute-start.1 = (bf16[128,896]{1,0:T(8,128)(2,1)S(1)}, bf16[128,896]{1,0:T(8,128)(2,1)S(1)}, u32[]{:S(2)}, u32[]{:S(2)}) collective-permute-start(bf16[128,896]{1,0:T(8,128)(2,1)S(1)} %get-tuple-element.101), channel_id=1, source_target_pairs={{0,1},{1,2},{2,3},{3,0},{4,5},{5,6},{6,7},{7,4},{8,9},{9,10},{10,1... | collective-permute-start | bytes 688136 | tf_op jit(solution)/shard_map/ppermute | solution.py:131
  6.6 0.7 collective-permute-start.2
  7.4 40.8 %copy-start.3 = (bf16[128,896]{1,0:T(8,128)(2,1)}, bf16[128,896]{1,0:T(8,128)(2,1)S(1)}, u32[]{:S(2)}) copy-start(bf16[128,896]{1,0:T(8,128)(2,1)S(1)} %add_convert_fusion.1) | copy-start | bytes 688132
  7.4 30.3 %collective-permute-start.3 = (bf16[128,896]{1,0:T(8,128)(2,1)S(1)}, bf16[128,896]{1,0:T(8,128)(2,1)S(1)}, u32[]{:S(2)}, u32[]{:S(2)}) collective-permute-start(bf16[128,896]{1,0:T(8,128)(2,1)S(1)} %add_convert_fusion.1), channel_id=1, source_target_pairs={{0,256},{1,257},{2,258},{3,259},{4,260},{5,261},{6,262},{7,263},{8... | collective-permute-start | bytes 688136 | tf_op jit(solution)/shard_map/ppermute | solution.py:131
  8.7 36.1 %collective-permute-start.4 = (bf16[128,896]{1,0:T(8,128)(2,1)S(1)}, bf16[128,896]{1,0:T(8,128)(2,1)S(1)}, u32[]{:S(2)}, u32[]{:S(2)}) collective-permute-start(bf16[128,896]{1,0:T(8,128)(2,1)S(1)} %add_convert_fusion.1), channel_id=1, source_target_pairs={{0,257},{1,258},{2,259},{3,256},{4,261},{5,262},{6,263},{7,260},{8... | collective-permute-start | bytes 688136 | tf_op jit(solution)/shard_map/ppermute | solution.py:131
  10.0 38.2 %collective-permute-start.5 = (bf16[128,896]{1,0:T(8,128)(2,1)S(1)}, bf16[128,896]{1,0:T(8,128)(2,1)S(1)}, u32[]{:S(2)}, u32[]{:S(2)}) collective-permute-start(bf16[128,896]{1,0:T(8,128)(2,1)S(1)} %add_convert_fusion.1), channel_id=1, source_target_pairs={{0,258},{1,259},{2,256},{3,257},{4,262},{5,263},{6,260},{7,261},{8... | collective-permute-start | bytes 688136 | tf_op jit(solution)/shard_map/ppermute | solution.py:131
  11.3 36.9 %collective-permute-start.6 = (bf16[128,896]{1,0:T(8,128)(2,1)S(1)}, bf16[128,896]{1,0:T(8,128)(2,1)S(1)}, u32[]{:S(2)}, u32[]{:S(2)}) collective-permute-start(bf16[128,896]{1,0:T(8,128)(2,1)S(1)} %add_convert_fusion.1), channel_id=1, source_target_pairs={{0,259},{1,256},{2,257},{3,258},{4,263},{5,260},{6,261},{7,262},{8... | collective-permute-start | bytes 688136 | tf_op jit(solution)/shard_map/ppermute | solution.py:131
  52.8 1.3 %copy-start.2 = (bf16[896,1024]{1,0:T(8,128)(2,1)}, bf16[896,1024]{1,0:T(8,128)(2,1)S(1)}, u32[]{:S(2)}) copy-start(bf16[896,1024]{1,0:T(8,128)(2,1)S(1)} %get-tuple-element.109) | copy-start | bytes 5505028
  54.0 31.8 %all-to-all-start = ((bf16[16,56,1024]{2,1,0:T(8,128)(2,1)}), bf16[16,56,1024]{2,1,0:T(8,128)(2,1)S(1)}, u32[]{:S(2)}, u32[]{:S(2)}) async-start(bf16[16,56,1024]{2,1,0:T(8,128)(2,1)} %bitcast.16), calls=%async_computation | async-start | bytes 3670016 | tf_op jit(solution)/shard_map/all_to_all | solution.py:197
  58.6 50.1 %copy-start.4 = (bf16[128,896]{1,0:T(8,128)(2,1)S(1)}, bf16[128,896]{1,0:T(8,128)(2,1)}, u32[]{:S(2)}) copy-start(bf16[128,896]{1,0:T(8,128)(2,1)} %copy-done.3) | copy-start | bytes 688132
  58.7 39.4 %collective-permute-start.7 = (bf16[128,896]{1,0:T(8,128)(2,1)}, bf16[128,896]{1,0:T(8,128)(2,1)S(1)}, u32[]{:S(2)}, u32[]{:S(2)}) collective-permute-start(bf16[128,896]{1,0:T(8,128)(2,1)} %get-tuple-element.106), channel_id=1, source_target_pairs={{256,258},{257,259},{258,256},{259,257},{260,262},{261,263},{262,2... | collective-permute-start | bytes 688136 | tf_op jit(solution)/shard_map/ppermute | solution.py:131
  62.5 43.5 %collective-permute-start.8 = (bf16[128,896]{1,0:T(8,128)(2,1)}, bf16[128,896]{1,0:T(8,128)(2,1)S(1)}, u32[]{:S(2)}, u32[]{:S(2)}) collective-permute-start(bf16[128,896]{1,0:T(8,128)(2,1)} %get-tuple-element.107), channel_id=1, source_target_pairs={{256,257},{257,258},{258,259},{259,256},{260,261},{261,262},{262,2... | collective-permute-start | bytes 688136 | tf_op jit(solution)/shard_map/ppermute | solution.py:131
  66.1 42.6 %collective-permute-start.9 = (bf16[128,896]{1,0:T(8,128)(2,1)}, bf16[128,896]{1,0:T(8,128)(2,1)S(1)}, u32[]{:S(2)}, u32[]{:S(2)}) collective-permute-start(bf16[128,896]{1,0:T(8,128)(2,1)} %get-tuple-element.108), channel_id=1, source_target_pairs={{256,259},{257,256},{258,257},{259,258},{260,263},{261,260},{262,2... | collective-permute-start | bytes 688136 | tf_op jit(solution)/shard_map/ppermute | solution.py:131
  86.2 23.4 %collective-permute-start.10 = (bf16[16,1024]{1,0:T(8,128)(2,1)S(1)}, bf16[16,1024]{1,0:T(8,128)(2,1)S(1)}, u32[]{:S(2)}, u32[]{:S(2)}) collective-permute-start(bf16[16,1024]{1,0:T(8,128)(2,1)S(1)} %get-tuple-element.124), channel_id=1, source_target_pairs={{0,0},{4,16},{8,32},{12,48},{16,4},{20,20},{24,36},{28,52},{32,8},... | collective-permute-start | bytes 98312 | tf_op jit(solution)/shard_map/ppermute | solution.py:216
  86.8 22.7 %collective-permute-start.11 = (bf16[16,1024]{1,0:T(8,128)(2,1)S(1)}, bf16[16,1024]{1,0:T(8,128)(2,1)S(1)}, u32[]{:S(2)}, u32[]{:S(2)}) collective-permute-start(bf16[16,1024]{1,0:T(8,128)(2,1)S(1)} %get-tuple-element.127), channel_id=1, source_target_pairs={{0,4},{4,20},{8,36},{12,52},{16,8},{20,24},{24,40},{28,56},{32,12}... | collective-permute-start | bytes 98312 | tf_op jit(solution)/shard_map/ppermute | solution.py:216
  98.1 15.9 %collective-permute-start.12 = (bf16[16,1024]{1,0:T(8,128)(2,1)S(1)}, bf16[16,1024]{1,0:T(8,128)(2,1)S(1)}, u32[]{:S(2)}, u32[]{:S(2)}) collective-permute-start(bf16[16,1024]{1,0:T(8,128)(2,1)S(1)} %get-tuple-element.126), channel_id=1, source_target_pairs={{0,8},{4,24},{8,40},{12,56},{16,12},{20,28},{24,44},{28,60},{32,0}... | collective-permute-start | bytes 98312 | tf_op jit(solution)/shard_map/ppermute | solution.py:216
  105.9 17.2 %collective-permute-start.13 = (bf16[16,1024]{1,0:T(8,128)(2,1)S(1)}, bf16[16,1024]{1,0:T(8,128)(2,1)S(1)}, u32[]{:S(2)}, u32[]{:S(2)}) collective-permute-start(bf16[16,1024]{1,0:T(8,128)(2,1)S(1)} %get-tuple-element.125), channel_id=1, source_target_pairs={{0,12},{4,28},{8,44},{12,60},{16,0},{20,16},{24,32},{28,48},{32,4}... | collective-permute-start | bytes 98312 | tf_op jit(solution)/shard_map/ppermute | solution.py:216

commit v2 on v1

v2 whole, which is shorter than its diff:
```python
import jax
import jax.numpy as jnp
from jax import lax
from jax.experimental import pallas as pl
from jax.experimental.pallas import tpu as pltpu
from jax.sharding import Mesh
from jax.sharding import PartitionSpec as P

HEAD_DIM = 128
SPAN = 64
NEIGH = 128
BLOCKS = 4
N_MP = 4
SIDE = 4
PADDED = 16
SCALE = HEAD_DIM ** (-0.5)
F32 = jnp.float32
BF16 = jnp.bfloat16
NT = (((1,), (1,)), ((), ()))
TN = (((0,), (0,)), ((), ()))
VMEM_LIMIT = 48 * 1024 * 1024


def mm(left, right, dims=(((1,), (0,)), ((), ()))):
    return lax.dot_general(left, right, dims, preferred_element_type=F32)


def block_rows(index):
    return pl.ds(pl.multiple_of(index * NEIGH, NEIGH), NEIGH)


def on_section(sec_ref, section):
    return pl.when(sec_ref[0] == section)


def decoder_kernel(mp_ref, span_ref, rows_ref, weight_ref, query_ref, grad_ref, lse_ref, delta_ref,
                   kv_grad_ref, part0, part1, part2, part3, kv_ref, part_ref):
    half = weight_ref.shape[1] // 2
    kv_ref[...] = mm(rows_ref[...], weight_ref[...]).astype(BF16)
    lane = lax.broadcasted_iota(jnp.int32, (1, 2 * SPAN), 1)
    used = []
    for block in range(BLOCKS):
        flags = [
            jnp.where((span_ref[c, 0] == block) | (span_ref[c, 1] == block), 1, 0) for c in range(2)
        ]
        used.append(jnp.where(lane < SPAN, flags[0], flags[1]) > 0)
    for head in range(half // HEAD_DIM):
        lo = head * HEAD_DIM
        query = query_ref[:, lo:lo + HEAD_DIM]
        grad = grad_ref[:, lo:lo + HEAD_DIM]
        lse = lse_ref[head:head + 1, :]
        delta = delta_ref[head:head + 1, :]
        key = kv_ref[:, lo:lo + HEAD_DIM]
        value = kv_ref[:, half + lo:half + lo + HEAD_DIM]
        shift = jnp.concatenate(
            [jnp.broadcast_to(jnp.where(flag, lse, jnp.inf), (NEIGH, 2 * SPAN)) for flag in used], axis=0
        )
        probs = jnp.exp(mm(key, query, NT) * SCALE - shift)
        value_grad = mm(probs.astype(BF16), grad)
        score_grad = probs * (mm(value, grad, NT) - delta)
        key_grad = mm(score_grad.astype(BF16), query) * SCALE
        kv_grad_ref[:, lo:lo + HEAD_DIM] = key_grad.astype(BF16)
        kv_grad_ref[:, half + lo:half + lo + HEAD_DIM] = value_grad.astype(BF16)
    part_ref[...] = mm(kv_grad_ref[...], weight_ref[...], NT).astype(BF16)
    for step, part in enumerate((part0, part1, part2, part3)):
        part[...] = part_ref[block_rows(lax.rem(mp_ref[0] + step, N_MP)), :]


def ordered(rows, order_ref):
    width = order_ref.shape[1]
    place = lax.broadcasted_iota(jnp.int32, (width, width), 0) == order_ref[...]
    return mm(rows, jnp.where(place, 1.0, 0.0).astype(BF16)).astype(BF16)


def store_chunks(out_ref, value):
    chunk = out_ref.shape[1]
    for index in range(out_ref.shape[0]):
        out_ref[index] = value[index * chunk:(index + 1) * chunk, :].astype(BF16)


def decoder_weight_kernel(sec_ref, rows_ref, kv_grad_ref, order_ref, first_ref, second_ref):
    @on_section(sec_ref, 0)
    def work():
        half = kv_grad_ref.shape[1] // 2
        rows = ordered(rows_ref[...], order_ref)
        store_chunks(second_ref, mm(rows, kv_grad_ref[:, half:], TN))
        store_chunks(first_ref, mm(rows, kv_grad_ref[:, :half], TN))


def prepare_kernel(rows_ref, weight_ref, order_ref, ordered_ref, hidden_ref, slope_ref):
    half = weight_ref.shape[1] // 2
    ordered_ref[...] = ordered(rows_ref[...], order_ref)
    pre = mm(rows_ref[...], weight_ref[:, :half])
    square = pre * pre
    tangent = jnp.tanh(0.7978845608 * (pre + 0.044715 * square * pre))
    hidden_ref[...] = (0.5 * pre * (1.0 + tangent)).astype(BF16)
    slope_ref[...] = 0.5 * (1.0 + tangent) + 0.5 * pre * (1.0 - tangent * tangent) * 0.7978845608 * (
        1.0 + 0.134145 * square
    )


def first_kernel(sec_ref, mp_ref, span_ref, rows_ref, weight_ref, query_ref, grad_ref, lse_ref, delta_ref, order_ref,
                 kv_grad_ref, part0, part1, part2, part3, ordered_ref, hidden_ref, slope_ref, kv_ref, part_ref):
    @on_section(sec_ref, 0)
    def decoder():
        decoder_kernel(
            mp_ref, span_ref, rows_ref, weight_ref, query_ref, grad_ref, lse_ref, delta_ref,
            kv_grad_ref, part0, part1, part2, part3, kv_ref, part_ref,
        )

    @on_section(sec_ref, 1)
    def encoder():
        prepare_kernel(rows_ref, weight_ref, order_ref, ordered_ref, hidden_ref, slope_ref)


def down_kernel(sec_ref, mp_ref, order_ref, hidden_ref, got0, got1, got2, got3, arrived_ref, second_ref):
    @on_section(sec_ref, 1)
    def work():
        for step, got in enumerate((got0, got3, got2, got1)):
            arrived_ref[block_rows(lax.rem(mp_ref[0] + step, N_MP)), :] = got[...]
        store_chunks(second_ref, mm(ordered(arrived_ref[...], order_ref), hidden_ref[...], TN))


def up_kernel(sec_ref, mp_ref, ordered_ref, weight_ref, slope_ref, arrived_ref, first_ref, part0, part1, part2, part3,
              part_ref):
    @on_section(sec_ref, 1)
    def work():
        half = weight_ref.shape[1] // 2
        hidden_grad = mm(arrived_ref[...], weight_ref[:, half:])
        pre_grad = (hidden_grad * slope_ref[...]).astype(BF16)
        store_chunks(first_ref, mm(ordered_ref[...], pre_grad, TN))
        part_ref[...] = mm(pre_grad, weight_ref[:, :half], NT).astype(BF16)
        for step, part in enumerate((part0, part1, part2, part3)):
            part[...] = part_ref[block_rows(lax.rem(mp_ref[0] + step, N_MP)), :]


def chunk_sum(piece_ref, total_ref):
    total = piece_ref[0].astype(F32)
    for source in range(1, piece_ref.shape[0]):
        total = total + piece_ref[source].astype(F32)
    count = total.shape[0]
    share = count // SIDE
    total_ref[:count, :] = total
    total_ref[count:, :] = jnp.zeros((total_ref.shape[0] - count, total_ref.shape[1]), F32)
    return jnp.concatenate(
        [total_ref[index * share:index * share + PADDED, :] for index in range(SIDE)], axis=0
    ).astype(BF16)


def early_sum_kernel(piece_ref, out_ref, total_ref):
    out_ref[...] = chunk_sum(piece_ref, total_ref)


def late_sum_kernel(sec_ref, piece_ref, early_ref, own_ref, other_ref, total_ref):
    late = chunk_sum(piece_ref, total_ref)

    @pl.when(sec_ref[0] == 0)
    def decoder():
        own_ref[...] = early_ref[...]
        other_ref[...] = late

    @pl.when(sec_ref[0] != 0)
    def encoder():
        own_ref[...] = late
        other_ref[...] = early_ref[...]


def join_kernel(zh_ref, own_ref, came_ref, out0, out1, out2, out3):
    half = own_ref.shape[1]
    for step, out in enumerate((out0, out1, out2, out3)):
        rows = pl.ds(pl.multiple_of(lax.rem(zh_ref[0] + step, SIDE) * PADDED, PADDED), PADDED)
        out[:, :half] = own_ref[rows, :]
        out[:, half:] = came_ref[rows, :]


def vmem():
    return pl.BlockSpec(memory_space=pltpu.VMEM)


def smem():
    return pl.BlockSpec(memory_space=pltpu.SMEM)


def call(kernel, outs, args, scalars=0, scratch=(), flops=0):
    return pl.pallas_call(
        kernel,
        out_shape=[jax.ShapeDtypeStruct(shape, kind) for shape, kind in outs],
        in_specs=[smem()] * scalars + [vmem()] * (len(args) - scalars),
        out_specs=[vmem()] * len(outs),
        scratch_shapes=list(scratch),
        compiler_params=pltpu.CompilerParams(vmem_limit_bytes=VMEM_LIMIT),
        cost_estimate=pl.CostEstimate(flops=flops, bytes_accessed=4 << 20, transcendentals=0),
    )(*args)


def mp_move(value, source, target, step):
    pairs = [(source * N_MP + m, target * N_MP + (m + step) % N_MP) for m in range(N_MP)]
    return lax.ppermute(value, ("sec", "mp"), pairs)


def mp_sum(parts, section):
    total = parts[0].astype(F32)
    for step in (2, 1, 3):
        total = total + mp_move(parts[step], section, section, step).astype(F32)
    return total.astype(BF16)


def shards(states, proj_weights, queries, out_grad, logsumexp, delta, span_blocks):
    rows = states[0]
    local_rows, width = rows.shape
    half = proj_weights.shape[3]
    weights = proj_weights[0].reshape(width, 2 * half)
    quarter = local_rows // N_MP
    pieces = SIDE * SIDE
    chunk = width // pieces
    share = chunk // SIDE
    sec = lax.axis_index("sec").astype(jnp.int32).reshape(1)
    mp = lax.axis_index("mp").astype(jnp.int32).reshape(1)
    zh = lax.axis_index("zh").astype(jnp.int32).reshape(1)
    is_decoder = sec[0] == 0
    order = jnp.arange(width, dtype=jnp.int32).reshape(SIDE, SIDE, SIDE, share)
    order = order.transpose(0, 2, 1, 3).reshape(1, width)

    part_outs = [((quarter, width), BF16)] * N_MP
    piece_out = ((pieces, chunk, half), BF16)
    col_out = ((local_rows, half), BF16)
    sum_out = ((SIDE * PADDED, half), BF16)
    part_scratch = pltpu.VMEM((local_rows, width), BF16)
    sum_scratch = pltpu.VMEM((SIDE * PADDED, half), F32)
    cols_flops = 2 * local_rows * width * half

    ordered_out = ((local_rows, width), BF16)
    kv_grad, *enc_parts, ordered_rows, hidden, slope = call(
        first_kernel,
        [((local_rows, 2 * half), BF16)] + part_outs + [ordered_out, col_out, ((local_rows, half), F32)],
        (sec, mp, span_blocks, rows, weights, queries, out_grad, logsumexp, delta, order),
        scalars=3,
        scratch=[pltpu.VMEM((local_rows, 2 * half), BF16), part_scratch],
        flops=4 * cols_flops,
    )
    enc_share = mp_sum(enc_parts, 0)
    got = [mp_move(enc_share, 0, 1, step) for step in range(N_MP)]

    first, second = call(
        decoder_weight_kernel, [piece_out] * 2, (sec, rows, kv_grad, order), scalars=1, flops=4 * cols_flops
    )
    second = lax.ppermute(second, "sec", [(0, 1)])
    early = lax.all_to_all(jnp.where(is_decoder, first, second), ("x", "y"), 0, 0, tiled=True)
    (early_sum,) = call(early_sum_kernel, [sum_out], (early,), scratch=[sum_scratch])
    early_sum, *got = lax.optimization_barrier((early_sum, *got))

    arrived, down = call(
        down_kernel, [ordered_out, piece_out], (sec, mp, order, hidden, *got), scalars=2, flops=3 * cols_flops
    )
    down = lax.ppermute(down, "sec", [(1, 0)])
    up, *in_parts = call(
        up_kernel,
        [piece_out] + part_outs,
        (sec, mp, ordered_rows, weights, slope, arrived),
        scalars=2,
        scratch=[part_scratch],
        flops=3 * cols_flops,
    )
    in_share = mp_sum(in_parts, 1)
    late = lax.all_to_all(jnp.where(is_decoder, down, up), ("x", "y"), 0, 0, tiled=True)
    own, other = call(late_sum_kernel, [sum_out] * 2, (sec, late, early_sum), scalars=1, scratch=[sum_scratch])
    came = lax.ppermute(other, "sec", [(0, 1), (1, 0)])
    blocks = call(join_kernel, [((PADDED, 2 * half), BF16)] * SIDE, (zh, own, came), scalars=1)
    total = blocks[0].astype(F32)
    for step in range(1, SIDE):
        pairs = [(source, (source + step) % SIDE) for source in range(SIDE)]
        total = total + lax.ppermute(blocks[step], "zh", pairs).astype(F32)
    weight_part = (total[:share] / (SIDE * SIDE * SIDE)).reshape(1, share, 2, half)
    return (jnp.where(is_decoder, enc_share, in_share)[None], weight_part)


def solution(mesh):
    split = Mesh(mesh.devices.reshape(2, SIDE, SIDE, SIDE, N_MP), ("sec", "x", "zh", "y", "mp"))
    dp = ("x", "zh", "y")
    in_specs = (
        P("sec", dp, None),
        P("sec", None, None, "mp"),
        P(dp, "mp"),
        P(dp, "mp"),
        P("mp", dp),
        P("mp", dp),
        P(dp, None),
    )
    out_specs = (P("sec", (*dp, "mp"), None), P("sec", dp, None, "mp"))
    return jax.shard_map(shards, mesh=split, in_specs=in_specs, out_specs=out_specs, check_vma=False)
```

time: 124 us -> 121 us (0.976); the launches traced: 124 us -> 119 us
  waiting for transfers between devices: 65.4 us -> 42.9 us
  starting transfers between devices: 45.2 us -> 54.7 us
  other arithmetic: 1.09 us -> 4.34 us
  local copies, waits for them, and re-layouts: 4.15 us -> 6.99 us
  Pallas kernels: 7.01 us -> 9.28 us
    ppermute x10, waiting for transfers between devices: 35.6 us -> 13.7 us  [mp_move(): return lax.ppermute(value, ('sec', 'mp'), pairs)]
    all_to_all x1 -> x2, starting transfers between devices: 4.62 us -> 10.7 us  [the longest x1 6.94 us: shards(): lax.all_to_all(jnp.where(is_decoder, down, up), ('x', 'y'), 0, 0, tiled=T...]
    ppermute x4 -> x6, starting transfers between devices: 22.5 us -> 27.1 us  [the longest x3 22.2 us: shards(): total = total + lax.ppermute(blocks[step], 'zh', pairs).astype(F32)]
    select_n x1 -> x2, other arithmetic: 0.03 us -> 3.34 us  [the longest x1 2.29 us: shards(): jnp.where(is_decoder, first, second)]
    unnamed x17 -> x29, local copies, waits for them, and re-layouts: 3.35 us -> 6.17 us
    pallas_call x3 -> x7, Pallas kernels: 7.01 us -> 9.28 us  [call(): pl.pallas_call(kernel, out_shape=[jax.ShapeDtypeStruct(shape, kind) for s...]
    all_to_all x1 -> x2, waiting for transfers between devices: 16.2 us -> 15.2 us  [the longest x1 8.4 us: shards(): lax.all_to_all(jnp.where(is_decoder, first, second), ('x', 'y'), 0, 0, ti...]
    ppermute x4 -> x6, waiting for transfers between devices: 13.6 us -> 14 us  [the longest x1 11 us: shards(): second = lax.ppermute(second, 'sec', [(0, 1)])]
  transfers between devices with their start and end apart: 15 -> 18, of which waited for: 6 -> 9; matrix products, arithmetic and copies ran while one was open for 1% -> 1% of each run, Pallas kernels for 0% -> 3%
where the time goes in v2:
time: 121 us; the launch traced here: 119 us
  starting transfers between devices  54.7 us (45%)
  waiting for transfers between devices  42.9 us (35%)
  Pallas kernels  9.28 us (8%)
  local copies, waits for them, and re-layouts  6.99 us (6%)
  other arithmetic  4.34 us (4%)
    ppermute x3, starting transfers between devices, shards(): total = total + lax.ppermute(blocks[step], 'zh', pairs).astype(F32)  22.2 us
    ppermute x10, starting transfers between devices, mp_move(): return lax.ppermute(value, ('sec', 'mp'), pairs)  16.8 us
    ppermute x10, waiting for transfers between devices, mp_move(): return lax.ppermute(value, ('sec', 'mp'), pairs)  13.7 us
    ppermute x1, waiting for transfers between devices, shards(): second = lax.ppermute(second, 'sec', [(0, 1)])  11 us
    pallas_call x7, Pallas kernels, call(): pl.pallas_call(kernel, out_shape=[jax.ShapeDtypeStruct(shape, kind) for s...  9.28 us
    all_to_all x1, waiting for transfers between devices, shards(): lax.all_to_all(jnp.where(is_decoder, first, second), ('x', 'y'), 0, 0, ti...  8.4 us
    all_to_all x1, starting transfers between devices, shards(): lax.all_to_all(jnp.where(is_decoder, down, up), ('x', 'y'), 0, 0, tiled=T...  6.94 us
    all_to_all x1, waiting for transfers between devices, shards(): lax.all_to_all(jnp.where(is_decoder, down, up), ('x', 'y'), 0, 0, tiled=T...  6.77 us
  transfers between devices with their start and end apart: 18, of which 9 were waited for; matrix products, arithmetic and copies ran while one was open for 1% of the time, Pallas kernels for 3%

profile of v2, /device:TPU:1, one launch (start us, length us, event | category | flops | bytes accessed | tf_op | source)
XLA Modules:
  0.0 119.2 jit_solution(18281258094942265908)
XLA Ops:
  0.7 0.0 copy-start
  0.7 0.0 copy-start.3
  0.7 0.0 copy-start.4
  0.7 0.0 copy-start.5
  0.7 0.0 copy-start.7
  0.7 3.3 %copy.9 = bf16[112,8,2,512]{3,1,2,0:T(8,128)(2,1)} copy(bf16[112,8,2,512]{3,2,1,0:T(2,128)(2,1)} %bitcast.11) | data formatting | bytes 3670016
  4.1 0.1 reshape.140.order_ref
  4.3 3.8 %shard_map.86 = (bf16[512,1024]{1,0:T(8,128)(2,1)S(1)}, bf16[128,896]{1,0:T(8,128)(2,1)S(1)}, bf16[128,896]{1,0:T(8,128)(2,1)S(1)}, bf16[128,896]{1,0:T(8,128)(2...) custom-call(s32[1]{0:T(128)} %bitcast.sec_ref, ...), custom_call_target="tpu_custom_call" | custom-call | flops 1879048192 | bytes 4194304 | tf_op jit(solution)/shard_map/pallas_call | solution.py:185
  8.1 0.9 copy-done.10
  9.0 0.8 copy-done.12
  9.8 0.7 copy-done.1
  10.5 0.4 copy-done.8
  10.9 1.3 %collective-permute-start.3 = (bf16[16,56,512]{2,1,0:T(8,128)(2,1)S(1)}, bf16[16,56,512]{2,1,0:T(8,128)(2,1)}, u32[]{:S(2)}, u32[]{:S(2)}) collective-permute-start(bf16[16,56,512]{2,1,0:T(8,128)(2,1)S(1)} %get-tuple-element.39), channel_id=1, source_target_pairs={{0,256},{1,257},{2,258},{3,259},{4,260},{5,261},{6,262},{7,263},{8... | collective-permute-start | bytes 2752520 | tf_op jit(solution)/shard_map/ppermute | solution.py:247
  12.2 11.0 %collective-permute-done.3 = bf16[16,56,512]{2,1,0:T(8,128)(2,1)} collective-permute-done((bf16[16,56,512]{2,1,0:T(8,128)(2,1)S(1)}, bf16[16,56,512]{2,1,0:T(8,128)(2,1)}, u32[]{:S(2)}, u32[]{:S(2)}) %collective-permute-start.3) | collective-permute-done | bytes 917536 | tf_op jit(solution)/shard_map/ppermute | solution.py:247
  23.2 2.3 %broadcast_select_fusion.1 = bf16[16,56,512]{2,1,0:T(8,128)(2,1)} fusion(bf16[16,56,512]{2,1,0:T(8,128)(2,1)S(1)} %get-tuple-element.38, bf16[16,56,512]{2,1,0:T(8,128)(2,1)} %collective-permute-done.3, pred[]{:T(512)S(6)} %eq.3), kind=kLoop, calls=%fused_computation.1 | loop fusion | flops 458752 | bytes 2752513 | tf_op jit(solution)/shard_map/jit(_where)/select_n | solution.py:248
  25.5 3.8 %all-to-all-start = ((bf16[16,56,512]{2,1,0:T(8,128)(2,1)}), bf16[16,56,512]{2,1,0:T(8,128)(2,1)S(1)}, u32[]{:S(2)}, u32[]{:S(2)}) async-start(bf16[16,56,512]{2,1,0:T(8,128)(2,1)} %broadcast_select_fusion.1), calls=%async_computation | async-start | bytes 1835008 | tf_op jit(solution)/shard_map/all_to_all | solution.py:248
  29.2 0.7 collective-permute-start.2
  29.9 0.7 collective-permute-start.1
  30.6 0.7 collective-permute-start
  31.3 0.1 add_convert_fusion.1
  31.5 1.3 %collective-permute-start.4 = (bf16[128,896]{1,0:T(8,128)(2,1)S(1)}, bf16[128,896]{1,0:T(8,128)(2,1)S(1)}, u32[]{:S(2)}, u32[]{:S(2)}) collective-permute-start(bf16[128,896]{1,0:T(8,128)(2,1)S(1)} %add_convert_fusion.1), channel_id=1, source_target_pairs={{0,256},{1,257},{2,258},{3,259},{4,260},{5,261},{6,262},{7,263},{8... | collective-permute-start | bytes 688136 | tf_op jit(solution)/shard_map/ppermute | solution.py:198
  32.8 1.3 %collective-permute-start.5 = (bf16[128,896]{1,0:T(8,128)(2,1)S(1)}, bf16[128,896]{1,0:T(8,128)(2,1)S(1)}, u32[]{:S(2)}, u32[]{:S(2)}) collective-permute-start(bf16[128,896]{1,0:T(8,128)(2,1)S(1)} %add_convert_fusion.1), channel_id=1, source_target_pairs={{0,257},{1,258},{2,259},{3,256},{4,261},{5,262},{6,263},{7,260},{8... | collective-permute-start | bytes 688136 | tf_op jit(solution)/shard_map/ppermute | solution.py:198
  34.1 1.3 %collective-permute-start.6 = (bf16[128,896]{1,0:T(8,128)(2,1)S(1)}, bf16[128,896]{1,0:T(8,128)(2,1)S(1)}, u32[]{:S(2)}, u32[]{:S(2)}) collective-permute-start(bf16[128,896]{1,0:T(8,128)(2,1)S(1)} %add_convert_fusion.1), channel_id=1, source_target_pairs={{0,258},{1,259},{2,256},{3,257},{4,262},{5,263},{6,260},{7,261},{8... | collective-permute-start | bytes 688136 | tf_op jit(solution)/shard_map/ppermute | solution.py:198
  35.4 1.3 %collective-permute-start.7 = (bf16[128,896]{1,0:T(8,128)(2,1)S(1)}, bf16[128,896]{1,0:T(8,128)(2,1)S(1)}, u32[]{:S(2)}, u32[]{:S(2)}) collective-permute-start(bf16[128,896]{1,0:T(8,128)(2,1)S(1)} %add_convert_fusion.1), channel_id=1, source_target_pairs={{0,259},{1,256},{2,257},{3,258},{4,263},{5,260},{6,261},{7,262},{8... | collective-permute-start | bytes 688136 | tf_op jit(solution)/shard_map/ppermute | solution.py:198
  36.7 8.4 %all-to-all-done.piece_ref = bf16[16,56,512]{2,1,0:T(8,128)(2,1)S(1)} async-done(((bf16[16,56,512]{2,1,0:T(8,128)(2,1)}), bf16[16,56,512]{2,1,0:T(8,128)(2,1)S(1)}, u32[]{:S(2)}, u32[]{:S(2)}) %all-to-all-start) | async-done | bytes 917536 | tf_op jit(solution)/shard_map/all_to_all | solution.py:248
  45.1 0.2 shard_map.88.early_ref
  45.2 4.5 %collective-permute-done.4.got0 = bf16[128,896]{1,0:T(8,128)(2,1)S(1)} collective-permute-done((bf16[128,896]{1,0:T(8,128)(2,1)S(1)}, bf16[128,896]{1,0:T(8,128)(2,1)S(1)}, u32[]{:S(2)}, u32[]{:S(2)}) %collective-permute-start.4) | collective-permute-done | bytes 229408 | tf_op jit(solution)/shard_map/ppermute | solution.py:198
  49.7 4.4 %collective-permute-done.5.got1 = bf16[128,896]{1,0:T(8,128)(2,1)S(1)} collective-permute-done((bf16[128,896]{1,0:T(8,128)(2,1)S(1)}, bf16[128,896]{1,0:T(8,128)(2,1)S(1)}, u32[]{:S(2)}, u32[]{:S(2)}) %collective-permute-start.5) | collective-permute-done | bytes 229408 | tf_op jit(solution)/shard_map/ppermute | solution.py:198
  54.2 4.8 %collective-permute-done.6.got2 = bf16[128,896]{1,0:T(8,128)(2,1)S(1)} collective-permute-done((bf16[128,896]{1,0:T(8,128)(2,1)S(1)}, bf16[128,896]{1,0:T(8,128)(2,1)S(1)}, u32[]{:S(2)}, u32[]{:S(2)}) %collective-permute-start.6) | collective-permute-done | bytes 229408 | tf_op jit(solution)/shard_map/ppermute | solution.py:198
  58.9 1.8 %shard_map.89 = (bf16[512,896]{1,0:T(8,128)(2,1)S(1)}, bf16[16,56,512]{2,1,0:T(8,128)(2,1)S(1)}) custom-call(s32[1]{0:T(128)} %bitcast.sec_ref, s32[1]{0:T(128)} %bitcast.1.mp_ref, s32[1,896]{1,0:T(1,128)S(1)} %reshape.140.order_ref, bf16[512,512]{1,0:T(8,128)(2,1)S(1)} %copy-done.13, bf16[128,896]{1,0:T(8,128)(2,1)S(1)} %collective-permute-done.4.got0, ...), custom_call_target="tpu_custom_call" | custom-call | flops 1409286144 | bytes 4194304 | tf_op jit(solution)/shard_map/pallas_call | solution.py:185
  60.7 1.3 %collective-permute-start.11 = (bf16[16,56,512]{2,1,0:T(8,128)(2,1)S(1)}, bf16[16,56,512]{2,1,0:T(8,128)(2,1)S(1)}, u32[]{:S(2)}, u32[]{:S(2)}) collective-permute-start(bf16[16,56,512]{2,1,0:T(8,128)(2,1)S(1)} %get-tuple-element.49), channel_id=1, source_target_pairs={{256,0},{257,1},{258,2},{259,3},{260,4},{261,5},{262,6},{263,7},{2... | collective-permute-start | bytes 2752520 | tf_op jit(solution)/shard_map/ppermute | solution.py:255
  62.1 3.4 %shard_map.90 = (bf16[16,56,512]{2,1,0:T(8,128)(2,1)S(1)}, bf16[128,896]{1,0:T(8,128)(2,1)S(1)}, bf16[128,896]{1,0:T(8,128)(2,1)S(1)}, bf16[128,896]{1,0:T(8,128)(2,1)S(1)}, bf16[128,896]{1,0:T(8,128)(2,1)S(1)}) custom-call(s32[1]{0:T(128)} %bitcast.sec_ref, s32[1]{0:T(128)} %bitcast.1.mp_ref, bf16[512,896]{1,0:T(8,128)(2,1)S(1)} %copy-done.11, ...), custom_call_target="tpu_custom_call" | custom-call | flops 1409286144 | bytes 4194304 | tf_op jit(solution)/shard_map/pallas_call | solution.py:185
  65.5 1.0 broadcast_select_fusion
  66.5 6.9 %all-to-all-start.1 = ((bf16[16,56,512]{2,1,0:T(8,128)(2,1)}), bf16[16,56,512]{2,1,0:T(8,128)(2,1)S(1)}, u32[]{:S(2)}, u32[]{:S(2)}) async-start(bf16[16,56,512]{2,1,0:T(8,128)(2,1)} %broadcast_select_fusion), calls=%async_computation.1 | async-start | bytes 1835008 | tf_op jit(solution)/shard_map/all_to_all | solution.py:265
  73.5 4.8 %collective-permute-start.10 = (bf16[128,896]{1,0:T(8,128)(2,1)S(1)}, bf16[128,896]{1,0:T(8,128)(2,1)S(1)}, u32[]{:S(2)}, u32[]{:S(2)}) collective-permute-start(bf16[128,896]{1,0:T(8,128)(2,1)S(1)} %get-tuple-element.48), channel_id=1, source_target_pairs={{256,259},{257,256},{258,257},{259,258},{260,263},{261,260},{262,2... | collective-permute-start | bytes 688136 | tf_op jit(solution)/shard_map/ppermute | solution.py:198
  78.3 1.9 %collective-permute-start.9 = (bf16[128,896]{1,0:T(8,128)(2,1)S(1)}, bf16[128,896]{1,0:T(8,128)(2,1)S(1)}, u32[]{:S(2)}, u32[]{:S(2)}) collective-permute-start(bf16[128,896]{1,0:T(8,128)(2,1)S(1)} %get-tuple-element.47), channel_id=1, source_target_pairs={{256,257},{257,258},{258,259},{259,256},{260,261},{261,262},{262,2... | collective-permute-start | bytes 688136 | tf_op jit(solution)/shard_map/ppermute | solution.py:198
  80.2 2.9 %collective-permute-start.8 = (bf16[128,896]{1,0:T(8,128)(2,1)S(1)}, bf16[128,896]{1,0:T(8,128)(2,1)S(1)}, u32[]{:S(2)}, u32[]{:S(2)}) collective-permute-start(bf16[128,896]{1,0:T(8,128)(2,1)S(1)} %get-tuple-element.46), channel_id=1, source_target_pairs={{256,258},{257,259},{258,256},{259,257},{260,262},{261,263},{262,2... | collective-permute-start | bytes 688136 | tf_op jit(solution)/shard_map/ppermute | solution.py:198
  83.2 6.8 %all-to-all-done.1.piece_ref = bf16[16,56,512]{2,1,0:T(8,128)(2,1)S(1)} async-done(((bf16[16,56,512]{2,1,0:T(8,128)(2,1)}), bf16[16,56,512]{2,1,0:T(8,128)(2,1)S(1)}, u32[]{:S(2)}, u32[]{:S(2)}) %all-to-all-start.1) | async-done | bytes 917536 | tf_op jit(solution)/shard_map/all_to_all | solution.py:265
  89.9 0.2 shard_map.91
  90.1 2.3 %collective-permute-start.12 = (bf16[64,512]{1,0:T(8,128)(2,1)S(1)}, bf16[64,512]{1,0:T(8,128)(2,1)S(1)}, u32[]{:S(2)}, u32[]{:S(2)}) collective-permute-start(bf16[64,512]{1,0:T(8,128)(2,1)S(1)} %get-tuple-element.53), channel_id=1, source_target_pairs={{0,256},{256,0},{1,257},{257,1},{2,258},{258,2},{3,259},{259,3},{4... | collective-permute-start | bytes 196616 | tf_op jit(solution)/shard_map/ppermute | solution.py:267
  92.4 0.9 collective-permute-done.12.came_ref
  93.3 10.0 %collective-permute-start.15 = (bf16[16,1024]{1,0:T(8,128)(2,1)S(1)}, bf16[16,1024]{1,0:T(8,128)(2,1)S(1)}, u32[]{:S(2)}, u32[]{:S(2)}) collective-permute-start(bf16[16,1024]{1,0:T(8,128)(2,1)S(1)} %get-tuple-element.57), channel_id=1, source_target_pairs={{0,48},{16,0},{32,16},{48,32},{1,49},{17,1},{33,17},{49,33},{2,50}... | collective-permute-start | bytes 98312 | tf_op jit(solution)/shard_map/ppermute | solution.py:272
  103.3 5.8 %collective-permute-start.14 = (bf16[16,1024]{1,0:T(8,128)(2,1)S(1)}, bf16[16,1024]{1,0:T(8,128)(2,1)S(1)}, u32[]{:S(2)}, u32[]{:S(2)}) collective-permute-start(bf16[16,1024]{1,0:T(8,128)(2,1)S(1)} %get-tuple-element.56), channel_id=1, source_target_pairs={{0,32},{16,48},{32,0},{48,16},{1,33},{17,49},{33,1},{49,17},{2,34}... | collective-permute-start | bytes 98312 | tf_op jit(solution)/shard_map/ppermute | solution.py:272
  109.1 6.4 %collective-permute-start.13 = (bf16[16,1024]{1,0:T(8,128)(2,1)S(1)}, bf16[16,1024]{1,0:T(8,128)(2,1)S(1)}, u32[]{:S(2)}, u32[]{:S(2)}) collective-permute-start(bf16[16,1024]{1,0:T(8,128)(2,1)S(1)} %get-tuple-element.55), channel_id=1, source_target_pairs={{0,16},{16,32},{32,48},{48,0},{1,17},{17,33},{33,49},{49,1},{2,18}... | collective-permute-start | bytes 98312 | tf_op jit(solution)/shard_map/ppermute | solution.py:272
  115.5 0.8 fusion.1
  116.4 0.3 collective-permute-done.14
  116.7 1.8 %collective-permute-done.13 = bf16[16,1024]{1,0:T(8,128)(2,1)S(1)} collective-permute-done((bf16[16,1024]{1,0:T(8,128)(2,1)S(1)}, bf16[16,1024]{1,0:T(8,128)(2,1)S(1)}, u32[]{:S(2)}, u32[]{:S(2)}) %collective-permute-start.13) | collective-permute-done | bytes 32800 | tf_op jit(solution)/shard_map/ppermute | solution.py:272
  118.6 0.7 reshape.142
  (32 shorter events, 0.1 us)
Async XLA Ops:
  0.7 3.5 %copy-start = (bf16[1,512,896]{2,1,0:T(8,128)(2,1)S(1)}, bf16[1,512,896]{2,1,0:T(8,128)(2,1)}, u32[]{:S(2)}) copy-start(bf16[1,512,896]{2,1,0:T(8,128)(2,1)} %param.7) | copy-start | bytes 2752516
  0.7 3.5 %copy-start.3 = (bf16[128,512]{1,0:T(8,128)(2,1)S(1)}, bf16[128,512]{1,0:T(8,128)(2,1)}, u32[]{:S(2)}) copy-start(bf16[128,512]{1,0:T(8,128)(2,1)} %query_ref.1) | copy-start | bytes 393220
  0.7 3.5 %copy-start.4 = (bf16[128,512]{1,0:T(8,128)(2,1)S(1)}, bf16[128,512]{1,0:T(8,128)(2,1)}, u32[]{:S(2)}) copy-start(bf16[128,512]{1,0:T(8,128)(2,1)} %grad_ref.1) | copy-start | bytes 393220
  0.7 3.5 %copy-start.5 = (f32[4,128]{1,0:T(4,128)S(1)}, f32[4,128]{1,0:T(4,128)}, u32[]{:S(2)}) copy-start(f32[4,128]{1,0:T(4,128)} %lse_ref.1) | copy-start | bytes 6148
  0.7 3.5 %copy-start.6 = (f32[4,128]{1,0:T(4,128)S(1)}, f32[4,128]{1,0:T(4,128)}, u32[]{:S(2)}) copy-start(f32[4,128]{1,0:T(4,128)} %delta_ref.1) | copy-start | bytes 6148
  0.7 3.5 %copy-start.7 = (s32[2,2]{1,0:T(2,128)S(1)}, s32[2,2]{1,0:T(2,128)}, u32[]{:S(2)}) copy-start(s32[2,2]{1,0:T(2,128)} %span_ref.1) | copy-start | bytes 52
  8.1 0.9 copy-start.10
  9.0 0.8 copy-start.12
  9.8 0.7 copy-start.1
  9.8 1.1 copy-start.8
  10.9 12.3 %collective-permute-start.3 = (bf16[16,56,512]{2,1,0:T(8,128)(2,1)S(1)}, bf16[16,56,512]{2,1,0:T(8,128)(2,1)}, u32[]{:S(2)}, u32[]{:S(2)}) collective-permute-start(bf16[16,56,512]{2,1,0:T(8,128)(2,1)S(1)} %get-tuple-element.39), channel_id=1, source_target_pairs={{0,256},{1,257},{2,258},{3,259},{4,260},{5,261},{6,262},{7,263},{8... | collective-permute-start | bytes 2752520 | tf_op jit(solution)/shard_map/ppermute | solution.py:247
  23.2 6.1 %copy-start.2 = (bf16[128,896]{1,0:T(8,128)(2,1)S(1)}, bf16[128,896]{1,0:T(8,128)(2,1)}, u32[]{:S(2)}) copy-start(bf16[128,896]{1,0:T(8,128)(2,1)} %copy-done.1) | copy-start | bytes 688132
  25.5 33.5 %copy-start.13 = (bf16[512,512]{1,0:T(8,128)(2,1)S(1)}, bf16[512,512]{1,0:T(8,128)(2,1)}, u32[]{:S(2)}) copy-start(bf16[512,512]{1,0:T(8,128)(2,1)} %copy-done.12) | copy-start | bytes 1572868
  25.5 19.6 %all-to-all-start = ((bf16[16,56,512]{2,1,0:T(8,128)(2,1)}), bf16[16,56,512]{2,1,0:T(8,128)(2,1)S(1)}, u32[]{:S(2)}, u32[]{:S(2)}) async-start(bf16[16,56,512]{2,1,0:T(8,128)(2,1)} %broadcast_select_fusion.1), calls=%async_computation | async-start | bytes 1835008 | tf_op jit(solution)/shard_map/all_to_all | solution.py:248
  29.2 2.1 %collective-permute-start.2 = (bf16[128,896]{1,0:T(8,128)(2,1)S(1)}, bf16[128,896]{1,0:T(8,128)(2,1)S(1)}, u32[]{:S(2)}, u32[]{:S(2)}) collective-permute-start(bf16[128,896]{1,0:T(8,128)(2,1)S(1)} %copy-done.2), channel_id=1, source_target_pairs={{0,3},{1,0},{2,1},{3,2},{4,7},{5,4},{6,5},{7,6},{8,11},{9,8},{10,9... | collective-permute-start | bytes 688136 | tf_op jit(solution)/shard_map/ppermute | solution.py:198
  29.9 1.4 %collective-permute-start.1 = (bf16[128,896]{1,0:T(8,128)(2,1)S(1)}, bf16[128,896]{1,0:T(8,128)(2,1)S(1)}, u32[]{:S(2)}, u32[]{:S(2)}) collective-permute-start(bf16[128,896]{1,0:T(8,128)(2,1)S(1)} %get-tuple-element.32), channel_id=1, source_target_pairs={{0,1},{1,2},{2,3},{3,0},{4,5},{5,6},{6,7},{7,4},{8,9},{9,10},{10,1... | collective-permute-start | bytes 688136 | tf_op jit(solution)/shard_map/ppermute | solution.py:198
  30.6 0.7 collective-permute-start
  31.5 18.3 %collective-permute-start.4 = (bf16[128,896]{1,0:T(8,128)(2,1)S(1)}, bf16[128,896]{1,0:T(8,128)(2,1)S(1)}, u32[]{:S(2)}, u32[]{:S(2)}) collective-permute-start(bf16[128,896]{1,0:T(8,128)(2,1)S(1)} %add_convert_fusion.1), channel_id=1, source_target_pairs={{0,256},{1,257},{2,258},{3,259},{4,260},{5,261},{6,262},{7,263},{8... | collective-permute-start | bytes 688136 | tf_op jit(solution)/shard_map/ppermute | solution.py:198
  32.8 21.4 %collective-permute-start.5 = (bf16[128,896]{1,0:T(8,128)(2,1)S(1)}, bf16[128,896]{1,0:T(8,128)(2,1)S(1)}, u32[]{:S(2)}, u32[]{:S(2)}) collective-permute-start(bf16[128,896]{1,0:T(8,128)(2,1)S(1)} %add_convert_fusion.1), channel_id=1, source_target_pairs={{0,257},{1,258},{2,259},{3,256},{4,261},{5,262},{6,263},{7,260},{8... | collective-permute-start | bytes 688136 | tf_op jit(solution)/shard_map/ppermute | solution.py:198
  34.1 24.9 %collective-permute-start.6 = (bf16[128,896]{1,0:T(8,128)(2,1)S(1)}, bf16[128,896]{1,0:T(8,128)(2,1)S(1)}, u32[]{:S(2)}, u32[]{:S(2)}) collective-permute-start(bf16[128,896]{1,0:T(8,128)(2,1)S(1)} %add_convert_fusion.1), channel_id=1, source_target_pairs={{0,258},{1,259},{2,256},{3,257},{4,262},{5,263},{6,260},{7,261},{8... | collective-permute-start | bytes 688136 | tf_op jit(solution)/shard_map/ppermute | solution.py:198
  35.4 23.6 %collective-permute-start.7 = (bf16[128,896]{1,0:T(8,128)(2,1)S(1)}, bf16[128,896]{1,0:T(8,128)(2,1)S(1)}, u32[]{:S(2)}, u32[]{:S(2)}) collective-permute-start(bf16[128,896]{1,0:T(8,128)(2,1)S(1)} %add_convert_fusion.1), channel_id=1, source_target_pairs={{0,259},{1,256},{2,257},{3,258},{4,263},{5,260},{6,261},{7,262},{8... | collective-permute-start | bytes 688136 | tf_op jit(solution)/shard_map/ppermute | solution.py:198
  58.9 3.1 %copy-start.9 = (f32[512,512]{1,0:T(8,128)S(1)}, f32[512,512]{1,0:T(8,128)}, u32[]{:S(2)}) copy-start(f32[512,512]{1,0:T(8,128)} %copy-done.8) | copy-start | bytes 3145732
  58.9 3.1 %copy-start.11 = (bf16[512,896]{1,0:T(8,128)(2,1)S(1)}, bf16[512,896]{1,0:T(8,128)(2,1)}, u32[]{:S(2)}) copy-start(bf16[512,896]{1,0:T(8,128)(2,1)} %copy-done.10) | copy-start | bytes 2752516
  60.7 4.8 %collective-permute-start.11 = (bf16[16,56,512]{2,1,0:T(8,128)(2,1)S(1)}, bf16[16,56,512]{2,1,0:T(8,128)(2,1)S(1)}, u32[]{:S(2)}, u32[]{:S(2)}) collective-permute-start(bf16[16,56,512]{2,1,0:T(8,128)(2,1)S(1)} %get-tuple-element.49), channel_id=1, source_target_pairs={{256,0},{257,1},{258,2},{259,3},{260,4},{261,5},{262,6},{263,7},{2... | collective-permute-start | bytes 2752520 | tf_op jit(solution)/shard_map/ppermute | solution.py:255
  66.5 23.4 %all-to-all-start.1 = ((bf16[16,56,512]{2,1,0:T(8,128)(2,1)}), bf16[16,56,512]{2,1,0:T(8,128)(2,1)S(1)}, u32[]{:S(2)}, u32[]{:S(2)}) async-start(bf16[16,56,512]{2,1,0:T(8,128)(2,1)} %broadcast_select_fusion), calls=%async_computation.1 | async-start | bytes 1835008 | tf_op jit(solution)/shard_map/all_to_all | solution.py:265
  73.5 35.6 %collective-permute-start.10 = (bf16[128,896]{1,0:T(8,128)(2,1)S(1)}, bf16[128,896]{1,0:T(8,128)(2,1)S(1)}, u32[]{:S(2)}, u32[]{:S(2)}) collective-permute-start(bf16[128,896]{1,0:T(8,128)(2,1)S(1)} %get-tuple-element.48), channel_id=1, source_target_pairs={{256,259},{257,256},{258,257},{259,258},{260,263},{261,260},{262,2... | collective-permute-start | bytes 688136 | tf_op jit(solution)/shard_map/ppermute | solution.py:198
  78.3 37.2 %collective-permute-start.9 = (bf16[128,896]{1,0:T(8,128)(2,1)S(1)}, bf16[128,896]{1,0:T(8,128)(2,1)S(1)}, u32[]{:S(2)}, u32[]{:S(2)}) collective-permute-start(bf16[128,896]{1,0:T(8,128)(2,1)S(1)} %get-tuple-element.47), channel_id=1, source_target_pairs={{256,257},{257,258},{258,259},{259,256},{260,261},{261,262},{262,2... | collective-permute-start | bytes 688136 | tf_op jit(solution)/shard_map/ppermute | solution.py:198
  80.2 35.3 %collective-permute-start.8 = (bf16[128,896]{1,0:T(8,128)(2,1)S(1)}, bf16[128,896]{1,0:T(8,128)(2,1)S(1)}, u32[]{:S(2)}, u32[]{:S(2)}) collective-permute-start(bf16[128,896]{1,0:T(8,128)(2,1)S(1)} %get-tuple-element.46), channel_id=1, source_target_pairs={{256,258},{257,259},{258,256},{259,257},{260,262},{261,263},{262,2... | collective-permute-start | bytes 688136 | tf_op jit(solution)/shard_map/ppermute | solution.py:198
  90.1 3.2 %collective-permute-start.12 = (bf16[64,512]{1,0:T(8,128)(2,1)S(1)}, bf16[64,512]{1,0:T(8,128)(2,1)S(1)}, u32[]{:S(2)}, u32[]{:S(2)}) collective-permute-start(bf16[64,512]{1,0:T(8,128)(2,1)S(1)} %get-tuple-element.53), channel_id=1, source_target_pairs={{0,256},{256,0},{1,257},{257,1},{2,258},{258,2},{3,259},{259,3},{4... | collective-permute-start | bytes 196616 | tf_op jit(solution)/shard_map/ppermute | solution.py:267
  93.3 23.1 %collective-permute-start.15 = (bf16[16,1024]{1,0:T(8,128)(2,1)S(1)}, bf16[16,1024]{1,0:T(8,128)(2,1)S(1)}, u32[]{:S(2)}, u32[]{:S(2)}) collective-permute-start(bf16[16,1024]{1,0:T(8,128)(2,1)S(1)} %get-tuple-element.57), channel_id=1, source_target_pairs={{0,48},{16,0},{32,16},{48,32},{1,49},{17,1},{33,17},{49,33},{2,50}... | collective-permute-start | bytes 98312 | tf_op jit(solution)/shard_map/ppermute | solution.py:272
  103.3 13.4 %collective-permute-start.14 = (bf16[16,1024]{1,0:T(8,128)(2,1)S(1)}, bf16[16,1024]{1,0:T(8,128)(2,1)S(1)}, u32[]{:S(2)}, u32[]{:S(2)}) collective-permute-start(bf16[16,1024]{1,0:T(8,128)(2,1)S(1)} %get-tuple-element.56), channel_id=1, source_target_pairs={{0,32},{16,48},{32,0},{48,16},{1,33},{17,49},{33,1},{49,17},{2,34}... | collective-permute-start | bytes 98312 | tf_op jit(solution)/shard_map/ppermute | solution.py:272
  109.1 9.4 %collective-permute-start.13 = (bf16[16,1024]{1,0:T(8,128)(2,1)S(1)}, bf16[16,1024]{1,0:T(8,128)(2,1)S(1)}, u32[]{:S(2)}, u32[]{:S(2)}) collective-permute-start(bf16[16,1024]{1,0:T(8,128)(2,1)S(1)} %get-tuple-element.55), channel_id=1, source_target_pairs={{0,16},{16,32},{32,48},{48,0},{1,17},{17,33},{33,49},{49,1},{2,18}... | collective-permute-start | bytes 98312 | tf_op jit(solution)/shard_map/ppermute | solution.py:272

commit v3 on v2

--- a/solution.py
+++ b/solution.py
@@ -18,7 +18,7 @@
 BF16 = jnp.bfloat16
 NT = (((1,), (1,)), ((), ()))
 TN = (((0,), (0,)), ((), ()))
-VMEM_LIMIT = 48 * 1024 * 1024
+VMEM_LIMIT = 12 * 1024 * 1024
 
 
 def mm(left, right, dims=(((1,), (0,)), ((), ()))):
@@ -72,19 +72,16 @@
     return mm(rows, jnp.where(place, 1.0, 0.0).astype(BF16)).astype(BF16)
 
 
-def store_chunks(out_ref, value):
-    chunk = out_ref.shape[1]
+def store_chunks(out_ref, value, column=0):
+    chunk, width = out_ref.shape[1], value.shape[1]
     for index in range(out_ref.shape[0]):
-        out_ref[index] = value[index * chunk:(index + 1) * chunk, :].astype(BF16)
-
-
-def decoder_weight_kernel(sec_ref, rows_ref, kv_grad_ref, order_ref, first_ref, second_ref):
+        out_ref[index, :, column:column + width] = value[index * chunk:(index + 1) * chunk, :].astype(BF16)
+
+
+def decoder_weight_kernel(sec_ref, rows_ref, kv_grad_ref, order_ref, partial_ref):
     @on_section(sec_ref, 0)
     def work():
-        half = kv_grad_ref.shape[1] // 2
-        rows = ordered(rows_ref[...], order_ref)
-        store_chunks(second_ref, mm(rows, kv_grad_ref[:, half:], TN))
-        store_chunks(first_ref, mm(rows, kv_grad_ref[:, :half], TN))
+        store_chunks(partial_ref, mm(ordered(rows_ref[...], order_ref), kv_grad_ref[...], TN))
 
 
 def prepare_kernel(rows_ref, weight_ref, order_ref, ordered_ref, hidden_ref, slope_ref):
@@ -113,28 +110,24 @@
         prepare_kernel(rows_ref, weight_ref, order_ref, ordered_ref, hidden_ref, slope_ref)
 
 
-def down_kernel(sec_ref, mp_ref, order_ref, hidden_ref, got0, got1, got2, got3, arrived_ref, second_ref):
-    @on_section(sec_ref, 1)
-    def work():
-        for step, got in enumerate((got0, got3, got2, got1)):
-            arrived_ref[block_rows(lax.rem(mp_ref[0] + step, N_MP)), :] = got[...]
-        store_chunks(second_ref, mm(ordered(arrived_ref[...], order_ref), hidden_ref[...], TN))
-
-
-def up_kernel(sec_ref, mp_ref, ordered_ref, weight_ref, slope_ref, arrived_ref, first_ref, part0, part1, part2, part3,
-              part_ref):
+def encoder_kernel(sec_ref, mp_ref, order_ref, ordered_ref, weight_ref, hidden_ref, slope_ref, got0, got1, got2, got3,
+                   keep_ref, partial_ref, part0, part1, part2, part3, arrived_ref, part_ref):
+    del keep_ref
     @on_section(sec_ref, 1)
     def work():
         half = weight_ref.shape[1] // 2
-        hidden_grad = mm(arrived_ref[...], weight_ref[:, half:])
-        pre_grad = (hidden_grad * slope_ref[...]).astype(BF16)
-        store_chunks(first_ref, mm(ordered_ref[...], pre_grad, TN))
+        for step, got in enumerate((got0, got3, got2, got1)):
+            arrived_ref[block_rows(lax.rem(mp_ref[0] + step, N_MP)), :] = got[...]
+        arrived = arrived_ref[...]
+        pre_grad = (mm(arrived, weight_ref[:, half:]) * slope_ref[...]).astype(BF16)
+        store_chunks(partial_ref, mm(ordered(arrived, order_ref), hidden_ref[...], TN), half)
+        store_chunks(partial_ref, mm(ordered_ref[...], pre_grad, TN))
         part_ref[...] = mm(pre_grad, weight_ref[:, :half], NT).astype(BF16)
         for step, part in enumerate((part0, part1, part2, part3)):
             part[...] = part_ref[block_rows(lax.rem(mp_ref[0] + step, N_MP)), :]
 
 
-def chunk_sum(piece_ref, total_ref):
+def sum_kernel(zh_ref, piece_ref, out0, out1, out2, out3, total_ref):
     total = piece_ref[0].astype(F32)
     for source in range(1, piece_ref.shape[0]):
         total = total + piece_ref[source].astype(F32)
@@ -142,35 +135,12 @@
     share = count // SIDE
     total_ref[:count, :] = total
     total_ref[count:, :] = jnp.zeros((total_ref.shape[0] - count, total_ref.shape[1]), F32)
-    return jnp.concatenate(
-        [total_ref[index * share:index * share + PADDED, :] for index in range(SIDE)], axis=0
-    ).astype(BF16)
-
-
-def early_sum_kernel(piece_ref, out_ref, total_ref):
-    out_ref[...] = chunk_sum(piece_ref, total_ref)
-
-
-def late_sum_kernel(sec_ref, piece_ref, early_ref, own_ref, other_ref, total_ref):
-    late = chunk_sum(piece_ref, total_ref)
-
-    @pl.when(sec_ref[0] == 0)
-    def decoder():
-        own_ref[...] = early_ref[...]
-        other_ref[...] = late
-
-    @pl.when(sec_ref[0] != 0)
-    def encoder():
-        own_ref[...] = late
-        other_ref[...] = early_ref[...]
-
-
-def join_kernel(zh_ref, own_ref, came_ref, out0, out1, out2, out3):
-    half = own_ref.shape[1]
-    for step, out in enumerate((out0, out1, out2, out3)):
-        rows = pl.ds(pl.multiple_of(lax.rem(zh_ref[0] + step, SIDE) * PADDED, PADDED), PADDED)
-        out[:, :half] = own_ref[rows, :]
-        out[:, half:] = came_ref[rows, :]
+    for block in range(SIDE):
+        rows = total_ref[block * share:block * share + PADDED, :].astype(BF16)
+        for step, out in enumerate((out0, out1, out2, out3)):
+            @pl.when(lax.rem(zh_ref[0] + step, SIDE) == block)
+            def store(rows=rows, out=out):
+                out[...] = rows
 
 
 def vmem():
@@ -181,13 +151,14 @@
     return pl.BlockSpec(memory_space=pltpu.SMEM)
 
 
-def call(kernel, outs, args, scalars=0, scratch=(), flops=0):
+def call(kernel, outs, args, scalars=0, scratch=(), flops=0, alias=None):
     return pl.pallas_call(
         kernel,
         out_shape=[jax.ShapeDtypeStruct(shape, kind) for shape, kind in outs],
         in_specs=[smem()] * scalars + [vmem()] * (len(args) - scalars),
         out_specs=[vmem()] * len(outs),
         scratch_shapes=list(scratch),
+        input_output_aliases=alias or {},
         compiler_params=pltpu.CompilerParams(vmem_limit_bytes=VMEM_LIMIT),
         cost_estimate=pl.CostEstimate(flops=flops, bytes_accessed=4 << 20, transcendentals=0),
     )(*args)
@@ -198,10 +169,14 @@
     return lax.ppermute(value, ("sec", "mp"), pairs)
 
 
-def mp_sum(parts, section):
+def mp_parts(parts, section):
+    return [parts[0]] + [mp_move(parts[step], section, section, step) for step in (2, 1, 3)]
+
+
+def mp_sum(parts):
     total = parts[0].astype(F32)
-    for step in (2, 1, 3):
-        total = total + mp_move(parts[step], section, section, step).astype(F32)
+    for part in parts[1:]:
+        total = total + part.astype(F32)
     return total.astype(BF16)
 
 
@@ -222,11 +197,10 @@
     order = order.transpose(0, 2, 1, 3).reshape(1, width)
 
     part_outs = [((quarter, width), BF16)] * N_MP
-    piece_out = ((pieces, chunk, half), BF16)
+    piece_out = ((pieces, chunk, 2 * half), BF16)
     col_out = ((local_rows, half), BF16)
-    sum_out = ((SIDE * PADDED, half), BF16)
     part_scratch = pltpu.VMEM((local_rows, width), BF16)
-    sum_scratch = pltpu.VMEM((SIDE * PADDED, half), F32)
+    sum_scratch = pltpu.VMEM((SIDE * PADDED, 2 * half), F32)
     cols_flops = 2 * local_rows * width * half
 
     ordered_out = ((local_rows, width), BF16)
@@ -238,38 +212,39 @@
         scratch=[pltpu.VMEM((local_rows, 2 * half), BF16), part_scratch],
         flops=4 * cols_flops,
     )
-    enc_share = mp_sum(enc_parts, 0)
-    got = [mp_move(enc_share, 0, 1, step) for step in range(N_MP)]
-
-    first, second = call(
-        decoder_weight_kernel, [piece_out] * 2, (sec, rows, kv_grad, order), scalars=1, flops=4 * cols_flops
-    )
-    second = lax.ppermute(second, "sec", [(0, 1)])
-    early = lax.all_to_all(jnp.where(is_decoder, first, second), ("x", "y"), 0, 0, tiled=True)
-    (early_sum,) = call(early_sum_kernel, [sum_out], (early,), scratch=[sum_scratch])
-    early_sum, *got = lax.optimization_barrier((early_sum, *got))
-
-    arrived, down = call(
-        down_kernel, [ordered_out, piece_out], (sec, mp, order, hidden, *got), scalars=2, flops=3 * cols_flops
-    )
-    down = lax.ppermute(down, "sec", [(1, 0)])
-    up, *in_parts = call(
-        up_kernel,
+    with jax.named_scope("enc_reduce"):
+        enc_parts = mp_parts(enc_parts, 0)
+    enc_share = mp_sum(enc_parts)
+    with jax.named_scope("enc_gather"):
+        got = [mp_move(enc_share, 0, 1, step) for step in (2, 1, 3, 0)]
+        got = [got[3], got[1], got[0], got[2]]
+
+    (partial,) = call(
+        decoder_weight_kernel, [piece_out], (sec, rows, kv_grad, order), scalars=1, flops=4 * cols_flops
+    )
+    partial, *in_parts = call(
+        encoder_kernel,
         [piece_out] + part_outs,
-        (sec, mp, ordered_rows, weights, slope, arrived),
+        (sec, mp, order, ordered_rows, weights, hidden, slope, *got, partial),
         scalars=2,
-        scratch=[part_scratch],
-        flops=3 * cols_flops,
-    )
-    in_share = mp_sum(in_parts, 1)
-    late = lax.all_to_all(jnp.where(is_decoder, down, up), ("x", "y"), 0, 0, tiled=True)
-    own, other = call(late_sum_kernel, [sum_out] * 2, (sec, late, early_sum), scalars=1, scratch=[sum_scratch])
-    came = lax.ppermute(other, "sec", [(0, 1), (1, 0)])
-    blocks = call(join_kernel, [((PADDED, 2 * half), BF16)] * SIDE, (zh, own, came), scalars=1)
+        scratch=[part_scratch] * 2,
+        flops=5 * cols_flops,
+        alias={11: 0},
+    )
+    with jax.named_scope("exchange"):
+        partial = lax.all_to_all(partial, ("x", "y"), 0, 0, tiled=True)
+    with jax.named_scope("in_reduce"):
+        in_parts = mp_parts(in_parts, 1)
+    in_share = mp_sum(in_parts)
+    blocks = call(
+        sum_kernel, [((PADDED, 2 * half), BF16)] * SIDE, (zh, partial), scalars=1, scratch=[sum_scratch]
+    )
     total = blocks[0].astype(F32)
     for step in range(1, SIDE):
         pairs = [(source, (source + step) % SIDE) for source in range(SIDE)]
-        total = total + lax.ppermute(blocks[step], "zh", pairs).astype(F32)
+        with jax.named_scope("zh_reduce"):
+            came = lax.ppermute(blocks[step], "zh", pairs)
+        total = total + came.astype(F32)
     weight_part = (total[:share] / (SIDE * SIDE * SIDE)).reshape(1, share, 2, half)
     return (jnp.where(is_decoder, enc_share, in_share)[None], weight_part)
 

time: 121 us -> 102 us (0.84)
  starting transfers between devices: 54.7 us -> 46.2 us
  local copies, waits for them, and re-layouts: 6.99 us -> 4.19 us
  Pallas kernels: 9.28 us -> 6.83 us
  other arithmetic: 4.34 us -> 1.94 us
  waiting for transfers between devices: 42.9 us -> 40.6 us
    ppermute x10, waiting for transfers between devices: 13.7 us -> 27.3 us  [mp_move(): return lax.ppermute(value, ('sec', 'mp'), pairs)]
    ppermute x6 -> x3, waiting for transfers between devices: 14 us -> 1.77 us  [shards(): came = lax.ppermute(blocks[step], 'zh', pairs)]
    all_to_all x2 -> x1, starting transfers between devices: 10.7 us -> 4.62 us  [shards(): partial = lax.all_to_all(partial, ('x', 'y'), 0, 0, tiled=True)]
    all_to_all x2 -> x1, waiting for transfers between devices: 15.2 us -> 11.5 us  [shards(): partial = lax.all_to_all(partial, ('x', 'y'), 0, 0, tiled=True)]
    ppermute x6 -> x3, starting transfers between devices: 27.1 us -> 23.7 us  [shards(): came = lax.ppermute(blocks[step], 'zh', pairs)]
    select_n x2 -> x0, other arithmetic: 3.34 us -> none  [the longest x1 2.29 us: shards(): jnp.where(is_decoder, first, second)]
    unnamed x29 -> x15, local copies, waits for them, and re-layouts: 6.17 us -> 3.37 us
    pallas_call x7 -> x4, Pallas kernels: 9.28 us -> 6.83 us  [call(): pl.pallas_call(kernel, out_shape=[jax.ShapeDtypeStruct(shape, kind) for s...]
  transfers between devices with their start and end apart: 18 -> 14, of which waited for: 9 -> 5; matrix products, arithmetic and copies ran while one was open for 1% -> 2% of each run, Pallas kernels for 3% -> 1%
where the time goes in v3:
time: 102 us; the launch traced here: 101 us
  starting transfers between devices  46.2 us (45%)
  waiting for transfers between devices  40.6 us (40%)
  Pallas kernels  6.83 us (7%)
  local copies, waits for them, and re-layouts  4.19 us (4%)
  other arithmetic  1.94 us (2%)
    ppermute x10, waiting for transfers between devices, mp_move(): return lax.ppermute(value, ('sec', 'mp'), pairs)  27.3 us
    ppermute x3, starting transfers between devices, shards(): came = lax.ppermute(blocks[step], 'zh', pairs)  23.7 us
    ppermute x10, starting transfers between devices, mp_move(): return lax.ppermute(value, ('sec', 'mp'), pairs)  17.9 us
    all_to_all x1, waiting for transfers between devices, shards(): partial = lax.all_to_all(partial, ('x', 'y'), 0, 0, tiled=True)  11.5 us
    pallas_call x4, Pallas kernels, call(): pl.pallas_call(kernel, out_shape=[jax.ShapeDtypeStruct(shape, kind) for s...  6.83 us
    all_to_all x1, starting transfers between devices, shards(): partial = lax.all_to_all(partial, ('x', 'y'), 0, 0, tiled=True)  4.62 us
    unnamed x15, local copies, waits for them, and re-layouts  3.37 us
  transfers between devices with their start and end apart: 14, of which 5 were waited for; matrix products, arithmetic and copies ran while one was open for 2% of the time, Pallas kernels for 1%

profile of v3, /device:TPU:1, one launch (start us, length us, event | category | flops | bytes accessed | tf_op | source)
XLA Modules:
  0.0 100.8 jit_solution(376569369319509727)
XLA Ops:
  0.7 0.1 reshape.140.order_ref
  0.8 0.0 copy-start.1
  0.8 0.0 copy-start.2
  0.8 0.0 copy-start.3
  0.8 0.0 copy-start.4
  0.8 0.0 copy-start.5
  0.9 0.0 copy-start.6
  0.9 2.1 %copy.10 = bf16[112,8,2,512]{3,1,2,0:T(8,128)(2,1)S(1)} copy(bf16[112,8,2,512]{3,2,1,0:T(2,128)(2,1)} %bitcast.13) | data formatting | bytes 3670016
  3.0 0.0 copy-done.1
  3.0 0.0 copy-done.2
  3.0 0.0 copy-done.3
  3.0 0.0 copy-done.4
  3.0 2.8 %shard_map.86 = (bf16[512,1024]{1,0:T(8,128)(2,1)S(1)}, bf16[128,896]{1,0:T(8,128)(2,1)S(1)}, bf16[128,896]{1,0:T(8,128)(2,1)S(1)}, bf16[128,896]{1,0:T(8,128)(2...) custom-call(s32[1]{0:T(128)} %bitcast.sec_ref, ...), custom_call_target="tpu_custom_call" | custom-call | flops 1879048192 | bytes 4194304 | tf_op jit(solution)/shard_map/pallas_call | solution.py:155
  5.9 0.7 collective-permute-start
  6.5 0.7 collective-permute-start.1
  7.2 0.7 collective-permute-start.2
  7.9 0.0 collective-permute-done
  7.9 0.0 collective-permute-done.1
  7.9 0.0 collective-permute-done.2
  7.9 0.1 add_convert_fusion.1
  8.1 1.3 %collective-permute-start.3 = (bf16[128,896]{1,0:T(8,128)(2,1)S(1)}, bf16[128,896]{1,0:T(8,128)(2,1)S(1)}, u32[]{:S(2)}, u32[]{:S(2)}) collective-permute-start(bf16[128,896]{1,0:T(8,128)(2,1)S(1)} %add_convert_fusion.1), channel_id=1, source_target_pairs={{0,256},{1,257},{2,258},{3,259},{4,260},{5,261},{6,262},{7,263},{8... | collective-permute-start | bytes 688136 | tf_op jit(solution)/shard_map/enc_gather/ppermute | solution.py:169
  9.4 1.3 %collective-permute-start.4 = (bf16[128,896]{1,0:T(8,128)(2,1)S(1)}, bf16[128,896]{1,0:T(8,128)(2,1)S(1)}, u32[]{:S(2)}, u32[]{:S(2)}) collective-permute-start(bf16[128,896]{1,0:T(8,128)(2,1)S(1)} %add_convert_fusion.1), channel_id=1, source_target_pairs={{0,257},{1,258},{2,259},{3,256},{4,261},{5,262},{6,263},{7,260},{8... | collective-permute-start | bytes 688136 | tf_op jit(solution)/shard_map/enc_gather/ppermute | solution.py:169
  10.7 1.3 %collective-permute-start.5 = (bf16[128,896]{1,0:T(8,128)(2,1)S(1)}, bf16[128,896]{1,0:T(8,128)(2,1)S(1)}, u32[]{:S(2)}, u32[]{:S(2)}) collective-permute-start(bf16[128,896]{1,0:T(8,128)(2,1)S(1)} %add_convert_fusion.1), channel_id=1, source_target_pairs={{0,258},{1,259},{2,256},{3,257},{4,262},{5,263},{6,260},{7,261},{8... | collective-permute-start | bytes 688136 | tf_op jit(solution)/shard_map/enc_gather/ppermute | solution.py:169
  12.0 1.3 %collective-permute-start.6 = (bf16[128,896]{1,0:T(8,128)(2,1)S(1)}, bf16[128,896]{1,0:T(8,128)(2,1)S(1)}, u32[]{:S(2)}, u32[]{:S(2)}) collective-permute-start(bf16[128,896]{1,0:T(8,128)(2,1)S(1)} %add_convert_fusion.1), channel_id=1, source_target_pairs={{0,259},{1,256},{2,257},{3,258},{4,263},{5,260},{6,261},{7,262},{8... | collective-permute-start | bytes 688136 | tf_op jit(solution)/shard_map/enc_gather/ppermute | solution.py:169
  13.3 16.8 %collective-permute-done.3.got0 = bf16[128,896]{1,0:T(8,128)(2,1)S(1)} collective-permute-done((bf16[128,896]{1,0:T(8,128)(2,1)S(1)}, bf16[128,896]{1,0:T(8,128)(2,1)S(1)}, u32[]{:S(2)}, u32[]{:S(2)}) %collective-permute-start.3) | collective-permute-done | bytes 229408 | tf_op jit(solution)/shard_map/enc_gather/ppermute | solution.py:169
  30.1 7.1 %collective-permute-done.4.got1 = bf16[128,896]{1,0:T(8,128)(2,1)S(1)} collective-permute-done((bf16[128,896]{1,0:T(8,128)(2,1)S(1)}, bf16[128,896]{1,0:T(8,128)(2,1)S(1)}, u32[]{:S(2)}, u32[]{:S(2)}) %collective-permute-start.4) | collective-permute-done | bytes 229408 | tf_op jit(solution)/shard_map/enc_gather/ppermute | solution.py:169
  37.2 3.4 %collective-permute-done.5.got2 = bf16[128,896]{1,0:T(8,128)(2,1)S(1)} collective-permute-done((bf16[128,896]{1,0:T(8,128)(2,1)S(1)}, bf16[128,896]{1,0:T(8,128)(2,1)S(1)}, u32[]{:S(2)}, u32[]{:S(2)}) %collective-permute-start.5) | collective-permute-done | bytes 229408 | tf_op jit(solution)/shard_map/enc_gather/ppermute | solution.py:169
  40.6 0.0 collective-permute-done.6.got3
  40.6 3.5 %shard_map.88 = (bf16[16,56,1024]{2,1,0:T(8,128)(2,1)S(1)}, bf16[128,896]{1,0:T(8,128)(2,1)S(1)}, bf16[128,896]{1,0:T(8,128)(2,1)S(1)}, bf16[128,896]{1,0:T(8,128)(2,1)S(1)}, bf16[128,896]{1,0:T(8,128)(2,1)S(1)}) custom-call(s32[1]{0:T(128)} %bitcast.sec_ref, s32[1]{0:T(128)} %bitcast.1.mp_ref, ...), custom_call_target="tpu_custom_call", output_to_operand_aliasing={{0}: (11, {})} | custom-call | flops 2348810240 | bytes 4194304 | tf_op jit(solution)/shard_map/pallas_call | solution.py:155
  44.1 0.0 copy-start
  44.1 1.3 %copy-done = bf16[16,56,1024]{2,1,0:T(8,128)(2,1)} copy-done((bf16[16,56,1024]{2,1,0:T(8,128)(2,1)}, bf16[16,56,1024]{2,1,0:T(8,128)(2,1)S(1)}, u32[]{:S(2)}) %copy-start) | copy-done | bytes 1835032
  45.3 4.6 %all-to-all-start = ((bf16[16,56,1024]{2,1,0:T(8,128)(2,1)}), bf16[16,56,1024]{2,1,0:T(8,128)(2,1)S(1)}, u32[]{:S(2)}, u32[]{:S(2)}) async-start(bf16[16,56,1024]{2,1,0:T(8,128)(2,1)} %copy-done), calls=%async_computation | async-start | bytes 3670016 | tf_op jit(solution)/shard_map/exchange/all_to_all | solution.py:235
  50.0 3.6 %collective-permute-start.7 = (bf16[128,896]{1,0:T(8,128)(2,1)S(1)}, bf16[128,896]{1,0:T(8,128)(2,1)S(1)}, u32[]{:S(2)}, u32[]{:S(2)}) collective-permute-start(bf16[128,896]{1,0:T(8,128)(2,1)S(1)} %get-tuple-element.28), channel_id=1, source_target_pairs={{256,258},{257,259},{258,256},{259,257},{260,262},{261,263},{262,2... | collective-permute-start | bytes 688136 | tf_op jit(solution)/shard_map/in_reduce/ppermute | solution.py:169
  53.6 3.6 %collective-permute-start.8 = (bf16[128,896]{1,0:T(8,128)(2,1)S(1)}, bf16[128,896]{1,0:T(8,128)(2,1)S(1)}, u32[]{:S(2)}, u32[]{:S(2)}) collective-permute-start(bf16[128,896]{1,0:T(8,128)(2,1)S(1)} %get-tuple-element.29), channel_id=1, source_target_pairs={{256,257},{257,258},{258,259},{259,256},{260,261},{261,262},{262,2... | collective-permute-start | bytes 688136 | tf_op jit(solution)/shard_map/in_reduce/ppermute | solution.py:169
  57.3 3.4 %collective-permute-start.9 = (bf16[128,896]{1,0:T(8,128)(2,1)S(1)}, bf16[128,896]{1,0:T(8,128)(2,1)}, u32[]{:S(2)}, u32[]{:S(2)}) collective-permute-start(bf16[128,896]{1,0:T(8,128)(2,1)S(1)} %get-tuple-element.30), channel_id=1, source_target_pairs={{256,259},{257,256},{258,257},{259,258},{260,263},{261,260},{262,2... | collective-permute-start | bytes 688136 | tf_op jit(solution)/shard_map/in_reduce/ppermute | solution.py:169
  60.7 11.5 %all-to-all-done.piece_ref = bf16[16,56,1024]{2,1,0:T(8,128)(2,1)S(1)} async-done(((bf16[16,56,1024]{2,1,0:T(8,128)(2,1)}), bf16[16,56,1024]{2,1,0:T(8,128)(2,1)S(1)}, u32[]{:S(2)}, u32[]{:S(2)}) %all-to-all-start) | async-done | bytes 1835040 | tf_op jit(solution)/shard_map/exchange/all_to_all | solution.py:235
  72.2 0.5 shard_map.89
  72.8 8.8 %collective-permute-start.10 = (bf16[16,1024]{1,0:T(8,128)(2,1)S(1)}, bf16[16,1024]{1,0:T(8,128)(2,1)S(1)}, u32[]{:S(2)}, u32[]{:S(2)}) collective-permute-start(bf16[16,1024]{1,0:T(8,128)(2,1)S(1)} %get-tuple-element.33), channel_id=1, source_target_pairs={{0,16},{16,32},{32,48},{48,0},{1,17},{17,33},{33,49},{49,1},{2,18}... | collective-permute-start | bytes 98312 | tf_op jit(solution)/shard_map/zh_reduce/ppermute | solution.py:246
  81.6 9.7 %collective-permute-start.11 = (bf16[16,1024]{1,0:T(8,128)(2,1)S(1)}, bf16[16,1024]{1,0:T(8,128)(2,1)S(1)}, u32[]{:S(2)}, u32[]{:S(2)}) collective-permute-start(bf16[16,1024]{1,0:T(8,128)(2,1)S(1)} %get-tuple-element.34), channel_id=1, source_target_pairs={{0,32},{16,48},{32,0},{48,16},{1,33},{17,49},{33,1},{49,17},{2,34}... | collective-permute-start | bytes 98312 | tf_op jit(solution)/shard_map/zh_reduce/ppermute | solution.py:246
  91.3 0.0 collective-permute-done.7
  91.3 5.2 %collective-permute-start.12 = (bf16[16,1024]{1,0:T(8,128)(2,1)S(1)}, bf16[16,1024]{1,0:T(8,128)(2,1)S(1)}, u32[]{:S(2)}, u32[]{:S(2)}) collective-permute-start(bf16[16,1024]{1,0:T(8,128)(2,1)S(1)} %get-tuple-element.35), channel_id=1, source_target_pairs={{0,48},{16,0},{32,16},{48,32},{1,49},{17,1},{33,17},{49,33},{2,50}... | collective-permute-start | bytes 98312 | tf_op jit(solution)/shard_map/zh_reduce/ppermute | solution.py:246
  96.5 0.0 collective-permute-done.8
  96.5 0.0 collective-permute-done.9
  96.5 1.8 %fusion.1 = bf16[1,128,896]{2,1,0:T(8,128)(2,1)} fusion(bf16[128,896]{1,0:T(8,128)(2,1)S(1)} %add_convert_fusion.1, bf16[128,896]{1,0:T(8,128)(2,1)} %collective-permute-done.9, bf16[128,896]{1,0:T(8,128)(2,1)S(1)} %collective-permute-done.8, bf16[128,896]{1,0:T(8,128)(2,1)S(1)} %collective-permute-done.7, bf16[128,896]{1,0:T(8,128)(2,1)S(1)} %get-tuple-element.27, ...), kind=kLoop, calls=%fused_computation.3 | loop fusion | flops 1032192 | bytes 1376257 | tf_op jit(solution)/shard_map/broadcast_in_dim | solution.py:249
  98.3 0.0 collective-permute-done.10
  98.3 0.0 collective-permute-done.11
  98.3 1.8 %collective-permute-done.12 = bf16[16,1024]{1,0:T(8,128)(2,1)S(1)} collective-permute-done((bf16[16,1024]{1,0:T(8,128)(2,1)S(1)}, bf16[16,1024]{1,0:T(8,128)(2,1)S(1)}, u32[]{:S(2)}, u32[]{:S(2)}) %collective-permute-start.12) | collective-permute-done | bytes 32800 | tf_op jit(solution)/shard_map/zh_reduce/ppermute | solution.py:246
  100.1 0.7 reshape.142
  (5 shorter events, 0.0 us)
Async XLA Ops:
  0.8 2.2 %copy-start.1 = (bf16[1,512,896]{2,1,0:T(8,128)(2,1)S(1)}, bf16[1,512,896]{2,1,0:T(8,128)(2,1)}, u32[]{:S(2)}) copy-start(bf16[1,512,896]{2,1,0:T(8,128)(2,1)} %param.7) | copy-start | bytes 2752516
  0.8 2.2 %copy-start.2 = (bf16[128,512]{1,0:T(8,128)(2,1)S(1)}, bf16[128,512]{1,0:T(8,128)(2,1)}, u32[]{:S(2)}) copy-start(bf16[128,512]{1,0:T(8,128)(2,1)} %query_ref.1) | copy-start | bytes 393220
  0.8 2.2 %copy-start.3 = (bf16[128,512]{1,0:T(8,128)(2,1)S(1)}, bf16[128,512]{1,0:T(8,128)(2,1)}, u32[]{:S(2)}) copy-start(bf16[128,512]{1,0:T(8,128)(2,1)} %grad_ref.1) | copy-start | bytes 393220
  0.8 2.2 %copy-start.4 = (f32[4,128]{1,0:T(4,128)S(1)}, f32[4,128]{1,0:T(4,128)}, u32[]{:S(2)}) copy-start(f32[4,128]{1,0:T(4,128)} %lse_ref.1) | copy-start | bytes 6148
  0.8 2.1 %copy-start.5 = (f32[4,128]{1,0:T(4,128)S(1)}, f32[4,128]{1,0:T(4,128)}, u32[]{:S(2)}) copy-start(f32[4,128]{1,0:T(4,128)} %delta_ref.1) | copy-start | bytes 6148
  0.9 2.1 %copy-start.6 = (s32[2,2]{1,0:T(2,128)S(1)}, s32[2,2]{1,0:T(2,128)}, u32[]{:S(2)}) copy-start(s32[2,2]{1,0:T(2,128)} %span_ref.1) | copy-start | bytes 52
  5.9 2.1 %collective-permute-start = (bf16[128,896]{1,0:T(8,128)(2,1)S(1)}, bf16[128,896]{1,0:T(8,128)(2,1)S(1)}, u32[]{:S(2)}, u32[]{:S(2)}) collective-permute-start(bf16[128,896]{1,0:T(8,128)(2,1)S(1)} %get-tuple-element.20), channel_id=1, source_target_pairs={{0,2},{1,3},{2,0},{3,1},{4,6},{5,7},{6,4},{7,5},{8,10},{9,11},{10,... | collective-permute-start | bytes 688136 | tf_op jit(solution)/shard_map/enc_reduce/ppermute | solution.py:169
  6.5 1.4 %collective-permute-start.1 = (bf16[128,896]{1,0:T(8,128)(2,1)S(1)}, bf16[128,896]{1,0:T(8,128)(2,1)S(1)}, u32[]{:S(2)}, u32[]{:S(2)}) collective-permute-start(bf16[128,896]{1,0:T(8,128)(2,1)S(1)} %get-tuple-element.21), channel_id=1, source_target_pairs={{0,1},{1,2},{2,3},{3,0},{4,5},{5,6},{6,7},{7,4},{8,9},{9,10},{10,1... | collective-permute-start | bytes 688136 | tf_op jit(solution)/shard_map/enc_reduce/ppermute | solution.py:169
  7.2 0.7 collective-permute-start.2
  8.1 22.0 %collective-permute-start.3 = (bf16[128,896]{1,0:T(8,128)(2,1)S(1)}, bf16[128,896]{1,0:T(8,128)(2,1)S(1)}, u32[]{:S(2)}, u32[]{:S(2)}) collective-permute-start(bf16[128,896]{1,0:T(8,128)(2,1)S(1)} %add_convert_fusion.1), channel_id=1, source_target_pairs={{0,256},{1,257},{2,258},{3,259},{4,260},{5,261},{6,262},{7,263},{8... | collective-permute-start | bytes 688136 | tf_op jit(solution)/shard_map/enc_gather/ppermute | solution.py:169
  9.4 27.9 %collective-permute-start.4 = (bf16[128,896]{1,0:T(8,128)(2,1)S(1)}, bf16[128,896]{1,0:T(8,128)(2,1)S(1)}, u32[]{:S(2)}, u32[]{:S(2)}) collective-permute-start(bf16[128,896]{1,0:T(8,128)(2,1)S(1)} %add_convert_fusion.1), channel_id=1, source_target_pairs={{0,257},{1,258},{2,259},{3,256},{4,261},{5,262},{6,263},{7,260},{8... | collective-permute-start | bytes 688136 | tf_op jit(solution)/shard_map/enc_gather/ppermute | solution.py:169
  10.7 29.9 %collective-permute-start.5 = (bf16[128,896]{1,0:T(8,128)(2,1)S(1)}, bf16[128,896]{1,0:T(8,128)(2,1)S(1)}, u32[]{:S(2)}, u32[]{:S(2)}) collective-permute-start(bf16[128,896]{1,0:T(8,128)(2,1)S(1)} %add_convert_fusion.1), channel_id=1, source_target_pairs={{0,258},{1,259},{2,256},{3,257},{4,262},{5,263},{6,260},{7,261},{8... | collective-permute-start | bytes 688136 | tf_op jit(solution)/shard_map/enc_gather/ppermute | solution.py:169
  12.0 28.6 %collective-permute-start.6 = (bf16[128,896]{1,0:T(8,128)(2,1)S(1)}, bf16[128,896]{1,0:T(8,128)(2,1)S(1)}, u32[]{:S(2)}, u32[]{:S(2)}) collective-permute-start(bf16[128,896]{1,0:T(8,128)(2,1)S(1)} %add_convert_fusion.1), channel_id=1, source_target_pairs={{0,259},{1,256},{2,257},{3,258},{4,263},{5,260},{6,261},{7,262},{8... | collective-permute-start | bytes 688136 | tf_op jit(solution)/shard_map/enc_gather/ppermute | solution.py:169
  44.1 1.3 %copy-start = (bf16[16,56,1024]{2,1,0:T(8,128)(2,1)}, bf16[16,56,1024]{2,1,0:T(8,128)(2,1)S(1)}, u32[]{:S(2)}) copy-start(bf16[16,56,1024]{2,1,0:T(8,128)(2,1)S(1)} %get-tuple-element.31) | copy-start | bytes 5505028
  45.3 26.9 %all-to-all-start = ((bf16[16,56,1024]{2,1,0:T(8,128)(2,1)}), bf16[16,56,1024]{2,1,0:T(8,128)(2,1)S(1)}, u32[]{:S(2)}, u32[]{:S(2)}) async-start(bf16[16,56,1024]{2,1,0:T(8,128)(2,1)} %copy-done), calls=%async_computation | async-start | bytes 3670016 | tf_op jit(solution)/shard_map/exchange/all_to_all | solution.py:235
  50.0 41.3 %collective-permute-start.7 = (bf16[128,896]{1,0:T(8,128)(2,1)S(1)}, bf16[128,896]{1,0:T(8,128)(2,1)S(1)}, u32[]{:S(2)}, u32[]{:S(2)}) collective-permute-start(bf16[128,896]{1,0:T(8,128)(2,1)S(1)} %get-tuple-element.28), channel_id=1, source_target_pairs={{256,258},{257,259},{258,256},{259,257},{260,262},{261,263},{262,2... | collective-permute-start | bytes 688136 | tf_op jit(solution)/shard_map/in_reduce/ppermute | solution.py:169
  53.6 42.9 %collective-permute-start.8 = (bf16[128,896]{1,0:T(8,128)(2,1)S(1)}, bf16[128,896]{1,0:T(8,128)(2,1)S(1)}, u32[]{:S(2)}, u32[]{:S(2)}) collective-permute-start(bf16[128,896]{1,0:T(8,128)(2,1)S(1)} %get-tuple-element.29), channel_id=1, source_target_pairs={{256,257},{257,258},{258,259},{259,256},{260,261},{261,262},{262,2... | collective-permute-start | bytes 688136 | tf_op jit(solution)/shard_map/in_reduce/ppermute | solution.py:169
  57.3 39.2 %collective-permute-start.9 = (bf16[128,896]{1,0:T(8,128)(2,1)S(1)}, bf16[128,896]{1,0:T(8,128)(2,1)}, u32[]{:S(2)}, u32[]{:S(2)}) collective-permute-start(bf16[128,896]{1,0:T(8,128)(2,1)S(1)} %get-tuple-element.30), channel_id=1, source_target_pairs={{256,259},{257,256},{258,257},{259,258},{260,263},{261,260},{262,2... | collective-permute-start | bytes 688136 | tf_op jit(solution)/shard_map/in_reduce/ppermute | solution.py:169
  72.8 25.5 %collective-permute-start.10 = (bf16[16,1024]{1,0:T(8,128)(2,1)S(1)}, bf16[16,1024]{1,0:T(8,128)(2,1)S(1)}, u32[]{:S(2)}, u32[]{:S(2)}) collective-permute-start(bf16[16,1024]{1,0:T(8,128)(2,1)S(1)} %get-tuple-element.33), channel_id=1, source_target_pairs={{0,16},{16,32},{32,48},{48,0},{1,17},{17,33},{33,49},{49,1},{2,18}... | collective-permute-start | bytes 98312 | tf_op jit(solution)/shard_map/zh_reduce/ppermute | solution.py:246
  81.6 16.7 %collective-permute-start.11 = (bf16[16,1024]{1,0:T(8,128)(2,1)S(1)}, bf16[16,1024]{1,0:T(8,128)(2,1)S(1)}, u32[]{:S(2)}, u32[]{:S(2)}) collective-permute-start(bf16[16,1024]{1,0:T(8,128)(2,1)S(1)} %get-tuple-element.34), channel_id=1, source_target_pairs={{0,32},{16,48},{32,0},{48,16},{1,33},{17,49},{33,1},{49,17},{2,34}... | collective-permute-start | bytes 98312 | tf_op jit(solution)/shard_map/zh_reduce/ppermute | solution.py:246
  91.3 8.8 %collective-permute-start.12 = (bf16[16,1024]{1,0:T(8,128)(2,1)S(1)}, bf16[16,1024]{1,0:T(8,128)(2,1)S(1)}, u32[]{:S(2)}, u32[]{:S(2)}) collective-permute-start(bf16[16,1024]{1,0:T(8,128)(2,1)S(1)} %get-tuple-element.35), channel_id=1, source_target_pairs={{0,48},{16,0},{32,16},{48,32},{1,49},{17,1},{33,17},{49,33},{2,50}... | collective-permute-start | bytes 98312 | tf_op jit(solution)/shard_map/zh_reduce/ppermute | solution.py:246

commit v4 on v3

--- a/solution.py
+++ b/solution.py
@@ -169,8 +169,9 @@
     return lax.ppermute(value, ("sec", "mp"), pairs)
 
 
-def mp_parts(parts, section):
-    return [parts[0]] + [mp_move(parts[step], section, section, step) for step in (2, 1, 3)]
+def mp_parts(parts, source, target):
+    moved = [mp_move(parts[step], source, target, step) for step in (2, 1, 3)]
+    return moved + [mp_move(parts[0], source, target, 0) if source != target else parts[0]]
 
 
 def mp_sum(parts):
@@ -213,11 +214,13 @@
         flops=4 * cols_flops,
     )
     with jax.named_scope("enc_reduce"):
-        enc_parts = mp_parts(enc_parts, 0)
+        enc_parts = mp_parts(enc_parts, 0, 1)
     enc_share = mp_sum(enc_parts)
     with jax.named_scope("enc_gather"):
-        got = [mp_move(enc_share, 0, 1, step) for step in (2, 1, 3, 0)]
-        got = [got[3], got[1], got[0], got[2]]
+        got = {step: mp_move(enc_share, 1, 1, step) for step in (2, 1, 3)}
+        got = [enc_share, got[1], got[2], got[3]]
+    with jax.named_scope("enc_out"):
+        enc_share = lax.ppermute(enc_share, "sec", [(1, 0)])
 
     (partial,) = call(
         decoder_weight_kernel, [piece_out], (sec, rows, kv_grad, order), scalars=1, flops=4 * cols_flops
@@ -234,7 +237,7 @@
     with jax.named_scope("exchange"):
         partial = lax.all_to_all(partial, ("x", "y"), 0, 0, tiled=True)
     with jax.named_scope("in_reduce"):
-        in_parts = mp_parts(in_parts, 1)
+        in_parts = mp_parts(in_parts, 1, 1)
     in_share = mp_sum(in_parts)
     blocks = call(
         sum_kernel, [((PADDED, 2 * half), BF16)] * SIDE, (zh, partial), scalars=1, scratch=[sum_scratch]

time: 102 us -> 95.8 us (0.939)
  waiting for transfers between devices: 40.6 us -> 27.8 us
  starting transfers between devices: 46.2 us -> 53.5 us
    ppermute x10, waiting for transfers between devices: 27.3 us -> 19.1 us  [mp_move(): return lax.ppermute(value, ('sec', 'mp'), pairs)]
    ppermute x10, starting transfers between devices: 17.9 us -> 23.7 us  [mp_move(): return lax.ppermute(value, ('sec', 'mp'), pairs)]
    all_to_all x1, waiting for transfers between devices: 11.5 us -> 6.74 us  [shards(): partial = lax.all_to_all(partial, ('x', 'y'), 0, 0, tiled=True)]
    ppermute x0 -> x1, starting transfers between devices: none -> 1.3 us  [shards(): enc_share = lax.ppermute(enc_share, 'sec', [(1, 0)])]
  transfers between devices with their start and end apart: 14 -> 15, of which waited for: 5 -> 6; matrix products, arithmetic and copies ran while one was open for 2% -> 2% of each run, Pallas kernels for 1% -> 1%
where the time goes in v4:
time: 95.8 us; the launch traced here: 95.3 us
  starting transfers between devices  53.5 us (56%)
  waiting for transfers between devices  27.8 us (29%)
  Pallas kernels  6.83 us (7%)
  local copies, waits for them, and re-layouts  4.18 us (4%)
  other arithmetic  2.04 us (2%)
  between operations  0.96 us (1%)
    ppermute x10, starting transfers between devices, mp_move(): return lax.ppermute(value, ('sec', 'mp'), pairs)  23.7 us
    ppermute x3, starting transfers between devices, shards(): came = lax.ppermute(blocks[step], 'zh', pairs)  23.4 us
    ppermute x10, waiting for transfers between devices, mp_move(): return lax.ppermute(value, ('sec', 'mp'), pairs)  19.1 us
    pallas_call x4, Pallas kernels, call(): pl.pallas_call(kernel, out_shape=[jax.ShapeDtypeStruct(shape, kind) for s...  6.83 us
    all_to_all x1, waiting for transfers between devices, shards(): partial = lax.all_to_all(partial, ('x', 'y'), 0, 0, tiled=True)  6.74 us
    all_to_all x1, starting transfers between devices, shards(): partial = lax.all_to_all(partial, ('x', 'y'), 0, 0, tiled=True)  5.03 us
    unnamed x15, local copies, waits for them, and re-layouts  3.37 us
  transfers between devices with their start and end apart: 15, of which 6 were waited for; matrix products, arithmetic and copies ran while one was open for 2% of the time, Pallas kernels for 1%

profile of v4, /device:TPU:1, one launch (start us, length us, event | category | flops | bytes accessed | tf_op | source)
XLA Modules:
  0.0 95.3 jit_solution(2853261596099531364)
XLA Ops:
  0.7 0.1 reshape.140.order_ref
  0.8 0.0 copy-start.1
  0.8 0.0 copy-start.2
  0.8 0.0 copy-start.3
  0.8 0.0 copy-start.4
  0.8 0.0 copy-start.5
  0.9 0.0 copy-start.6
  0.9 2.1 %copy.10 = bf16[112,8,2,512]{3,1,2,0:T(8,128)(2,1)S(1)} copy(bf16[112,8,2,512]{3,2,1,0:T(2,128)(2,1)} %bitcast.13) | data formatting | bytes 3670016
  3.0 0.0 copy-done.1
  3.0 0.0 copy-done.2
  3.0 0.0 copy-done.3
  3.0 2.8 %shard_map.86 = (bf16[512,1024]{1,0:T(8,128)(2,1)S(1)}, bf16[128,896]{1,0:T(8,128)(2,1)S(1)}, bf16[128,896]{1,0:T(8,128)(2,1)S(1)}, bf16[128,896]{1,0:T(8,128)(2...) custom-call(s32[1]{0:T(128)} %bitcast.sec_ref, ...), custom_call_target="tpu_custom_call" | custom-call | flops 1879048192 | bytes 4194304 | tf_op jit(solution)/shard_map/pallas_call | solution.py:155
  5.9 1.3 %collective-permute-start = (bf16[128,896]{1,0:T(8,128)(2,1)S(1)}, bf16[128,896]{1,0:T(8,128)(2,1)S(1)}, u32[]{:S(2)}, u32[]{:S(2)}) collective-permute-start(bf16[128,896]{1,0:T(8,128)(2,1)S(1)} %get-tuple-element.19), channel_id=1, source_target_pairs={{0,258},{1,259},{2,256},{3,257},{4,262},{5,263},{6,260},{7,261},{8... | collective-permute-start | bytes 688136 | tf_op jit(solution)/shard_map/enc_reduce/ppermute | solution.py:169
  7.2 1.3 %collective-permute-start.1 = (bf16[128,896]{1,0:T(8,128)(2,1)S(1)}, bf16[128,896]{1,0:T(8,128)(2,1)S(1)}, u32[]{:S(2)}, u32[]{:S(2)}) collective-permute-start(bf16[128,896]{1,0:T(8,128)(2,1)S(1)} %get-tuple-element.20), channel_id=1, source_target_pairs={{0,257},{1,258},{2,259},{3,256},{4,261},{5,262},{6,263},{7,260},{8... | collective-permute-start | bytes 688136 | tf_op jit(solution)/shard_map/enc_reduce/ppermute | solution.py:169
  8.5 1.3 %collective-permute-start.2 = (bf16[128,896]{1,0:T(8,128)(2,1)S(1)}, bf16[128,896]{1,0:T(8,128)(2,1)S(1)}, u32[]{:S(2)}, u32[]{:S(2)}) collective-permute-start(bf16[128,896]{1,0:T(8,128)(2,1)S(1)} %get-tuple-element.21), channel_id=1, source_target_pairs={{0,259},{1,256},{2,257},{3,258},{4,263},{5,260},{6,261},{7,262},{8... | collective-permute-start | bytes 688136 | tf_op jit(solution)/shard_map/enc_reduce/ppermute | solution.py:169
  9.8 1.3 %collective-permute-start.3 = (bf16[128,896]{1,0:T(8,128)(2,1)S(1)}, bf16[128,896]{1,0:T(8,128)(2,1)S(1)}, u32[]{:S(2)}, u32[]{:S(2)}) collective-permute-start(bf16[128,896]{1,0:T(8,128)(2,1)S(1)} %get-tuple-element.22), channel_id=1, source_target_pairs={{0,256},{1,257},{2,258},{3,259},{4,260},{5,261},{6,262},{7,263},{8... | collective-permute-start | bytes 688136 | tf_op jit(solution)/shard_map/enc_reduce/ppermute | solution.py:169
  11.1 10.1 %collective-permute-done = bf16[128,896]{1,0:T(8,128)(2,1)S(1)} collective-permute-done((bf16[128,896]{1,0:T(8,128)(2,1)S(1)}, bf16[128,896]{1,0:T(8,128)(2,1)S(1)}, u32[]{:S(2)}, u32[]{:S(2)}) %collective-permute-start) | collective-permute-done | bytes 229408 | tf_op jit(solution)/shard_map/enc_reduce/ppermute | solution.py:169
  21.1 0.0 collective-permute-done.1
  21.1 2.1 %collective-permute-done.2 = bf16[128,896]{1,0:T(8,128)(2,1)S(1)} collective-permute-done((bf16[128,896]{1,0:T(8,128)(2,1)S(1)}, bf16[128,896]{1,0:T(8,128)(2,1)S(1)}, u32[]{:S(2)}, u32[]{:S(2)}) %collective-permute-start.2) | collective-permute-done | bytes 229408 | tf_op jit(solution)/shard_map/enc_reduce/ppermute | solution.py:169
  23.3 0.0 collective-permute-done.3
  23.3 0.1 add_convert_fusion.1.got0
  23.4 2.4 %collective-permute-start.5 = (bf16[128,896]{1,0:T(8,128)(2,1)S(1)}, bf16[128,896]{1,0:T(8,128)(2,1)S(1)}, u32[]{:S(2)}, u32[]{:S(2)}) collective-permute-start(bf16[128,896]{1,0:T(8,128)(2,1)S(1)} %add_convert_fusion.1.got0), channel_id=1, source_target_pairs={{256,257},{257,258},{258,259},{259,256},{260,261},{261,262},{262,2... | collective-permute-start | bytes 688136 | tf_op jit(solution)/shard_map/enc_gather/ppermute | solution.py:169
  25.8 5.1 %collective-permute-start.6 = (bf16[128,896]{1,0:T(8,128)(2,1)S(1)}, bf16[128,896]{1,0:T(8,128)(2,1)S(1)}, u32[]{:S(2)}, u32[]{:S(2)}) collective-permute-start(bf16[128,896]{1,0:T(8,128)(2,1)S(1)} %add_convert_fusion.1.got0), channel_id=1, source_target_pairs={{256,258},{257,259},{258,256},{259,257},{260,262},{261,263},{262,2... | collective-permute-start | bytes 688136 | tf_op jit(solution)/shard_map/enc_gather/ppermute | solution.py:169
  30.9 1.9 %collective-permute-start.7 = (bf16[128,896]{1,0:T(8,128)(2,1)S(1)}, bf16[128,896]{1,0:T(8,128)(2,1)S(1)}, u32[]{:S(2)}, u32[]{:S(2)}) collective-permute-start(bf16[128,896]{1,0:T(8,128)(2,1)S(1)} %add_convert_fusion.1.got0), channel_id=1, source_target_pairs={{256,259},{257,256},{258,257},{259,258},{260,263},{261,260},{262,2... | collective-permute-start | bytes 688136 | tf_op jit(solution)/shard_map/enc_gather/ppermute | solution.py:169
  32.9 0.0 collective-permute-done.5.got1
  32.9 4.3 %collective-permute-done.6.got2 = bf16[128,896]{1,0:T(8,128)(2,1)S(1)} collective-permute-done((bf16[128,896]{1,0:T(8,128)(2,1)S(1)}, bf16[128,896]{1,0:T(8,128)(2,1)S(1)}, u32[]{:S(2)}, u32[]{:S(2)}) %collective-permute-start.6) | collective-permute-done | bytes 229408 | tf_op jit(solution)/shard_map/enc_gather/ppermute | solution.py:169
  37.2 2.6 %collective-permute-done.7.got3 = bf16[128,896]{1,0:T(8,128)(2,1)S(1)} collective-permute-done((bf16[128,896]{1,0:T(8,128)(2,1)S(1)}, bf16[128,896]{1,0:T(8,128)(2,1)S(1)}, u32[]{:S(2)}, u32[]{:S(2)}) %collective-permute-start.7) | collective-permute-done | bytes 229408 | tf_op jit(solution)/shard_map/enc_gather/ppermute | solution.py:169
  39.8 3.5 %shard_map.88 = (bf16[16,56,1024]{2,1,0:T(8,128)(2,1)S(1)}, bf16[128,896]{1,0:T(8,128)(2,1)S(1)}, bf16[128,896]{1,0:T(8,128)(2,1)S(1)}, bf16[128,896]{1,0:T(8,128)(2,1)S(1)}, bf16[128,896]{1,0:T(8,128)(2,1)S(1)}) custom-call(s32[1]{0:T(128)} %bitcast.sec_ref, s32[1]{0:T(128)} %bitcast.1.mp_ref, ...), custom_call_target="tpu_custom_call", output_to_operand_aliasing={{0}: (11, {})} | custom-call | flops 2348810240 | bytes 4194304 | tf_op jit(solution)/shard_map/pallas_call | solution.py:155
  43.3 1.3 %copy-done = bf16[16,56,1024]{2,1,0:T(8,128)(2,1)} copy-done((bf16[16,56,1024]{2,1,0:T(8,128)(2,1)}, bf16[16,56,1024]{2,1,0:T(8,128)(2,1)S(1)}, u32[]{:S(2)}) %copy-start) | copy-done | bytes 1835032
  44.5 5.0 %all-to-all-start = ((bf16[16,56,1024]{2,1,0:T(8,128)(2,1)}), bf16[16,56,1024]{2,1,0:T(8,128)(2,1)S(1)}, u32[]{:S(2)}, u32[]{:S(2)}) async-start(bf16[16,56,1024]{2,1,0:T(8,128)(2,1)} %copy-done), calls=%async_computation | async-start | bytes 3670016 | tf_op jit(solution)/shard_map/exchange/all_to_all | solution.py:238
  49.6 1.3 %collective-permute-start.4 = (bf16[128,896]{1,0:T(8,128)(2,1)S(1)}, bf16[128,896]{1,0:T(8,128)(2,1)S(1)}, u32[]{:S(2)}, u32[]{:S(2)}) collective-permute-start(bf16[128,896]{1,0:T(8,128)(2,1)S(1)} %add_convert_fusion.1.got0), channel_id=1, source_target_pairs={{256,0},{257,1},{258,2},{259,3},{260,4},{261,5},{262,6},{263,7},{2... | collective-permute-start | bytes 688136 | tf_op jit(solution)/shard_map/enc_out/ppermute | solution.py:223
  50.9 5.0 %collective-permute-start.10 = (bf16[128,896]{1,0:T(8,128)(2,1)S(1)}, bf16[128,896]{1,0:T(8,128)(2,1)S(1)}, u32[]{:S(2)}, u32[]{:S(2)}) collective-permute-start(bf16[128,896]{1,0:T(8,128)(2,1)S(1)} %get-tuple-element.29), channel_id=1, source_target_pairs={{256,259},{257,256},{258,257},{259,258},{260,263},{261,260},{262,2... | collective-permute-start | bytes 688136 | tf_op jit(solution)/shard_map/in_reduce/ppermute | solution.py:169
  55.9 1.9 %collective-permute-start.8 = (bf16[128,896]{1,0:T(8,128)(2,1)S(1)}, bf16[128,896]{1,0:T(8,128)(2,1)}, u32[]{:S(2)}, u32[]{:S(2)}) collective-permute-start(bf16[128,896]{1,0:T(8,128)(2,1)S(1)} %get-tuple-element.27), channel_id=1, source_target_pairs={{256,258},{257,259},{258,256},{259,257},{260,262},{261,263},{262,2... | collective-permute-start | bytes 688136 | tf_op jit(solution)/shard_map/in_reduce/ppermute | solution.py:169
  57.8 2.2 %collective-permute-start.9 = (bf16[128,896]{1,0:T(8,128)(2,1)S(1)}, bf16[128,896]{1,0:T(8,128)(2,1)}, u32[]{:S(2)}, u32[]{:S(2)}) collective-permute-start(bf16[128,896]{1,0:T(8,128)(2,1)S(1)} %get-tuple-element.28), channel_id=1, source_target_pairs={{256,257},{257,258},{258,259},{259,256},{260,261},{261,262},{262,2... | collective-permute-start | bytes 688136 | tf_op jit(solution)/shard_map/in_reduce/ppermute | solution.py:169
  60.0 6.7 %all-to-all-done.piece_ref = bf16[16,56,1024]{2,1,0:T(8,128)(2,1)S(1)} async-done(((bf16[16,56,1024]{2,1,0:T(8,128)(2,1)}), bf16[16,56,1024]{2,1,0:T(8,128)(2,1)S(1)}, u32[]{:S(2)}, u32[]{:S(2)}) %all-to-all-start) | async-done | bytes 1835040 | tf_op jit(solution)/shard_map/exchange/all_to_all | solution.py:238
  66.8 0.5 shard_map.89
  67.3 8.9 %collective-permute-start.11 = (bf16[16,1024]{1,0:T(8,128)(2,1)S(1)}, bf16[16,1024]{1,0:T(8,128)(2,1)S(1)}, u32[]{:S(2)}, u32[]{:S(2)}) collective-permute-start(bf16[16,1024]{1,0:T(8,128)(2,1)S(1)} %get-tuple-element.33), channel_id=1, source_target_pairs={{0,16},{16,32},{32,48},{48,0},{1,17},{17,33},{33,49},{49,1},{2,18}... | collective-permute-start | bytes 98312 | tf_op jit(solution)/shard_map/zh_reduce/ppermute | solution.py:249
  76.2 0.0 collective-permute-done.4
  76.2 9.4 %collective-permute-start.12 = (bf16[16,1024]{1,0:T(8,128)(2,1)S(1)}, bf16[16,1024]{1,0:T(8,128)(2,1)S(1)}, u32[]{:S(2)}, u32[]{:S(2)}) collective-permute-start(bf16[16,1024]{1,0:T(8,128)(2,1)S(1)} %get-tuple-element.34), channel_id=1, source_target_pairs={{0,32},{16,48},{32,0},{48,16},{1,33},{17,49},{33,1},{49,17},{2,34}... | collective-permute-start | bytes 98312 | tf_op jit(solution)/shard_map/zh_reduce/ppermute | solution.py:249
  85.6 0.0 collective-permute-done.10
  85.6 5.2 %collective-permute-start.13 = (bf16[16,1024]{1,0:T(8,128)(2,1)S(1)}, bf16[16,1024]{1,0:T(8,128)(2,1)S(1)}, u32[]{:S(2)}, u32[]{:S(2)}) collective-permute-start(bf16[16,1024]{1,0:T(8,128)(2,1)S(1)} %get-tuple-element.35), channel_id=1, source_target_pairs={{0,48},{16,0},{32,16},{48,32},{1,49},{17,1},{33,17},{49,33},{2,50}... | collective-permute-start | bytes 98312 | tf_op jit(solution)/shard_map/zh_reduce/ppermute | solution.py:249
  90.8 0.0 collective-permute-done.8
  90.8 0.0 collective-permute-done.9
  90.8 1.9 %fusion.1 = bf16[1,128,896]{2,1,0:T(8,128)(2,1)} fusion(bf16[128,896]{1,0:T(8,128)(2,1)S(1)} %collective-permute-done.4, bf16[128,896]{1,0:T(8,128)(2,1)S(1)} %get-tuple-element.30, bf16[128,896]{1,0:T(8,128)(2,1)S(1)} %collective-permute-done.10, bf16[128,896]{1,0:T(8,128)(2,1)} %collective-permute-done.9, bf16[128,896]{1,0:T(8,128)(2,1)} %collective-permute-done.8, ...), kind=kLoop, calls=%fused_computation.3 | loop fusion | flops 1032192 | bytes 1376257 | tf_op jit(solution)/shard_map/broadcast_in_dim | solution.py:252
  92.7 0.0 collective-permute-done.11
  92.7 0.0 collective-permute-done.12
  92.7 1.9 %collective-permute-done.13 = bf16[16,1024]{1,0:T(8,128)(2,1)S(1)} collective-permute-done((bf16[16,1024]{1,0:T(8,128)(2,1)S(1)}, bf16[16,1024]{1,0:T(8,128)(2,1)S(1)}, u32[]{:S(2)}, u32[]{:S(2)}) %collective-permute-start.13) | collective-permute-done | bytes 32800 | tf_op jit(solution)/shard_map/zh_reduce/ppermute | solution.py:249
  94.6 0.7 reshape.142
  (7 shorter events, 0.0 us)
Async XLA Ops:
  0.8 2.2 %copy-start.1 = (bf16[1,512,896]{2,1,0:T(8,128)(2,1)S(1)}, bf16[1,512,896]{2,1,0:T(8,128)(2,1)}, u32[]{:S(2)}) copy-start(bf16[1,512,896]{2,1,0:T(8,128)(2,1)} %param.7) | copy-start | bytes 2752516
  0.8 2.2 %copy-start.2 = (bf16[128,512]{1,0:T(8,128)(2,1)S(1)}, bf16[128,512]{1,0:T(8,128)(2,1)}, u32[]{:S(2)}) copy-start(bf16[128,512]{1,0:T(8,128)(2,1)} %query_ref.1) | copy-start | bytes 393220
  0.8 2.2 %copy-start.3 = (bf16[128,512]{1,0:T(8,128)(2,1)S(1)}, bf16[128,512]{1,0:T(8,128)(2,1)}, u32[]{:S(2)}) copy-start(bf16[128,512]{1,0:T(8,128)(2,1)} %grad_ref.1) | copy-start | bytes 393220
  0.8 2.2 %copy-start.4 = (f32[4,128]{1,0:T(4,128)S(1)}, f32[4,128]{1,0:T(4,128)}, u32[]{:S(2)}) copy-start(f32[4,128]{1,0:T(4,128)} %lse_ref.1) | copy-start | bytes 6148
  0.8 2.1 %copy-start.5 = (f32[4,128]{1,0:T(4,128)S(1)}, f32[4,128]{1,0:T(4,128)}, u32[]{:S(2)}) copy-start(f32[4,128]{1,0:T(4,128)} %delta_ref.1) | copy-start | bytes 6148
  0.9 2.1 %copy-start.6 = (s32[2,2]{1,0:T(2,128)S(1)}, s32[2,2]{1,0:T(2,128)}, u32[]{:S(2)}) copy-start(s32[2,2]{1,0:T(2,128)} %span_ref.1) | copy-start | bytes 52
  5.9 15.3 %collective-permute-start = (bf16[128,896]{1,0:T(8,128)(2,1)S(1)}, bf16[128,896]{1,0:T(8,128)(2,1)S(1)}, u32[]{:S(2)}, u32[]{:S(2)}) collective-permute-start(bf16[128,896]{1,0:T(8,128)(2,1)S(1)} %get-tuple-element.19), channel_id=1, source_target_pairs={{0,258},{1,259},{2,256},{3,257},{4,262},{5,263},{6,260},{7,261},{8... | collective-permute-start | bytes 688136 | tf_op jit(solution)/shard_map/enc_reduce/ppermute | solution.py:169
  7.2 14.0 %collective-permute-start.1 = (bf16[128,896]{1,0:T(8,128)(2,1)S(1)}, bf16[128,896]{1,0:T(8,128)(2,1)S(1)}, u32[]{:S(2)}, u32[]{:S(2)}) collective-permute-start(bf16[128,896]{1,0:T(8,128)(2,1)S(1)} %get-tuple-element.20), channel_id=1, source_target_pairs={{0,257},{1,258},{2,259},{3,256},{4,261},{5,262},{6,263},{7,260},{8... | collective-permute-start | bytes 688136 | tf_op jit(solution)/shard_map/enc_reduce/ppermute | solution.py:169
  8.5 14.8 %collective-permute-start.2 = (bf16[128,896]{1,0:T(8,128)(2,1)S(1)}, bf16[128,896]{1,0:T(8,128)(2,1)S(1)}, u32[]{:S(2)}, u32[]{:S(2)}) collective-permute-start(bf16[128,896]{1,0:T(8,128)(2,1)S(1)} %get-tuple-element.21), channel_id=1, source_target_pairs={{0,259},{1,256},{2,257},{3,258},{4,263},{5,260},{6,261},{7,262},{8... | collective-permute-start | bytes 688136 | tf_op jit(solution)/shard_map/enc_reduce/ppermute | solution.py:169
  9.8 13.5 %collective-permute-start.3 = (bf16[128,896]{1,0:T(8,128)(2,1)S(1)}, bf16[128,896]{1,0:T(8,128)(2,1)S(1)}, u32[]{:S(2)}, u32[]{:S(2)}) collective-permute-start(bf16[128,896]{1,0:T(8,128)(2,1)S(1)} %get-tuple-element.22), channel_id=1, source_target_pairs={{0,256},{1,257},{2,258},{3,259},{4,260},{5,261},{6,262},{7,263},{8... | collective-permute-start | bytes 688136 | tf_op jit(solution)/shard_map/enc_reduce/ppermute | solution.py:169
  23.4 9.5 %collective-permute-start.5 = (bf16[128,896]{1,0:T(8,128)(2,1)S(1)}, bf16[128,896]{1,0:T(8,128)(2,1)S(1)}, u32[]{:S(2)}, u32[]{:S(2)}) collective-permute-start(bf16[128,896]{1,0:T(8,128)(2,1)S(1)} %add_convert_fusion.1.got0), channel_id=1, source_target_pairs={{256,257},{257,258},{258,259},{259,256},{260,261},{261,262},{262,2... | collective-permute-start | bytes 688136 | tf_op jit(solution)/shard_map/enc_gather/ppermute | solution.py:169
  25.8 11.3 %collective-permute-start.6 = (bf16[128,896]{1,0:T(8,128)(2,1)S(1)}, bf16[128,896]{1,0:T(8,128)(2,1)S(1)}, u32[]{:S(2)}, u32[]{:S(2)}) collective-permute-start(bf16[128,896]{1,0:T(8,128)(2,1)S(1)} %add_convert_fusion.1.got0), channel_id=1, source_target_pairs={{256,258},{257,259},{258,256},{259,257},{260,262},{261,263},{262,2... | collective-permute-start | bytes 688136 | tf_op jit(solution)/shard_map/enc_gather/ppermute | solution.py:169
  30.9 8.9 %collective-permute-start.7 = (bf16[128,896]{1,0:T(8,128)(2,1)S(1)}, bf16[128,896]{1,0:T(8,128)(2,1)S(1)}, u32[]{:S(2)}, u32[]{:S(2)}) collective-permute-start(bf16[128,896]{1,0:T(8,128)(2,1)S(1)} %add_convert_fusion.1.got0), channel_id=1, source_target_pairs={{256,259},{257,256},{258,257},{259,258},{260,263},{261,260},{262,2... | collective-permute-start | bytes 688136 | tf_op jit(solution)/shard_map/enc_gather/ppermute | solution.py:169
  43.3 1.3 %copy-start = (bf16[16,56,1024]{2,1,0:T(8,128)(2,1)}, bf16[16,56,1024]{2,1,0:T(8,128)(2,1)S(1)}, u32[]{:S(2)}) copy-start(bf16[16,56,1024]{2,1,0:T(8,128)(2,1)S(1)} %get-tuple-element.31) | copy-start | bytes 5505028
  44.5 22.2 %all-to-all-start = ((bf16[16,56,1024]{2,1,0:T(8,128)(2,1)}), bf16[16,56,1024]{2,1,0:T(8,128)(2,1)S(1)}, u32[]{:S(2)}, u32[]{:S(2)}) async-start(bf16[16,56,1024]{2,1,0:T(8,128)(2,1)} %copy-done), calls=%async_computation | async-start | bytes 3670016 | tf_op jit(solution)/shard_map/exchange/all_to_all | solution.py:238
  49.6 26.6 %collective-permute-start.4 = (bf16[128,896]{1,0:T(8,128)(2,1)S(1)}, bf16[128,896]{1,0:T(8,128)(2,1)S(1)}, u32[]{:S(2)}, u32[]{:S(2)}) collective-permute-start(bf16[128,896]{1,0:T(8,128)(2,1)S(1)} %add_convert_fusion.1.got0), channel_id=1, source_target_pairs={{256,0},{257,1},{258,2},{259,3},{260,4},{261,5},{262,6},{263,7},{2... | collective-permute-start | bytes 688136 | tf_op jit(solution)/shard_map/enc_out/ppermute | solution.py:223
  50.9 34.7 %collective-permute-start.10 = (bf16[128,896]{1,0:T(8,128)(2,1)S(1)}, bf16[128,896]{1,0:T(8,128)(2,1)S(1)}, u32[]{:S(2)}, u32[]{:S(2)}) collective-permute-start(bf16[128,896]{1,0:T(8,128)(2,1)S(1)} %get-tuple-element.29), channel_id=1, source_target_pairs={{256,259},{257,256},{258,257},{259,258},{260,263},{261,260},{262,2... | collective-permute-start | bytes 688136 | tf_op jit(solution)/shard_map/in_reduce/ppermute | solution.py:169
  55.9 34.9 %collective-permute-start.8 = (bf16[128,896]{1,0:T(8,128)(2,1)S(1)}, bf16[128,896]{1,0:T(8,128)(2,1)}, u32[]{:S(2)}, u32[]{:S(2)}) collective-permute-start(bf16[128,896]{1,0:T(8,128)(2,1)S(1)} %get-tuple-element.27), channel_id=1, source_target_pairs={{256,258},{257,259},{258,256},{259,257},{260,262},{261,263},{262,2... | collective-permute-start | bytes 688136 | tf_op jit(solution)/shard_map/in_reduce/ppermute | solution.py:169
  57.8 32.9 %collective-permute-start.9 = (bf16[128,896]{1,0:T(8,128)(2,1)S(1)}, bf16[128,896]{1,0:T(8,128)(2,1)}, u32[]{:S(2)}, u32[]{:S(2)}) collective-permute-start(bf16[128,896]{1,0:T(8,128)(2,1)S(1)} %get-tuple-element.28), channel_id=1, source_target_pairs={{256,257},{257,258},{258,259},{259,256},{260,261},{261,262},{262,2... | collective-permute-start | bytes 688136 | tf_op jit(solution)/shard_map/in_reduce/ppermute | solution.py:169
  67.3 25.4 %collective-permute-start.11 = (bf16[16,1024]{1,0:T(8,128)(2,1)S(1)}, bf16[16,1024]{1,0:T(8,128)(2,1)S(1)}, u32[]{:S(2)}, u32[]{:S(2)}) collective-permute-start(bf16[16,1024]{1,0:T(8,128)(2,1)S(1)} %get-tuple-element.33), channel_id=1, source_target_pairs={{0,16},{16,32},{32,48},{48,0},{1,17},{17,33},{33,49},{49,1},{2,18}... | collective-permute-start | bytes 98312 | tf_op jit(solution)/shard_map/zh_reduce/ppermute | solution.py:249
  76.2 16.5 %collective-permute-start.12 = (bf16[16,1024]{1,0:T(8,128)(2,1)S(1)}, bf16[16,1024]{1,0:T(8,128)(2,1)S(1)}, u32[]{:S(2)}, u32[]{:S(2)}) collective-permute-start(bf16[16,1024]{1,0:T(8,128)(2,1)S(1)} %get-tuple-element.34), channel_id=1, source_target_pairs={{0,32},{16,48},{32,0},{48,16},{1,33},{17,49},{33,1},{49,17},{2,34}... | collective-permute-start | bytes 98312 | tf_op jit(solution)/shard_map/zh_reduce/ppermute | solution.py:249
  85.6 9.0 %collective-permute-start.13 = (bf16[16,1024]{1,0:T(8,128)(2,1)S(1)}, bf16[16,1024]{1,0:T(8,128)(2,1)S(1)}, u32[]{:S(2)}, u32[]{:S(2)}) collective-permute-start(bf16[16,1024]{1,0:T(8,128)(2,1)S(1)} %get-tuple-element.35), channel_id=1, source_target_pairs={{0,48},{16,0},{32,16},{48,32},{1,49},{17,1},{33,17},{49,33},{2,50}... | collective-permute-start | bytes 98312 | tf_op jit(solution)/shard_map/zh_reduce/ppermute | solution.py:249

commit v5 on v4

--- a/solution.py
+++ b/solution.py
@@ -33,8 +33,31 @@
     return pl.when(sec_ref[0] == section)
 
 
-def decoder_kernel(mp_ref, span_ref, rows_ref, weight_ref, query_ref, grad_ref, lse_ref, delta_ref,
-                   kv_grad_ref, part0, part1, part2, part3, kv_ref, part_ref):
+def first_kernel(sec_ref, mp_ref, span_ref, rows_ref, weight_ref, query_ref, grad_ref, lse_ref, delta_ref,
+                 order_ref, kv_grad_ref, part0, part1, part2, part3, hidden_ref, slope_ref, ordered_ref, kv_ref, part_ref):
+    @on_section(sec_ref, 0)
+    def decoder():
+        decoder_work(
+            mp_ref, span_ref, rows_ref, weight_ref, query_ref, grad_ref, lse_ref, delta_ref,
+            kv_grad_ref, part0, part1, part2, part3, kv_ref, part_ref,
+        )
+
+    @on_section(sec_ref, 1)
+    def encoder():
+        half = weight_ref.shape[1] // 2
+        pre = mm(rows_ref[...], weight_ref[:, :half])
+        square = pre * pre
+        tangent = jnp.tanh(0.7978845608 * (pre + 0.044715 * square * pre))
+        hidden_ref[...] = (0.5 * pre * (1.0 + tangent)).astype(BF16)
+        slope_ref[...] = 0.5 * (1.0 + tangent) + 0.5 * pre * (1.0 - tangent * tangent) * 0.7978845608 * (
+            1.0 + 0.134145 * square
+        )
+        place = places(order_ref)
+        ordered_ref[...] = mm(rows_ref[...], place).astype(BF16)
+
+
+def decoder_work(mp_ref, span_ref, rows_ref, weight_ref, query_ref, grad_ref, lse_ref, delta_ref,
+                 kv_grad_ref, part0, part1, part2, part3, kv_ref, part_ref):
     half = weight_ref.shape[1] // 2
     kv_ref[...] = mm(rows_ref[...], weight_ref[...]).astype(BF16)
     lane = lax.broadcasted_iota(jnp.int32, (1, 2 * SPAN), 1)
@@ -66,10 +89,10 @@
         part[...] = part_ref[block_rows(lax.rem(mp_ref[0] + step, N_MP)), :]
 
 
-def ordered(rows, order_ref):
+def places(order_ref):
     width = order_ref.shape[1]
     place = lax.broadcasted_iota(jnp.int32, (width, width), 0) == order_ref[...]
-    return mm(rows, jnp.where(place, 1.0, 0.0).astype(BF16)).astype(BF16)
+    return jnp.where(place, 1.0, 0.0).astype(BF16)
 
 
 def store_chunks(out_ref, value, column=0):
@@ -78,51 +101,42 @@
         out_ref[index, :, column:column + width] = value[index * chunk:(index + 1) * chunk, :].astype(BF16)
 
 
-def decoder_weight_kernel(sec_ref, rows_ref, kv_grad_ref, order_ref, partial_ref):
-    @on_section(sec_ref, 0)
-    def work():
-        store_chunks(partial_ref, mm(ordered(rows_ref[...], order_ref), kv_grad_ref[...], TN))
-
-
-def prepare_kernel(rows_ref, weight_ref, order_ref, ordered_ref, hidden_ref, slope_ref):
-    half = weight_ref.shape[1] // 2
-    ordered_ref[...] = ordered(rows_ref[...], order_ref)
-    pre = mm(rows_ref[...], weight_ref[:, :half])
-    square = pre * pre
-    tangent = jnp.tanh(0.7978845608 * (pre + 0.044715 * square * pre))
-    hidden_ref[...] = (0.5 * pre * (1.0 + tangent)).astype(BF16)
-    slope_ref[...] = 0.5 * (1.0 + tangent) + 0.5 * pre * (1.0 - tangent * tangent) * 0.7978845608 * (
-        1.0 + 0.134145 * square
-    )
-
-
-def first_kernel(sec_ref, mp_ref, span_ref, rows_ref, weight_ref, query_ref, grad_ref, lse_ref, delta_ref, order_ref,
-                 kv_grad_ref, part0, part1, part2, part3, ordered_ref, hidden_ref, slope_ref, kv_ref, part_ref):
+def middle_kernel(sec_ref, rows_ref, weight_ref, kv_grad_ref, order_ref, partial_ref, down_ref):
     @on_section(sec_ref, 0)
     def decoder():
-        decoder_kernel(
-            mp_ref, span_ref, rows_ref, weight_ref, query_ref, grad_ref, lse_ref, delta_ref,
-            kv_grad_ref, part0, part1, part2, part3, kv_ref, part_ref,
-        )
+        rows = mm(rows_ref[...], places(order_ref)).astype(BF16)
+        store_chunks(partial_ref, mm(rows, kv_grad_ref[...], TN))
 
     @on_section(sec_ref, 1)
     def encoder():
-        prepare_kernel(rows_ref, weight_ref, order_ref, ordered_ref, hidden_ref, slope_ref)
-
-
-def encoder_kernel(sec_ref, mp_ref, order_ref, ordered_ref, weight_ref, hidden_ref, slope_ref, got0, got1, got2, got3,
-                   keep_ref, partial_ref, part0, part1, part2, part3, arrived_ref, part_ref):
+        half = weight_ref.shape[1] // 2
+        down_ref[...] = mm(places(order_ref), weight_ref[:, half:], TN).astype(BF16)
+
+
+def share_kernel(sec_ref, order_ref, got0, got1, got2, got3, share_ref, ordered_ref):
+    @on_section(sec_ref, 1)
+    def work():
+        total = got0[...].astype(F32)
+        for got in (got1, got2, got3):
+            total = total + got[...].astype(F32)
+        share = total.astype(BF16)
+        share_ref[...] = share
+        ordered_ref[...] = mm(share, places(order_ref)).astype(BF16)
+
+
+def encoder_kernel(sec_ref, mp_ref, ordered_ref, weight_ref, down_ref, hidden_ref, slope_ref, got0, got1, got2, got3, keep_ref,
+                   partial_ref, part0, part1, part2, part3, pre_grad_ref, arrived_ref, part_ref):
     del keep_ref
     @on_section(sec_ref, 1)
     def work():
-        half = weight_ref.shape[1] // 2
+        half = hidden_ref.shape[1]
         for step, got in enumerate((got0, got3, got2, got1)):
             arrived_ref[block_rows(lax.rem(mp_ref[0] + step, N_MP)), :] = got[...]
         arrived = arrived_ref[...]
-        pre_grad = (mm(arrived, weight_ref[:, half:]) * slope_ref[...]).astype(BF16)
-        store_chunks(partial_ref, mm(ordered(arrived, order_ref), hidden_ref[...], TN), half)
-        store_chunks(partial_ref, mm(ordered_ref[...], pre_grad, TN))
-        part_ref[...] = mm(pre_grad, weight_ref[:, :half], NT).astype(BF16)
+        store_chunks(partial_ref, mm(arrived, hidden_ref[...], TN), half)
+        pre_grad_ref[...] = (mm(arrived, down_ref[...]) * slope_ref[...]).astype(BF16)
+        store_chunks(partial_ref, mm(ordered_ref[...], pre_grad_ref[...], TN))
+        part_ref[...] = mm(pre_grad_ref[...], weight_ref[:, :half], NT).astype(BF16)
         for step, part in enumerate((part0, part1, part2, part3)):
             part[...] = part_ref[block_rows(lax.rem(mp_ref[0] + step, N_MP)), :]
 
@@ -205,40 +219,49 @@
     cols_flops = 2 * local_rows * width * half
 
     ordered_out = ((local_rows, width), BF16)
-    kv_grad, *enc_parts, ordered_rows, hidden, slope = call(
+    kv_grad, *enc_parts, hidden, slope, ordered_rows = call(
         first_kernel,
-        [((local_rows, 2 * half), BF16)] + part_outs + [ordered_out, col_out, ((local_rows, half), F32)],
+        [((local_rows, 2 * half), BF16)] + part_outs + [col_out, ((local_rows, half), F32), ordered_out],
         (sec, mp, span_blocks, rows, weights, queries, out_grad, logsumexp, delta, order),
         scalars=3,
         scratch=[pltpu.VMEM((local_rows, 2 * half), BF16), part_scratch],
         flops=4 * cols_flops,
     )
+    partial, down = call(
+        middle_kernel,
+        [piece_out, ((width, half), BF16)],
+        (sec, rows, weights, kv_grad, order),
+        scalars=1,
+        flops=6 * cols_flops,
+    )
     with jax.named_scope("enc_reduce"):
         enc_parts = mp_parts(enc_parts, 0, 1)
-    enc_share = mp_sum(enc_parts)
+    enc_share, ordered_share = call(
+        share_kernel,
+        [((quarter, width), BF16)] * 2,
+        (sec, order, *enc_parts),
+        scalars=1,
+        flops=2 * quarter * width * width,
+    )
     with jax.named_scope("enc_gather"):
-        got = {step: mp_move(enc_share, 1, 1, step) for step in (2, 1, 3)}
-        got = [enc_share, got[1], got[2], got[3]]
+        got = {step: mp_move(ordered_share, 1, 1, step) for step in (2, 1, 3)}
+        got = [ordered_share, got[1], got[2], got[3]]
     with jax.named_scope("enc_out"):
         enc_share = lax.ppermute(enc_share, "sec", [(1, 0)])
 
-    (partial,) = call(
-        decoder_weight_kernel, [piece_out], (sec, rows, kv_grad, order), scalars=1, flops=4 * cols_flops
-    )
     partial, *in_parts = call(
         encoder_kernel,
         [piece_out] + part_outs,
-        (sec, mp, order, ordered_rows, weights, hidden, slope, *got, partial),
+        (sec, mp, ordered_rows, weights, down, hidden, slope, *got, partial),
         scalars=2,
-        scratch=[part_scratch] * 2,
-        flops=5 * cols_flops,
+        scratch=[pltpu.VMEM((local_rows, half), BF16), part_scratch, part_scratch],
+        flops=4 * cols_flops,
         alias={11: 0},
     )
     with jax.named_scope("exchange"):
         partial = lax.all_to_all(partial, ("x", "y"), 0, 0, tiled=True)
     with jax.named_scope("in_reduce"):
-        in_parts = mp_parts(in_parts, 1, 1)
-    in_share = mp_sum(in_parts)
+        in_share = mp_sum(mp_parts(in_parts, 1, 1))
     blocks = call(
         sum_kernel, [((PADDED, 2 * half), BF16)] * SIDE, (zh, partial), scalars=1, scratch=[sum_scratch]
     )

time: 95.8 us -> 93.2 us (0.973)
  waiting for transfers between devices: 27.8 us -> 24.7 us
    ppermute x3, waiting for transfers between devices: 1.88 us -> 0.02 us  [shards(): came = lax.ppermute(blocks[step], 'zh', pairs)]
    ppermute x10, waiting for transfers between devices: 19.1 us -> 18 us  [mp_move(): return lax.ppermute(value, ('sec', 'mp'), pairs)]
    pallas_call x4 -> x5, Pallas kernels: 6.83 us -> 7.41 us  [call(): pl.pallas_call(kernel, out_shape=[jax.ShapeDtypeStruct(shape, kind) for s...]
  transfers between devices with their start and end apart: 15 -> 15, of which waited for: 6 -> 5; matrix products, arithmetic and copies ran while one was open for 2% -> 2% of each run, Pallas kernels for 1% -> 2%
where the time goes in v5:
time: 93.2 us; the launch traced here: 92.7 us
  starting transfers between devices  53.5 us (57%)
  waiting for transfers between devices  24.7 us (27%)
  Pallas kernels  7.41 us (8%)
  local copies, waits for them, and re-layouts  4.17 us (4%)
  other arithmetic  1.92 us (2%)
  between operations  0.97 us (1%)
    ppermute x10, starting transfers between devices, mp_move(): return lax.ppermute(value, ('sec', 'mp'), pairs)  23.8 us
    ppermute x3, starting transfers between devices, shards(): came = lax.ppermute(blocks[step], 'zh', pairs)  23.4 us
    ppermute x10, waiting for transfers between devices, mp_move(): return lax.ppermute(value, ('sec', 'mp'), pairs)  18 us
    pallas_call x5, Pallas kernels, call(): pl.pallas_call(kernel, out_shape=[jax.ShapeDtypeStruct(shape, kind) for s...  7.41 us
    all_to_all x1, waiting for transfers between devices, shards(): partial = lax.all_to_all(partial, ('x', 'y'), 0, 0, tiled=True)  6.73 us
    all_to_all x1, starting transfers between devices, shards(): partial = lax.all_to_all(partial, ('x', 'y'), 0, 0, tiled=True)  5 us
    unnamed x15, local copies, waits for them, and re-layouts  3.36 us
    broadcast_in_dim x1, other arithmetic, shards(): return (jnp.where(is_decoder, enc_share, in_share)[None], weight_part)  1.89 us
  transfers between devices with their start and end apart: 15, of which 5 were waited for; matrix products, arithmetic and copies ran while one was open for 2% of the time, Pallas kernels for 2%

profile of v5, /device:TPU:1, one launch (start us, length us, event | category | flops | bytes accessed | tf_op | source)
XLA Modules:
  0.0 92.7 jit_solution(17065188393798823363)
XLA Ops:
  0.7 0.1 reshape.139.order_ref
  0.8 0.0 copy-start.1
  0.8 0.0 copy-start.2
  0.8 0.0 copy-start.3
  0.8 0.0 copy-start.4
  0.8 0.0 copy-start.5
  0.9 0.0 copy-start.6
  0.9 2.1 %copy.10 = bf16[112,8,2,512]{3,1,2,0:T(8,128)(2,1)S(1)} copy(bf16[112,8,2,512]{3,2,1,0:T(2,128)(2,1)} %bitcast.14) | data formatting | bytes 3670016
  3.0 0.0 copy-done.1
  3.0 0.0 copy-done.2
  3.0 2.8 %shard_map.86 = (bf16[512,1024]{1,0:T(8,128)(2,1)S(1)}, bf16[128,896]{1,0:T(8,128)(2,1)S(1)}, bf16[128,896]{1,0:T(8,128)(2,1)S(1)}, bf16[128,896]{1,0:T(8,128)(2...) custom-call(s32[1]{0:T(128)} %bitcast.sec_ref, ...), custom_call_target="tpu_custom_call" | custom-call | flops 1879048192 | bytes 4194304 | tf_op jit(solution)/shard_map/pallas_call | solution.py:169
  5.8 1.3 %collective-permute-start = (bf16[128,896]{1,0:T(8,128)(2,1)S(1)}, bf16[128,896]{1,0:T(8,128)(2,1)S(1)}, u32[]{:S(2)}, u32[]{:S(2)}) collective-permute-start(bf16[128,896]{1,0:T(8,128)(2,1)S(1)} %get-tuple-element.23), channel_id=1, source_target_pairs={{0,258},{1,259},{2,256},{3,257},{4,262},{5,263},{6,260},{7,261},{8... | collective-permute-start | bytes 688136 | tf_op jit(solution)/shard_map/enc_reduce/ppermute | solution.py:183
  7.1 1.3 %collective-permute-start.1 = (bf16[128,896]{1,0:T(8,128)(2,1)S(1)}, bf16[128,896]{1,0:T(8,128)(2,1)S(1)}, u32[]{:S(2)}, u32[]{:S(2)}) collective-permute-start(bf16[128,896]{1,0:T(8,128)(2,1)S(1)} %get-tuple-element.24), channel_id=1, source_target_pairs={{0,257},{1,258},{2,259},{3,256},{4,261},{5,262},{6,263},{7,260},{8... | collective-permute-start | bytes 688136 | tf_op jit(solution)/shard_map/enc_reduce/ppermute | solution.py:183
  8.4 1.3 %collective-permute-start.2 = (bf16[128,896]{1,0:T(8,128)(2,1)S(1)}, bf16[128,896]{1,0:T(8,128)(2,1)S(1)}, u32[]{:S(2)}, u32[]{:S(2)}) collective-permute-start(bf16[128,896]{1,0:T(8,128)(2,1)S(1)} %get-tuple-element.25), channel_id=1, source_target_pairs={{0,259},{1,256},{2,257},{3,258},{4,263},{5,260},{6,261},{7,262},{8... | collective-permute-start | bytes 688136 | tf_op jit(solution)/shard_map/enc_reduce/ppermute | solution.py:183
  9.7 1.3 %collective-permute-start.3 = (bf16[128,896]{1,0:T(8,128)(2,1)S(1)}, bf16[128,896]{1,0:T(8,128)(2,1)S(1)}, u32[]{:S(2)}, u32[]{:S(2)}) collective-permute-start(bf16[128,896]{1,0:T(8,128)(2,1)S(1)} %get-tuple-element.26), channel_id=1, source_target_pairs={{0,256},{1,257},{2,258},{3,259},{4,260},{5,261},{6,262},{7,263},{8... | collective-permute-start | bytes 688136 | tf_op jit(solution)/shard_map/enc_reduce/ppermute | solution.py:183
  11.0 10.1 %collective-permute-done.got0 = bf16[128,896]{1,0:T(8,128)(2,1)S(1)} collective-permute-done((bf16[128,896]{1,0:T(8,128)(2,1)S(1)}, bf16[128,896]{1,0:T(8,128)(2,1)S(1)}, u32[]{:S(2)}, u32[]{:S(2)}) %collective-permute-start) | collective-permute-done | bytes 229408 | tf_op jit(solution)/shard_map/enc_reduce/ppermute | solution.py:183
  21.1 0.0 collective-permute-done.1.got1
  21.1 2.1 %collective-permute-done.2.got2 = bf16[128,896]{1,0:T(8,128)(2,1)S(1)} collective-permute-done((bf16[128,896]{1,0:T(8,128)(2,1)S(1)}, bf16[128,896]{1,0:T(8,128)(2,1)S(1)}, u32[]{:S(2)}, u32[]{:S(2)}) %collective-permute-start.2) | collective-permute-done | bytes 229408 | tf_op jit(solution)/shard_map/enc_reduce/ppermute | solution.py:183
  23.2 0.0 collective-permute-done.3.got3
  23.2 0.5 shard_map.87
  23.8 2.5 %collective-permute-start.5 = (bf16[128,896]{1,0:T(8,128)(2,1)S(1)}, bf16[128,896]{1,0:T(8,128)(2,1)S(1)}, u32[]{:S(2)}, u32[]{:S(2)}) collective-permute-start(bf16[128,896]{1,0:T(8,128)(2,1)S(1)} %get-tuple-element.33.got0), channel_id=1, source_target_pairs={{256,257},{257,258},{258,259},{259,256},{260,261},{261,262},{262,2... | collective-permute-start | bytes 688136 | tf_op jit(solution)/shard_map/enc_gather/ppermute | solution.py:183
  26.2 5.1 %collective-permute-start.6 = (bf16[128,896]{1,0:T(8,128)(2,1)S(1)}, bf16[128,896]{1,0:T(8,128)(2,1)S(1)}, u32[]{:S(2)}, u32[]{:S(2)}) collective-permute-start(bf16[128,896]{1,0:T(8,128)(2,1)S(1)} %get-tuple-element.33.got0), channel_id=1, source_target_pairs={{256,258},{257,259},{258,256},{259,257},{260,262},{261,263},{262,2... | collective-permute-start | bytes 688136 | tf_op jit(solution)/shard_map/enc_gather/ppermute | solution.py:183
  31.4 1.9 %collective-permute-start.7 = (bf16[128,896]{1,0:T(8,128)(2,1)S(1)}, bf16[128,896]{1,0:T(8,128)(2,1)S(1)}, u32[]{:S(2)}, u32[]{:S(2)}) collective-permute-start(bf16[128,896]{1,0:T(8,128)(2,1)S(1)} %get-tuple-element.33.got0), channel_id=1, source_target_pairs={{256,259},{257,256},{258,257},{259,258},{260,263},{261,260},{262,2... | collective-permute-start | bytes 688136 | tf_op jit(solution)/shard_map/enc_gather/ppermute | solution.py:183
  33.3 1.2 %shard_map.88 = (bf16[16,56,1024]{2,1,0:T(8,128)(2,1)S(1)}, bf16[896,512]{1,0:T(8,128)(2,1)S(1)}) custom-call(s32[1]{0:T(128)} %bitcast.sec_ref, bf16[512,896]{1,0:T(8,128)(2,1)S(1)} %bitcast.13, bf16[896,1024]{1,0:T(8,128)(2,1)S(1)} %bitcast.10, bf16[512,1024]{1,0:T(8,128)(2,1)S(1)} %get-tuple-element.29.kv_grad_ref, s32[1,896]{1,0:T(1,128)S(1)} %reshape.139.order_ref), custom_call_target="tpu_custom_call" | custom-call | flops 2818572288 | bytes 4194304 | tf_op jit(solution)/shard_map/pallas_call | solution.py:169
  34.4 0.0 collective-permute-done.5.got1
  34.5 3.3 %collective-permute-done.6.got2 = bf16[128,896]{1,0:T(8,128)(2,1)S(1)} collective-permute-done((bf16[128,896]{1,0:T(8,128)(2,1)S(1)}, bf16[128,896]{1,0:T(8,128)(2,1)S(1)}, u32[]{:S(2)}, u32[]{:S(2)}) %collective-permute-start.6) | collective-permute-done | bytes 229408 | tf_op jit(solution)/shard_map/enc_gather/ppermute | solution.py:183
  37.8 2.4 %collective-permute-done.7.got3 = bf16[128,896]{1,0:T(8,128)(2,1)S(1)} collective-permute-done((bf16[128,896]{1,0:T(8,128)(2,1)S(1)}, bf16[128,896]{1,0:T(8,128)(2,1)S(1)}, u32[]{:S(2)}, u32[]{:S(2)}) %collective-permute-start.7) | collective-permute-done | bytes 229408 | tf_op jit(solution)/shard_map/enc_gather/ppermute | solution.py:183
  40.2 2.4 %shard_map.89 = (bf16[16,56,1024]{2,1,0:T(8,128)(2,1)S(1)}, bf16[128,896]{1,0:T(8,128)(2,1)S(1)}, bf16[128,896]{1,0:T(8,128)(2,1)S(1)}, bf16[128,896]{1,0:T(8,128)(2,1)S(1)}, bf16[128,896]{1,0:T(8,128)(2,1)S(1)}) custom-call(s32[1]{0:T(128)} %bitcast.sec_ref, s32[1]{0:T(128)} %bitcast.1.mp_ref, ...), custom_call_target="tpu_custom_call", output_to_operand_aliasing={{0}: (11, {})} | custom-call | flops 1879048192 | bytes 4194304 | tf_op jit(solution)/shard_map/pallas_call | solution.py:169
  42.6 1.2 %copy-done = bf16[16,56,1024]{2,1,0:T(8,128)(2,1)} copy-done((bf16[16,56,1024]{2,1,0:T(8,128)(2,1)}, bf16[16,56,1024]{2,1,0:T(8,128)(2,1)S(1)}, u32[]{:S(2)}) %copy-start) | copy-done | bytes 1835032
  43.9 5.0 %all-to-all-start = ((bf16[16,56,1024]{2,1,0:T(8,128)(2,1)}), bf16[16,56,1024]{2,1,0:T(8,128)(2,1)S(1)}, u32[]{:S(2)}, u32[]{:S(2)}) async-start(bf16[16,56,1024]{2,1,0:T(8,128)(2,1)} %copy-done), calls=%async_computation | async-start | bytes 3670016 | tf_op jit(solution)/shard_map/exchange/all_to_all | solution.py:262
  48.9 1.3 %collective-permute-start.4 = (bf16[128,896]{1,0:T(8,128)(2,1)S(1)}, bf16[128,896]{1,0:T(8,128)(2,1)S(1)}, u32[]{:S(2)}, u32[]{:S(2)}) collective-permute-start(bf16[128,896]{1,0:T(8,128)(2,1)S(1)} %get-tuple-element.27), channel_id=1, source_target_pairs={{256,0},{257,1},{258,2},{259,3},{260,4},{261,5},{262,6},{263,7},{2... | collective-permute-start | bytes 688136 | tf_op jit(solution)/shard_map/enc_out/ppermute | solution.py:250
  50.2 5.0 %collective-permute-start.10 = (bf16[128,896]{1,0:T(8,128)(2,1)S(1)}, bf16[128,896]{1,0:T(8,128)(2,1)S(1)}, u32[]{:S(2)}, u32[]{:S(2)}) collective-permute-start(bf16[128,896]{1,0:T(8,128)(2,1)S(1)} %get-tuple-element.37), channel_id=1, source_target_pairs={{256,259},{257,256},{258,257},{259,258},{260,263},{261,260},{262,2... | collective-permute-start | bytes 688136 | tf_op jit(solution)/shard_map/in_reduce/ppermute | solution.py:183
  55.2 1.9 %collective-permute-start.9 = (bf16[128,896]{1,0:T(8,128)(2,1)S(1)}, bf16[128,896]{1,0:T(8,128)(2,1)}, u32[]{:S(2)}, u32[]{:S(2)}) collective-permute-start(bf16[128,896]{1,0:T(8,128)(2,1)S(1)} %get-tuple-element.36), channel_id=1, source_target_pairs={{256,257},{257,258},{258,259},{259,256},{260,261},{261,262},{262,2... | collective-permute-start | bytes 688136 | tf_op jit(solution)/shard_map/in_reduce/ppermute | solution.py:183
  57.1 2.2 %collective-permute-start.8 = (bf16[128,896]{1,0:T(8,128)(2,1)S(1)}, bf16[128,896]{1,0:T(8,128)(2,1)}, u32[]{:S(2)}, u32[]{:S(2)}) collective-permute-start(bf16[128,896]{1,0:T(8,128)(2,1)S(1)} %get-tuple-element.35), channel_id=1, source_target_pairs={{256,258},{257,259},{258,256},{259,257},{260,262},{261,263},{262,2... | collective-permute-start | bytes 688136 | tf_op jit(solution)/shard_map/in_reduce/ppermute | solution.py:183
  59.4 6.7 %all-to-all-done.piece_ref = bf16[16,56,1024]{2,1,0:T(8,128)(2,1)S(1)} async-done(((bf16[16,56,1024]{2,1,0:T(8,128)(2,1)}), bf16[16,56,1024]{2,1,0:T(8,128)(2,1)S(1)}, u32[]{:S(2)}, u32[]{:S(2)}) %all-to-all-start) | async-done | bytes 1835040 | tf_op jit(solution)/shard_map/exchange/all_to_all | solution.py:262
  66.1 0.5 shard_map.90
  66.6 11.2 %collective-permute-start.13 = (bf16[16,1024]{1,0:T(8,128)(2,1)S(1)}, bf16[16,1024]{1,0:T(8,128)(2,1)S(1)}, u32[]{:S(2)}, u32[]{:S(2)}) collective-permute-start(bf16[16,1024]{1,0:T(8,128)(2,1)S(1)} %get-tuple-element.43), channel_id=1, source_target_pairs={{0,48},{16,0},{32,16},{48,32},{1,49},{17,1},{33,17},{49,33},{2,50}... | collective-permute-start | bytes 98312 | tf_op jit(solution)/shard_map/zh_reduce/ppermute | solution.py:272
  77.9 0.0 collective-permute-done.4
  77.9 4.9 %collective-permute-start.12 = (bf16[16,1024]{1,0:T(8,128)(2,1)S(1)}, bf16[16,1024]{1,0:T(8,128)(2,1)S(1)}, u32[]{:S(2)}, u32[]{:S(2)}) collective-permute-start(bf16[16,1024]{1,0:T(8,128)(2,1)S(1)} %get-tuple-element.42), channel_id=1, source_target_pairs={{0,32},{16,48},{32,0},{48,16},{1,33},{17,49},{33,1},{49,17},{2,34}... | collective-permute-start | bytes 98312 | tf_op jit(solution)/shard_map/zh_reduce/ppermute | solution.py:272
  82.8 0.0 collective-permute-done.10
  82.8 7.3 %collective-permute-start.11 = (bf16[16,1024]{1,0:T(8,128)(2,1)S(1)}, bf16[16,1024]{1,0:T(8,128)(2,1)S(1)}, u32[]{:S(2)}, u32[]{:S(2)}) collective-permute-start(bf16[16,1024]{1,0:T(8,128)(2,1)S(1)} %get-tuple-element.41), channel_id=1, source_target_pairs={{0,16},{16,32},{32,48},{48,0},{1,17},{17,33},{33,49},{49,1},{2,18}... | collective-permute-start | bytes 98312 | tf_op jit(solution)/shard_map/zh_reduce/ppermute | solution.py:272
  90.1 0.0 collective-permute-done.9
  90.1 0.0 collective-permute-done.8
  90.1 1.9 %fusion.1 = bf16[1,128,896]{2,1,0:T(8,128)(2,1)} fusion(bf16[128,896]{1,0:T(8,128)(2,1)S(1)} %collective-permute-done.4, bf16[128,896]{1,0:T(8,128)(2,1)S(1)} %get-tuple-element.38, bf16[128,896]{1,0:T(8,128)(2,1)S(1)} %collective-permute-done.10, bf16[128,896]{1,0:T(8,128)(2,1)} %collective-permute-done.9, bf16[128,896]{1,0:T(8,128)(2,1)} %collective-permute-done.8, ...), kind=kLoop, calls=%fused_computation.2 | loop fusion | flops 1032192 | bytes 1376257 | tf_op jit(solution)/shard_map/broadcast_in_dim | solution.py:275
  92.0 0.0 collective-permute-done.13
  92.0 0.0 collective-permute-done.12
  92.0 0.0 collective-permute-done.11
  92.0 0.7 reshape.142
  (7 shorter events, 0.0 us)
Async XLA Ops:
  0.8 2.2 %copy-start.1 = (bf16[1,512,896]{2,1,0:T(8,128)(2,1)S(1)}, bf16[1,512,896]{2,1,0:T(8,128)(2,1)}, u32[]{:S(2)}) copy-start(bf16[1,512,896]{2,1,0:T(8,128)(2,1)} %param.7) | copy-start | bytes 2752516
  0.8 2.2 %copy-start.2 = (bf16[128,512]{1,0:T(8,128)(2,1)S(1)}, bf16[128,512]{1,0:T(8,128)(2,1)}, u32[]{:S(2)}) copy-start(bf16[128,512]{1,0:T(8,128)(2,1)} %query_ref.1) | copy-start | bytes 393220
  0.8 2.2 %copy-start.3 = (bf16[128,512]{1,0:T(8,128)(2,1)S(1)}, bf16[128,512]{1,0:T(8,128)(2,1)}, u32[]{:S(2)}) copy-start(bf16[128,512]{1,0:T(8,128)(2,1)} %grad_ref.1) | copy-start | bytes 393220
  0.8 2.2 %copy-start.4 = (f32[4,128]{1,0:T(4,128)S(1)}, f32[4,128]{1,0:T(4,128)}, u32[]{:S(2)}) copy-start(f32[4,128]{1,0:T(4,128)} %lse_ref.1) | copy-start | bytes 6148
  0.8 2.1 %copy-start.5 = (f32[4,128]{1,0:T(4,128)S(1)}, f32[4,128]{1,0:T(4,128)}, u32[]{:S(2)}) copy-start(f32[4,128]{1,0:T(4,128)} %delta_ref.1) | copy-start | bytes 6148
  0.9 2.1 %copy-start.6 = (s32[2,2]{1,0:T(2,128)S(1)}, s32[2,2]{1,0:T(2,128)}, u32[]{:S(2)}) copy-start(s32[2,2]{1,0:T(2,128)} %span_ref.1) | copy-start | bytes 52
  5.8 15.3 %collective-permute-start = (bf16[128,896]{1,0:T(8,128)(2,1)S(1)}, bf16[128,896]{1,0:T(8,128)(2,1)S(1)}, u32[]{:S(2)}, u32[]{:S(2)}) collective-permute-start(bf16[128,896]{1,0:T(8,128)(2,1)S(1)} %get-tuple-element.23), channel_id=1, source_target_pairs={{0,258},{1,259},{2,256},{3,257},{4,262},{5,263},{6,260},{7,261},{8... | collective-permute-start | bytes 688136 | tf_op jit(solution)/shard_map/enc_reduce/ppermute | solution.py:183
  7.1 14.0 %collective-permute-start.1 = (bf16[128,896]{1,0:T(8,128)(2,1)S(1)}, bf16[128,896]{1,0:T(8,128)(2,1)S(1)}, u32[]{:S(2)}, u32[]{:S(2)}) collective-permute-start(bf16[128,896]{1,0:T(8,128)(2,1)S(1)} %get-tuple-element.24), channel_id=1, source_target_pairs={{0,257},{1,258},{2,259},{3,256},{4,261},{5,262},{6,263},{7,260},{8... | collective-permute-start | bytes 688136 | tf_op jit(solution)/shard_map/enc_reduce/ppermute | solution.py:183
  8.4 14.8 %collective-permute-start.2 = (bf16[128,896]{1,0:T(8,128)(2,1)S(1)}, bf16[128,896]{1,0:T(8,128)(2,1)S(1)}, u32[]{:S(2)}, u32[]{:S(2)}) collective-permute-start(bf16[128,896]{1,0:T(8,128)(2,1)S(1)} %get-tuple-element.25), channel_id=1, source_target_pairs={{0,259},{1,256},{2,257},{3,258},{4,263},{5,260},{6,261},{7,262},{8... | collective-permute-start | bytes 688136 | tf_op jit(solution)/shard_map/enc_reduce/ppermute | solution.py:183
  9.7 13.5 %collective-permute-start.3 = (bf16[128,896]{1,0:T(8,128)(2,1)S(1)}, bf16[128,896]{1,0:T(8,128)(2,1)S(1)}, u32[]{:S(2)}, u32[]{:S(2)}) collective-permute-start(bf16[128,896]{1,0:T(8,128)(2,1)S(1)} %get-tuple-element.26), channel_id=1, source_target_pairs={{0,256},{1,257},{2,258},{3,259},{4,260},{5,261},{6,262},{7,263},{8... | collective-permute-start | bytes 688136 | tf_op jit(solution)/shard_map/enc_reduce/ppermute | solution.py:183
  23.8 10.7 %collective-permute-start.5 = (bf16[128,896]{1,0:T(8,128)(2,1)S(1)}, bf16[128,896]{1,0:T(8,128)(2,1)S(1)}, u32[]{:S(2)}, u32[]{:S(2)}) collective-permute-start(bf16[128,896]{1,0:T(8,128)(2,1)S(1)} %get-tuple-element.33.got0), channel_id=1, source_target_pairs={{256,257},{257,258},{258,259},{259,256},{260,261},{261,262},{262,2... | collective-permute-start | bytes 688136 | tf_op jit(solution)/shard_map/enc_gather/ppermute | solution.py:183
  26.2 11.5 %collective-permute-start.6 = (bf16[128,896]{1,0:T(8,128)(2,1)S(1)}, bf16[128,896]{1,0:T(8,128)(2,1)S(1)}, u32[]{:S(2)}, u32[]{:S(2)}) collective-permute-start(bf16[128,896]{1,0:T(8,128)(2,1)S(1)} %get-tuple-element.33.got0), channel_id=1, source_target_pairs={{256,258},{257,259},{258,256},{259,257},{260,262},{261,263},{262,2... | collective-permute-start | bytes 688136 | tf_op jit(solution)/shard_map/enc_gather/ppermute | solution.py:183
  31.4 8.9 %collective-permute-start.7 = (bf16[128,896]{1,0:T(8,128)(2,1)S(1)}, bf16[128,896]{1,0:T(8,128)(2,1)S(1)}, u32[]{:S(2)}, u32[]{:S(2)}) collective-permute-start(bf16[128,896]{1,0:T(8,128)(2,1)S(1)} %get-tuple-element.33.got0), channel_id=1, source_target_pairs={{256,259},{257,256},{258,257},{259,258},{260,263},{261,260},{262,2... | collective-permute-start | bytes 688136 | tf_op jit(solution)/shard_map/enc_gather/ppermute | solution.py:183
  42.6 1.3 %copy-start = (bf16[16,56,1024]{2,1,0:T(8,128)(2,1)}, bf16[16,56,1024]{2,1,0:T(8,128)(2,1)S(1)}, u32[]{:S(2)}) copy-start(bf16[16,56,1024]{2,1,0:T(8,128)(2,1)S(1)} %get-tuple-element.39) | copy-start | bytes 5505028
  43.9 22.2 %all-to-all-start = ((bf16[16,56,1024]{2,1,0:T(8,128)(2,1)}), bf16[16,56,1024]{2,1,0:T(8,128)(2,1)S(1)}, u32[]{:S(2)}, u32[]{:S(2)}) async-start(bf16[16,56,1024]{2,1,0:T(8,128)(2,1)} %copy-done), calls=%async_computation | async-start | bytes 3670016 | tf_op jit(solution)/shard_map/exchange/all_to_all | solution.py:262
  48.9 29.0 %collective-permute-start.4 = (bf16[128,896]{1,0:T(8,128)(2,1)S(1)}, bf16[128,896]{1,0:T(8,128)(2,1)S(1)}, u32[]{:S(2)}, u32[]{:S(2)}) collective-permute-start(bf16[128,896]{1,0:T(8,128)(2,1)S(1)} %get-tuple-element.27), channel_id=1, source_target_pairs={{256,0},{257,1},{258,2},{259,3},{260,4},{261,5},{262,6},{263,7},{2... | collective-permute-start | bytes 688136 | tf_op jit(solution)/shard_map/enc_out/ppermute | solution.py:250
  50.2 32.6 %collective-permute-start.10 = (bf16[128,896]{1,0:T(8,128)(2,1)S(1)}, bf16[128,896]{1,0:T(8,128)(2,1)S(1)}, u32[]{:S(2)}, u32[]{:S(2)}) collective-permute-start(bf16[128,896]{1,0:T(8,128)(2,1)S(1)} %get-tuple-element.37), channel_id=1, source_target_pairs={{256,259},{257,256},{258,257},{259,258},{260,263},{261,260},{262,2... | collective-permute-start | bytes 688136 | tf_op jit(solution)/shard_map/in_reduce/ppermute | solution.py:183
  55.2 34.9 %collective-permute-start.9 = (bf16[128,896]{1,0:T(8,128)(2,1)S(1)}, bf16[128,896]{1,0:T(8,128)(2,1)}, u32[]{:S(2)}, u32[]{:S(2)}) collective-permute-start(bf16[128,896]{1,0:T(8,128)(2,1)S(1)} %get-tuple-element.36), channel_id=1, source_target_pairs={{256,257},{257,258},{258,259},{259,256},{260,261},{261,262},{262,2... | collective-permute-start | bytes 688136 | tf_op jit(solution)/shard_map/in_reduce/ppermute | solution.py:183
  57.1 32.9 %collective-permute-start.8 = (bf16[128,896]{1,0:T(8,128)(2,1)S(1)}, bf16[128,896]{1,0:T(8,128)(2,1)}, u32[]{:S(2)}, u32[]{:S(2)}) collective-permute-start(bf16[128,896]{1,0:T(8,128)(2,1)S(1)} %get-tuple-element.35), channel_id=1, source_target_pairs={{256,258},{257,259},{258,256},{259,257},{260,262},{261,263},{262,2... | collective-permute-start | bytes 688136 | tf_op jit(solution)/shard_map/in_reduce/ppermute | solution.py:183
  66.6 25.4 %collective-permute-start.13 = (bf16[16,1024]{1,0:T(8,128)(2,1)S(1)}, bf16[16,1024]{1,0:T(8,128)(2,1)S(1)}, u32[]{:S(2)}, u32[]{:S(2)}) collective-permute-start(bf16[16,1024]{1,0:T(8,128)(2,1)S(1)} %get-tuple-element.43), channel_id=1, source_target_pairs={{0,48},{16,0},{32,16},{48,32},{1,49},{17,1},{33,17},{49,33},{2,50}... | collective-permute-start | bytes 98312 | tf_op jit(solution)/shard_map/zh_reduce/ppermute | solution.py:272
  77.9 14.1 %collective-permute-start.12 = (bf16[16,1024]{1,0:T(8,128)(2,1)S(1)}, bf16[16,1024]{1,0:T(8,128)(2,1)S(1)}, u32[]{:S(2)}, u32[]{:S(2)}) collective-permute-start(bf16[16,1024]{1,0:T(8,128)(2,1)S(1)} %get-tuple-element.42), channel_id=1, source_target_pairs={{0,32},{16,48},{32,0},{48,16},{1,33},{17,49},{33,1},{49,17},{2,34}... | collective-permute-start | bytes 98312 | tf_op jit(solution)/shard_map/zh_reduce/ppermute | solution.py:272
  82.8 9.2 %collective-permute-start.11 = (bf16[16,1024]{1,0:T(8,128)(2,1)S(1)}, bf16[16,1024]{1,0:T(8,128)(2,1)S(1)}, u32[]{:S(2)}, u32[]{:S(2)}) collective-permute-start(bf16[16,1024]{1,0:T(8,128)(2,1)S(1)} %get-tuple-element.41), channel_id=1, source_target_pairs={{0,16},{16,32},{32,48},{48,0},{1,17},{17,33},{33,49},{49,1},{2,18}... | collective-permute-start | bytes 98312 | tf_op jit(solution)/shard_map/zh_reduce/ppermute | solution.py:272

commit v6 on v5

--- a/solution.py
+++ b/solution.py
@@ -11,6 +11,8 @@
 NEIGH = 128
 BLOCKS = 4
 N_MP = 4
+OUTER = (0, 3)
+INNER = (1, 2)
 SIDE = 4
 PADDED = 16
 SCALE = HEAD_DIM ** (-0.5)
@@ -141,7 +143,7 @@
             part[...] = part_ref[block_rows(lax.rem(mp_ref[0] + step, N_MP)), :]
 
 
-def sum_kernel(zh_ref, piece_ref, out0, out1, out2, out3, total_ref):
+def sum_kernel(zh_ref, piece_ref, keep_ref, send_ref, total_ref):
     total = piece_ref[0].astype(F32)
     for source in range(1, piece_ref.shape[0]):
         total = total + piece_ref[source].astype(F32)
@@ -149,12 +151,30 @@
     share = count // SIDE
     total_ref[:count, :] = total
     total_ref[count:, :] = jnp.zeros((total_ref.shape[0] - count, total_ref.shape[1]), F32)
-    for block in range(SIDE):
-        rows = total_ref[block * share:block * share + PADDED, :].astype(BF16)
-        for step, out in enumerate((out0, out1, out2, out3)):
-            @pl.when(lax.rem(zh_ref[0] + step, SIDE) == block)
-            def store(rows=rows, out=out):
-                out[...] = rows
+    inner = (zh_ref[0] == 1) | (zh_ref[0] == 2)
+
+    def put(out_ref, blocks):
+        for index, block in enumerate(blocks):
+            rows = total_ref[block * share:block * share + PADDED, :]
+            out_ref[index * PADDED:(index + 1) * PADDED, :] = rows.astype(out_ref.dtype)
+
+    @pl.when(inner)
+    def inner_side():
+        put(keep_ref, INNER)
+        put(send_ref, OUTER)
+
+    @pl.when(jnp.logical_not(inner))
+    def outer_side():
+        put(keep_ref, OUTER)
+        put(send_ref, INNER)
+
+
+def halve_kernel(zh_ref, keep_ref, came_ref, own_ref, send_ref):
+    upper = zh_ref[0] >= 2
+    total = keep_ref[...] + came_ref[...].astype(F32)
+    lower_block, upper_block = total[:PADDED, :], total[PADDED:, :]
+    own_ref[...] = jnp.where(upper, upper_block, lower_block)
+    send_ref[...] = jnp.where(upper, lower_block, upper_block).astype(BF16)
 
 
 def vmem():
@@ -262,15 +282,15 @@
         partial = lax.all_to_all(partial, ("x", "y"), 0, 0, tiled=True)
     with jax.named_scope("in_reduce"):
         in_share = mp_sum(mp_parts(in_parts, 1, 1))
-    blocks = call(
-        sum_kernel, [((PADDED, 2 * half), BF16)] * SIDE, (zh, partial), scalars=1, scratch=[sum_scratch]
-    )
-    total = blocks[0].astype(F32)
-    for step in range(1, SIDE):
-        pairs = [(source, (source + step) % SIDE) for source in range(SIDE)]
-        with jax.named_scope("zh_reduce"):
-            came = lax.ppermute(blocks[step], "zh", pairs)
-        total = total + came.astype(F32)
+    block_shape = (PADDED, 2 * half)
+    pair_shape = (2 * PADDED, 2 * half)
+    keep, send = call(sum_kernel, [(pair_shape, F32), (pair_shape, BF16)], (zh, partial), scalars=1, scratch=[sum_scratch])
+    with jax.named_scope("zh_first"):
+        came = lax.ppermute(send, "zh", [(0, 1), (1, 0), (2, 3), (3, 2)])
+    own, send = call(halve_kernel, [(block_shape, F32), (block_shape, BF16)], (zh, keep, came), scalars=1)
+    with jax.named_scope("zh_second"):
+        came = lax.ppermute(send, "zh", [(0, 3), (3, 0), (1, 2), (2, 1)])
+    total = own + came.astype(F32)
     weight_part = (total[:share] / (SIDE * SIDE * SIDE)).reshape(1, share, 2, half)
     return (jnp.where(is_decoder, enc_share, in_share)[None], weight_part)
 

time: 93.2 us -> 89.8 us (0.964)
  starting transfers between devices: 53.5 us -> 48 us
  waiting for transfers between devices: 24.7 us -> 27 us
    ppermute x3 -> x2, starting transfers between devices: 23.4 us -> 17.9 us  [the longest x1 9.01 us: shards(): came = lax.ppermute(send, 'zh', [(0, 3), (3, 0), (1, 2), (2, 1)])]
    ppermute x3 -> x2, waiting for transfers between devices: 0.02 us -> 2.34 us  [the longest x1 2.34 us: shards(): came = lax.ppermute(send, 'zh', [(0, 1), (1, 0), (2, 3), (3, 2)])]
    pallas_call x5 -> x6, Pallas kernels: 7.41 us -> 7.18 us  [call(): pl.pallas_call(kernel, out_shape=[jax.ShapeDtypeStruct(shape, kind) for s...]
  transfers between devices with their start and end apart: 15 -> 14, of which waited for: 5 -> 6; matrix products, arithmetic and copies ran while one was open for 2% -> 2% of each run, Pallas kernels for 2% -> 2%
where the time goes in v6:
time: 89.8 us; the launch traced here: 89.3 us
  starting transfers between devices  48 us (53%)
  waiting for transfers between devices  27 us (30%)
  Pallas kernels  7.18 us (8%)
  local copies, waits for them, and re-layouts  4.17 us (5%)
  other arithmetic  2.02 us (2%)
  between operations  0.96 us (1%)
    ppermute x10, starting transfers between devices, mp_move(): return lax.ppermute(value, ('sec', 'mp'), pairs)  23.8 us
    ppermute x10, waiting for transfers between devices, mp_move(): return lax.ppermute(value, ('sec', 'mp'), pairs)  18 us
    ppermute x1, starting transfers between devices, shards(): came = lax.ppermute(send, 'zh', [(0, 3), (3, 0), (1, 2), (2, 1)])  9.01 us
    ppermute x1, starting transfers between devices, shards(): came = lax.ppermute(send, 'zh', [(0, 1), (1, 0), (2, 3), (3, 2)])  8.86 us
    pallas_call x6, Pallas kernels, call(): pl.pallas_call(kernel, out_shape=[jax.ShapeDtypeStruct(shape, kind) for s...  7.18 us
    all_to_all x1, waiting for transfers between devices, shards(): partial = lax.all_to_all(partial, ('x', 'y'), 0, 0, tiled=True)  6.73 us
    all_to_all x1, starting transfers between devices, shards(): partial = lax.all_to_all(partial, ('x', 'y'), 0, 0, tiled=True)  5 us
    unnamed x15, local copies, waits for them, and re-layouts  3.36 us
  transfers between devices with their start and end apart: 14, of which 6 were waited for; matrix products, arithmetic and copies ran while one was open for 2% of the time, Pallas kernels for 2%

profile of v6, /device:TPU:1, one launch (start us, length us, event | category | flops | bytes accessed | tf_op | source)
XLA Modules:
  0.0 89.3 jit_solution(2521768683296036972)
XLA Ops:
  0.7 0.1 reshape.139.order_ref
  0.8 0.0 copy-start.1
  0.8 0.0 copy-start.2
  0.8 0.0 copy-start.3
  0.8 0.0 copy-start.4
  0.8 0.0 copy-start.5
  0.9 0.0 copy-start.6
  0.9 2.1 %copy.10 = bf16[112,8,2,512]{3,1,2,0:T(8,128)(2,1)S(1)} copy(bf16[112,8,2,512]{3,2,1,0:T(2,128)(2,1)} %bitcast.14) | data formatting | bytes 3670016
  3.0 0.0 copy-done.1
  3.0 0.0 copy-done.2
  3.0 0.0 copy-done.3
  3.0 0.0 copy-done.4
  3.0 2.8 %shard_map.86 = (bf16[512,1024]{1,0:T(8,128)(2,1)S(1)}, bf16[128,896]{1,0:T(8,128)(2,1)S(1)}, bf16[128,896]{1,0:T(8,128)(2,1)S(1)}, bf16[128,896]{1,0:T(8,128)(2...) custom-call(s32[1]{0:T(128)} %bitcast.sec_ref, ...), custom_call_target="tpu_custom_call" | custom-call | flops 1879048192 | bytes 4194304 | tf_op jit(solution)/shard_map/pallas_call | solution.py:189
  5.8 1.3 %collective-permute-start = (bf16[128,896]{1,0:T(8,128)(2,1)S(1)}, bf16[128,896]{1,0:T(8,128)(2,1)S(1)}, u32[]{:S(2)}, u32[]{:S(2)}) collective-permute-start(bf16[128,896]{1,0:T(8,128)(2,1)S(1)} %get-tuple-element.23), channel_id=1, source_target_pairs={{0,258},{1,259},{2,256},{3,257},{4,262},{5,263},{6,260},{7,261},{8... | collective-permute-start | bytes 688136 | tf_op jit(solution)/shard_map/enc_reduce/ppermute | solution.py:203
  7.1 1.3 %collective-permute-start.1 = (bf16[128,896]{1,0:T(8,128)(2,1)S(1)}, bf16[128,896]{1,0:T(8,128)(2,1)S(1)}, u32[]{:S(2)}, u32[]{:S(2)}) collective-permute-start(bf16[128,896]{1,0:T(8,128)(2,1)S(1)} %get-tuple-element.24), channel_id=1, source_target_pairs={{0,257},{1,258},{2,259},{3,256},{4,261},{5,262},{6,263},{7,260},{8... | collective-permute-start | bytes 688136 | tf_op jit(solution)/shard_map/enc_reduce/ppermute | solution.py:203
  8.4 1.3 %collective-permute-start.2 = (bf16[128,896]{1,0:T(8,128)(2,1)S(1)}, bf16[128,896]{1,0:T(8,128)(2,1)S(1)}, u32[]{:S(2)}, u32[]{:S(2)}) collective-permute-start(bf16[128,896]{1,0:T(8,128)(2,1)S(1)} %get-tuple-element.25), channel_id=1, source_target_pairs={{0,259},{1,256},{2,257},{3,258},{4,263},{5,260},{6,261},{7,262},{8... | collective-permute-start | bytes 688136 | tf_op jit(solution)/shard_map/enc_reduce/ppermute | solution.py:203
  9.7 1.3 %collective-permute-start.3 = (bf16[128,896]{1,0:T(8,128)(2,1)S(1)}, bf16[128,896]{1,0:T(8,128)(2,1)S(1)}, u32[]{:S(2)}, u32[]{:S(2)}) collective-permute-start(bf16[128,896]{1,0:T(8,128)(2,1)S(1)} %get-tuple-element.26), channel_id=1, source_target_pairs={{0,256},{1,257},{2,258},{3,259},{4,260},{5,261},{6,262},{7,263},{8... | collective-permute-start | bytes 688136 | tf_op jit(solution)/shard_map/enc_reduce/ppermute | solution.py:203
  11.0 10.1 %collective-permute-done.got0 = bf16[128,896]{1,0:T(8,128)(2,1)S(1)} collective-permute-done((bf16[128,896]{1,0:T(8,128)(2,1)S(1)}, bf16[128,896]{1,0:T(8,128)(2,1)S(1)}, u32[]{:S(2)}, u32[]{:S(2)}) %collective-permute-start) | collective-permute-done | bytes 229408 | tf_op jit(solution)/shard_map/enc_reduce/ppermute | solution.py:203
  21.1 0.0 collective-permute-done.1.got1
  21.1 2.1 %collective-permute-done.2.got2 = bf16[128,896]{1,0:T(8,128)(2,1)S(1)} collective-permute-done((bf16[128,896]{1,0:T(8,128)(2,1)S(1)}, bf16[128,896]{1,0:T(8,128)(2,1)S(1)}, u32[]{:S(2)}, u32[]{:S(2)}) %collective-permute-start.2) | collective-permute-done | bytes 229408 | tf_op jit(solution)/shard_map/enc_reduce/ppermute | solution.py:203
  23.2 0.0 collective-permute-done.3.got3
  23.2 0.5 shard_map.87
  23.8 2.5 %collective-permute-start.5 = (bf16[128,896]{1,0:T(8,128)(2,1)S(1)}, bf16[128,896]{1,0:T(8,128)(2,1)S(1)}, u32[]{:S(2)}, u32[]{:S(2)}) collective-permute-start(bf16[128,896]{1,0:T(8,128)(2,1)S(1)} %get-tuple-element.33.got0), channel_id=1, source_target_pairs={{256,257},{257,258},{258,259},{259,256},{260,261},{261,262},{262,2... | collective-permute-start | bytes 688136 | tf_op jit(solution)/shard_map/enc_gather/ppermute | solution.py:203
  26.2 5.1 %collective-permute-start.6 = (bf16[128,896]{1,0:T(8,128)(2,1)S(1)}, bf16[128,896]{1,0:T(8,128)(2,1)S(1)}, u32[]{:S(2)}, u32[]{:S(2)}) collective-permute-start(bf16[128,896]{1,0:T(8,128)(2,1)S(1)} %get-tuple-element.33.got0), channel_id=1, source_target_pairs={{256,258},{257,259},{258,256},{259,257},{260,262},{261,263},{262,2... | collective-permute-start | bytes 688136 | tf_op jit(solution)/shard_map/enc_gather/ppermute | solution.py:203
  31.4 1.9 %collective-permute-start.7 = (bf16[128,896]{1,0:T(8,128)(2,1)S(1)}, bf16[128,896]{1,0:T(8,128)(2,1)S(1)}, u32[]{:S(2)}, u32[]{:S(2)}) collective-permute-start(bf16[128,896]{1,0:T(8,128)(2,1)S(1)} %get-tuple-element.33.got0), channel_id=1, source_target_pairs={{256,259},{257,256},{258,257},{259,258},{260,263},{261,260},{262,2... | collective-permute-start | bytes 688136 | tf_op jit(solution)/shard_map/enc_gather/ppermute | solution.py:203
  33.3 1.2 %shard_map.88 = (bf16[16,56,1024]{2,1,0:T(8,128)(2,1)S(1)}, bf16[896,512]{1,0:T(8,128)(2,1)S(1)}) custom-call(s32[1]{0:T(128)} %bitcast.sec_ref, bf16[512,896]{1,0:T(8,128)(2,1)S(1)} %bitcast.13, bf16[896,1024]{1,0:T(8,128)(2,1)S(1)} %bitcast.10, bf16[512,1024]{1,0:T(8,128)(2,1)S(1)} %get-tuple-element.29.kv_grad_ref, s32[1,896]{1,0:T(1,128)S(1)} %reshape.139.order_ref), custom_call_target="tpu_custom_call" | custom-call | flops 2818572288 | bytes 4194304 | tf_op jit(solution)/shard_map/pallas_call | solution.py:189
  34.4 0.0 collective-permute-done.5.got1
  34.5 3.3 %collective-permute-done.6.got2 = bf16[128,896]{1,0:T(8,128)(2,1)S(1)} collective-permute-done((bf16[128,896]{1,0:T(8,128)(2,1)S(1)}, bf16[128,896]{1,0:T(8,128)(2,1)S(1)}, u32[]{:S(2)}, u32[]{:S(2)}) %collective-permute-start.6) | collective-permute-done | bytes 229408 | tf_op jit(solution)/shard_map/enc_gather/ppermute | solution.py:203
  37.8 2.4 %collective-permute-done.7.got3 = bf16[128,896]{1,0:T(8,128)(2,1)S(1)} collective-permute-done((bf16[128,896]{1,0:T(8,128)(2,1)S(1)}, bf16[128,896]{1,0:T(8,128)(2,1)S(1)}, u32[]{:S(2)}, u32[]{:S(2)}) %collective-permute-start.7) | collective-permute-done | bytes 229408 | tf_op jit(solution)/shard_map/enc_gather/ppermute | solution.py:203
  40.2 2.4 %shard_map.89 = (bf16[16,56,1024]{2,1,0:T(8,128)(2,1)S(1)}, bf16[128,896]{1,0:T(8,128)(2,1)S(1)}, bf16[128,896]{1,0:T(8,128)(2,1)S(1)}, bf16[128,896]{1,0:T(8,128)(2,1)S(1)}, bf16[128,896]{1,0:T(8,128)(2,1)S(1)}) custom-call(s32[1]{0:T(128)} %bitcast.sec_ref, s32[1]{0:T(128)} %bitcast.1.mp_ref, ...), custom_call_target="tpu_custom_call", output_to_operand_aliasing={{0}: (11, {})} | custom-call | flops 1879048192 | bytes 4194304 | tf_op jit(solution)/shard_map/pallas_call | solution.py:189
  42.6 1.2 %copy-done = bf16[16,56,1024]{2,1,0:T(8,128)(2,1)} copy-done((bf16[16,56,1024]{2,1,0:T(8,128)(2,1)}, bf16[16,56,1024]{2,1,0:T(8,128)(2,1)S(1)}, u32[]{:S(2)}) %copy-start) | copy-done | bytes 1835032
  43.9 5.0 %all-to-all-start = ((bf16[16,56,1024]{2,1,0:T(8,128)(2,1)}), bf16[16,56,1024]{2,1,0:T(8,128)(2,1)S(1)}, u32[]{:S(2)}, u32[]{:S(2)}) async-start(bf16[16,56,1024]{2,1,0:T(8,128)(2,1)} %copy-done), calls=%async_computation | async-start | bytes 3670016 | tf_op jit(solution)/shard_map/exchange/all_to_all | solution.py:282
  48.9 1.3 %collective-permute-start.4 = (bf16[128,896]{1,0:T(8,128)(2,1)S(1)}, bf16[128,896]{1,0:T(8,128)(2,1)S(1)}, u32[]{:S(2)}, u32[]{:S(2)}) collective-permute-start(bf16[128,896]{1,0:T(8,128)(2,1)S(1)} %get-tuple-element.27), channel_id=1, source_target_pairs={{256,0},{257,1},{258,2},{259,3},{260,4},{261,5},{262,6},{263,7},{2... | collective-permute-start | bytes 688136 | tf_op jit(solution)/shard_map/enc_out/ppermute | solution.py:270
  50.2 5.0 %collective-permute-start.10 = (bf16[128,896]{1,0:T(8,128)(2,1)S(1)}, bf16[128,896]{1,0:T(8,128)(2,1)}, u32[]{:S(2)}, u32[]{:S(2)}) collective-permute-start(bf16[128,896]{1,0:T(8,128)(2,1)S(1)} %get-tuple-element.37), channel_id=1, source_target_pairs={{256,259},{257,256},{258,257},{259,258},{260,263},{261,260},{262,2... | collective-permute-start | bytes 688136 | tf_op jit(solution)/shard_map/in_reduce/ppermute | solution.py:203
  55.2 1.9 %collective-permute-start.9 = (bf16[128,896]{1,0:T(8,128)(2,1)S(1)}, bf16[128,896]{1,0:T(8,128)(2,1)}, u32[]{:S(2)}, u32[]{:S(2)}) collective-permute-start(bf16[128,896]{1,0:T(8,128)(2,1)S(1)} %get-tuple-element.36), channel_id=1, source_target_pairs={{256,257},{257,258},{258,259},{259,256},{260,261},{261,262},{262,2... | collective-permute-start | bytes 688136 | tf_op jit(solution)/shard_map/in_reduce/ppermute | solution.py:203
  57.1 2.2 %collective-permute-start.8 = (bf16[128,896]{1,0:T(8,128)(2,1)S(1)}, bf16[128,896]{1,0:T(8,128)(2,1)}, u32[]{:S(2)}, u32[]{:S(2)}) collective-permute-start(bf16[128,896]{1,0:T(8,128)(2,1)S(1)} %get-tuple-element.35), channel_id=1, source_target_pairs={{256,258},{257,259},{258,256},{259,257},{260,262},{261,263},{262,2... | collective-permute-start | bytes 688136 | tf_op jit(solution)/shard_map/in_reduce/ppermute | solution.py:203
  59.4 6.7 %all-to-all-done.piece_ref = bf16[16,56,1024]{2,1,0:T(8,128)(2,1)S(1)} async-done(((bf16[16,56,1024]{2,1,0:T(8,128)(2,1)}), bf16[16,56,1024]{2,1,0:T(8,128)(2,1)S(1)}, u32[]{:S(2)}, u32[]{:S(2)}) %all-to-all-start) | async-done | bytes 1835040 | tf_op jit(solution)/shard_map/exchange/all_to_all | solution.py:282
  66.1 0.3 shard_map.90
  66.4 8.9 %collective-permute-start.11 = (bf16[32,1024]{1,0:T(8,128)(2,1)S(1)}, bf16[32,1024]{1,0:T(8,128)(2,1)S(1)}, u32[]{:S(2)}, u32[]{:S(2)}) collective-permute-start(bf16[32,1024]{1,0:T(8,128)(2,1)S(1)} %get-tuple-element.41), channel_id=1, source_target_pairs={{0,16},{16,0},{32,48},{48,32},{1,17},{17,1},{33,49},{49,33},{2,18}... | collective-permute-start | bytes 196616 | tf_op jit(solution)/shard_map/zh_first/ppermute | solution.py:289
  75.2 2.3 %collective-permute-done.11.came_ref = bf16[32,1024]{1,0:T(8,128)(2,1)S(1)} collective-permute-done((bf16[32,1024]{1,0:T(8,128)(2,1)S(1)}, bf16[32,1024]{1,0:T(8,128)(2,1)S(1)}, u32[]{:S(2)}, u32[]{:S(2)}) %collective-permute-start.11) | collective-permute-done | bytes 65568 | tf_op jit(solution)/shard_map/zh_first/ppermute | solution.py:289
  77.6 9.0 %collective-permute-start.12 = (bf16[16,1024]{1,0:T(8,128)(2,1)S(1)}, bf16[16,1024]{1,0:T(8,128)(2,1)S(1)}, u32[]{:S(2)}, u32[]{:S(2)}) collective-permute-start(bf16[16,1024]{1,0:T(8,128)(2,1)S(1)} %get-tuple-element.43), channel_id=1, source_target_pairs={{0,48},{48,0},{16,32},{32,16},{1,49},{49,1},{17,33},{33,17},{2,50}... | collective-permute-start | bytes 98312 | tf_op jit(solution)/shard_map/zh_second/ppermute | solution.py:292
  86.6 0.0 collective-permute-done.4
  86.6 0.0 collective-permute-done.10
  86.6 0.0 collective-permute-done.9
  86.6 0.0 collective-permute-done.8
  86.6 2.0 %fusion.1 = bf16[1,128,896]{2,1,0:T(8,128)(2,1)} fusion(bf16[128,896]{1,0:T(8,128)(2,1)S(1)} %collective-permute-done.4, bf16[128,896]{1,0:T(8,128)(2,1)S(1)} %get-tuple-element.38, bf16[128,896]{1,0:T(8,128)(2,1)} %collective-permute-done.10, bf16[128,896]{1,0:T(8,128)(2,1)} %collective-permute-done.9, bf16[128,896]{1,0:T(8,128)(2,1)} %collective-permute-done.8, ...), kind=kLoop, calls=%fused_computation.2 | loop fusion | flops 1032192 | bytes 1376257 | tf_op jit(solution)/shard_map/broadcast_in_dim | solution.py:295
  88.6 0.0 collective-permute-done.12
  88.7 0.7 reshape.142
  (6 shorter events, 0.0 us)
Async XLA Ops:
  0.8 2.2 %copy-start.1 = (bf16[1,512,896]{2,1,0:T(8,128)(2,1)S(1)}, bf16[1,512,896]{2,1,0:T(8,128)(2,1)}, u32[]{:S(2)}) copy-start(bf16[1,512,896]{2,1,0:T(8,128)(2,1)} %param.7) | copy-start | bytes 2752516
  0.8 2.2 %copy-start.2 = (bf16[128,512]{1,0:T(8,128)(2,1)S(1)}, bf16[128,512]{1,0:T(8,128)(2,1)}, u32[]{:S(2)}) copy-start(bf16[128,512]{1,0:T(8,128)(2,1)} %query_ref.1) | copy-start | bytes 393220
  0.8 2.2 %copy-start.3 = (bf16[128,512]{1,0:T(8,128)(2,1)S(1)}, bf16[128,512]{1,0:T(8,128)(2,1)}, u32[]{:S(2)}) copy-start(bf16[128,512]{1,0:T(8,128)(2,1)} %grad_ref.1) | copy-start | bytes 393220
  0.8 2.2 %copy-start.4 = (f32[4,128]{1,0:T(4,128)S(1)}, f32[4,128]{1,0:T(4,128)}, u32[]{:S(2)}) copy-start(f32[4,128]{1,0:T(4,128)} %lse_ref.1) | copy-start | bytes 6148
  0.8 2.1 %copy-start.5 = (f32[4,128]{1,0:T(4,128)S(1)}, f32[4,128]{1,0:T(4,128)}, u32[]{:S(2)}) copy-start(f32[4,128]{1,0:T(4,128)} %delta_ref.1) | copy-start | bytes 6148
  0.9 2.1 %copy-start.6 = (s32[2,2]{1,0:T(2,128)S(1)}, s32[2,2]{1,0:T(2,128)}, u32[]{:S(2)}) copy-start(s32[2,2]{1,0:T(2,128)} %span_ref.1) | copy-start | bytes 52
  5.8 15.3 %collective-permute-start = (bf16[128,896]{1,0:T(8,128)(2,1)S(1)}, bf16[128,896]{1,0:T(8,128)(2,1)S(1)}, u32[]{:S(2)}, u32[]{:S(2)}) collective-permute-start(bf16[128,896]{1,0:T(8,128)(2,1)S(1)} %get-tuple-element.23), channel_id=1, source_target_pairs={{0,258},{1,259},{2,256},{3,257},{4,262},{5,263},{6,260},{7,261},{8... | collective-permute-start | bytes 688136 | tf_op jit(solution)/shard_map/enc_reduce/ppermute | solution.py:203
  7.1 14.0 %collective-permute-start.1 = (bf16[128,896]{1,0:T(8,128)(2,1)S(1)}, bf16[128,896]{1,0:T(8,128)(2,1)S(1)}, u32[]{:S(2)}, u32[]{:S(2)}) collective-permute-start(bf16[128,896]{1,0:T(8,128)(2,1)S(1)} %get-tuple-element.24), channel_id=1, source_target_pairs={{0,257},{1,258},{2,259},{3,256},{4,261},{5,262},{6,263},{7,260},{8... | collective-permute-start | bytes 688136 | tf_op jit(solution)/shard_map/enc_reduce/ppermute | solution.py:203
  8.4 14.8 %collective-permute-start.2 = (bf16[128,896]{1,0:T(8,128)(2,1)S(1)}, bf16[128,896]{1,0:T(8,128)(2,1)S(1)}, u32[]{:S(2)}, u32[]{:S(2)}) collective-permute-start(bf16[128,896]{1,0:T(8,128)(2,1)S(1)} %get-tuple-element.25), channel_id=1, source_target_pairs={{0,259},{1,256},{2,257},{3,258},{4,263},{5,260},{6,261},{7,262},{8... | collective-permute-start | bytes 688136 | tf_op jit(solution)/shard_map/enc_reduce/ppermute | solution.py:203
  9.7 13.5 %collective-permute-start.3 = (bf16[128,896]{1,0:T(8,128)(2,1)S(1)}, bf16[128,896]{1,0:T(8,128)(2,1)S(1)}, u32[]{:S(2)}, u32[]{:S(2)}) collective-permute-start(bf16[128,896]{1,0:T(8,128)(2,1)S(1)} %get-tuple-element.26), channel_id=1, source_target_pairs={{0,256},{1,257},{2,258},{3,259},{4,260},{5,261},{6,262},{7,263},{8... | collective-permute-start | bytes 688136 | tf_op jit(solution)/shard_map/enc_reduce/ppermute | solution.py:203
  23.8 10.7 %collective-permute-start.5 = (bf16[128,896]{1,0:T(8,128)(2,1)S(1)}, bf16[128,896]{1,0:T(8,128)(2,1)S(1)}, u32[]{:S(2)}, u32[]{:S(2)}) collective-permute-start(bf16[128,896]{1,0:T(8,128)(2,1)S(1)} %get-tuple-element.33.got0), channel_id=1, source_target_pairs={{256,257},{257,258},{258,259},{259,256},{260,261},{261,262},{262,2... | collective-permute-start | bytes 688136 | tf_op jit(solution)/shard_map/enc_gather/ppermute | solution.py:203
  26.2 11.5 %collective-permute-start.6 = (bf16[128,896]{1,0:T(8,128)(2,1)S(1)}, bf16[128,896]{1,0:T(8,128)(2,1)S(1)}, u32[]{:S(2)}, u32[]{:S(2)}) collective-permute-start(bf16[128,896]{1,0:T(8,128)(2,1)S(1)} %get-tuple-element.33.got0), channel_id=1, source_target_pairs={{256,258},{257,259},{258,256},{259,257},{260,262},{261,263},{262,2... | collective-permute-start | bytes 688136 | tf_op jit(solution)/shard_map/enc_gather/ppermute | solution.py:203
  31.4 8.9 %collective-permute-start.7 = (bf16[128,896]{1,0:T(8,128)(2,1)S(1)}, bf16[128,896]{1,0:T(8,128)(2,1)S(1)}, u32[]{:S(2)}, u32[]{:S(2)}) collective-permute-start(bf16[128,896]{1,0:T(8,128)(2,1)S(1)} %get-tuple-element.33.got0), channel_id=1, source_target_pairs={{256,259},{257,256},{258,257},{259,258},{260,263},{261,260},{262,2... | collective-permute-start | bytes 688136 | tf_op jit(solution)/shard_map/enc_gather/ppermute | solution.py:203
  42.6 1.3 %copy-start = (bf16[16,56,1024]{2,1,0:T(8,128)(2,1)}, bf16[16,56,1024]{2,1,0:T(8,128)(2,1)S(1)}, u32[]{:S(2)}) copy-start(bf16[16,56,1024]{2,1,0:T(8,128)(2,1)S(1)} %get-tuple-element.39) | copy-start | bytes 5505028
  43.9 22.2 %all-to-all-start = ((bf16[16,56,1024]{2,1,0:T(8,128)(2,1)}), bf16[16,56,1024]{2,1,0:T(8,128)(2,1)S(1)}, u32[]{:S(2)}, u32[]{:S(2)}) async-start(bf16[16,56,1024]{2,1,0:T(8,128)(2,1)} %copy-done), calls=%async_computation | async-start | bytes 3670016 | tf_op jit(solution)/shard_map/exchange/all_to_all | solution.py:282
  48.9 37.7 %collective-permute-start.4 = (bf16[128,896]{1,0:T(8,128)(2,1)S(1)}, bf16[128,896]{1,0:T(8,128)(2,1)S(1)}, u32[]{:S(2)}, u32[]{:S(2)}) collective-permute-start(bf16[128,896]{1,0:T(8,128)(2,1)S(1)} %get-tuple-element.27), channel_id=1, source_target_pairs={{256,0},{257,1},{258,2},{259,3},{260,4},{261,5},{262,6},{263,7},{2... | collective-permute-start | bytes 688136 | tf_op jit(solution)/shard_map/enc_out/ppermute | solution.py:270
  50.2 36.4 %collective-permute-start.10 = (bf16[128,896]{1,0:T(8,128)(2,1)S(1)}, bf16[128,896]{1,0:T(8,128)(2,1)}, u32[]{:S(2)}, u32[]{:S(2)}) collective-permute-start(bf16[128,896]{1,0:T(8,128)(2,1)S(1)} %get-tuple-element.37), channel_id=1, source_target_pairs={{256,259},{257,256},{258,257},{259,258},{260,263},{261,260},{262,2... | collective-permute-start | bytes 688136 | tf_op jit(solution)/shard_map/in_reduce/ppermute | solution.py:203
  55.2 31.4 %collective-permute-start.9 = (bf16[128,896]{1,0:T(8,128)(2,1)S(1)}, bf16[128,896]{1,0:T(8,128)(2,1)}, u32[]{:S(2)}, u32[]{:S(2)}) collective-permute-start(bf16[128,896]{1,0:T(8,128)(2,1)S(1)} %get-tuple-element.36), channel_id=1, source_target_pairs={{256,257},{257,258},{258,259},{259,256},{260,261},{261,262},{262,2... | collective-permute-start | bytes 688136 | tf_op jit(solution)/shard_map/in_reduce/ppermute | solution.py:203
  57.1 29.5 %collective-permute-start.8 = (bf16[128,896]{1,0:T(8,128)(2,1)S(1)}, bf16[128,896]{1,0:T(8,128)(2,1)}, u32[]{:S(2)}, u32[]{:S(2)}) collective-permute-start(bf16[128,896]{1,0:T(8,128)(2,1)S(1)} %get-tuple-element.35), channel_id=1, source_target_pairs={{256,258},{257,259},{258,256},{259,257},{260,262},{261,263},{262,2... | collective-permute-start | bytes 688136 | tf_op jit(solution)/shard_map/in_reduce/ppermute | solution.py:203
  66.4 11.2 %collective-permute-start.11 = (bf16[32,1024]{1,0:T(8,128)(2,1)S(1)}, bf16[32,1024]{1,0:T(8,128)(2,1)S(1)}, u32[]{:S(2)}, u32[]{:S(2)}) collective-permute-start(bf16[32,1024]{1,0:T(8,128)(2,1)S(1)} %get-tuple-element.41), channel_id=1, source_target_pairs={{0,16},{16,0},{32,48},{48,32},{1,17},{17,1},{33,49},{49,33},{2,18}... | collective-permute-start | bytes 196616 | tf_op jit(solution)/shard_map/zh_first/ppermute | solution.py:289
  77.6 11.1 %collective-permute-start.12 = (bf16[16,1024]{1,0:T(8,128)(2,1)S(1)}, bf16[16,1024]{1,0:T(8,128)(2,1)S(1)}, u32[]{:S(2)}, u32[]{:S(2)}) collective-permute-start(bf16[16,1024]{1,0:T(8,128)(2,1)S(1)} %get-tuple-element.43), channel_id=1, source_target_pairs={{0,48},{48,0},{16,32},{32,16},{1,49},{49,1},{17,33},{33,17},{2,50}... | collective-permute-start | bytes 98312 | tf_op jit(solution)/shard_map/zh_second/ppermute | solution.py:292

commit v7 on v6

--- a/solution.py
+++ b/solution.py
@@ -126,8 +126,8 @@
         ordered_ref[...] = mm(share, places(order_ref)).astype(BF16)
 
 
-def encoder_kernel(sec_ref, mp_ref, ordered_ref, weight_ref, down_ref, hidden_ref, slope_ref, got0, got1, got2, got3, keep_ref,
-                   partial_ref, part0, part1, part2, part3, pre_grad_ref, arrived_ref, part_ref):
+def encoder_kernel(sec_ref, mp_ref, ordered_ref, down_ref, hidden_ref, slope_ref, got0, got1, got2, got3, keep_ref,
+                   partial_ref, pre_grad_ref, arrived_ref):
     del keep_ref
     @on_section(sec_ref, 1)
     def work():
@@ -138,6 +138,12 @@
         store_chunks(partial_ref, mm(arrived, hidden_ref[...], TN), half)
         pre_grad_ref[...] = (mm(arrived, down_ref[...]) * slope_ref[...]).astype(BF16)
         store_chunks(partial_ref, mm(ordered_ref[...], pre_grad_ref[...], TN))
+
+
+def input_kernel(sec_ref, mp_ref, weight_ref, pre_grad_ref, part0, part1, part2, part3, part_ref):
+    @on_section(sec_ref, 1)
+    def work():
+        half = pre_grad_ref.shape[1]
         part_ref[...] = mm(pre_grad_ref[...], weight_ref[:, :half], NT).astype(BF16)
         for step, part in enumerate((part0, part1, part2, part3)):
             part[...] = part_ref[block_rows(lax.rem(mp_ref[0] + step, N_MP)), :]
@@ -175,6 +181,13 @@
     lower_block, upper_block = total[:PADDED, :], total[PADDED:, :]
     own_ref[...] = jnp.where(upper, upper_block, lower_block)
     send_ref[...] = jnp.where(upper, lower_block, upper_block).astype(BF16)
+
+
+def last_kernel(own_ref, came_ref, out_ref):
+    share, half = out_ref.shape[1], out_ref.shape[3]
+    total = (own_ref[...] + came_ref[...].astype(F32)) * (1.0 / (SIDE * SIDE * SIDE))
+    for column in range(2):
+        out_ref[0, :, column, :] = total[:share, column * half:(column + 1) * half]
 
 
 def vmem():
@@ -269,15 +282,24 @@
     with jax.named_scope("enc_out"):
         enc_share = lax.ppermute(enc_share, "sec", [(1, 0)])
 
-    partial, *in_parts = call(
+    partial, pre_grad = call(
         encoder_kernel,
-        [piece_out] + part_outs,
-        (sec, mp, ordered_rows, weights, down, hidden, slope, *got, partial),
+        [piece_out, col_out],
+        (sec, mp, ordered_rows, down, hidden, slope, *got, partial),
         scalars=2,
-        scratch=[pltpu.VMEM((local_rows, half), BF16), part_scratch, part_scratch],
+        scratch=[part_scratch],
         flops=4 * cols_flops,
-        alias={11: 0},
-    )
+        alias={10: 0},
+    )
+    in_parts = call(
+        input_kernel,
+        part_outs,
+        (sec, mp, weights, pre_grad),
+        scalars=2,
+        scratch=[part_scratch],
+        flops=cols_flops,
+    )
+    partial, *in_parts = lax.optimization_barrier((partial, *in_parts))
     with jax.named_scope("exchange"):
         partial = lax.all_to_all(partial, ("x", "y"), 0, 0, tiled=True)
     with jax.named_scope("in_reduce"):
@@ -287,12 +309,12 @@
     keep, send = call(sum_kernel, [(pair_shape, F32), (pair_shape, BF16)], (zh, partial), scalars=1, scratch=[sum_scratch])
     with jax.named_scope("zh_first"):
         came = lax.ppermute(send, "zh", [(0, 1), (1, 0), (2, 3), (3, 2)])
+    came, row_part = lax.optimization_barrier((came, jnp.where(is_decoder, enc_share, in_share)[None]))
     own, send = call(halve_kernel, [(block_shape, F32), (block_shape, BF16)], (zh, keep, came), scalars=1)
     with jax.named_scope("zh_second"):
         came = lax.ppermute(send, "zh", [(0, 3), (3, 0), (1, 2), (2, 1)])
-    total = own + came.astype(F32)
-    weight_part = (total[:share] / (SIDE * SIDE * SIDE)).reshape(1, share, 2, half)
-    return (jnp.where(is_decoder, enc_share, in_share)[None], weight_part)
+    (weight_part,) = call(last_kernel, [((1, share, 2, half), F32)], (own, came))
+    return (row_part, weight_part)
 
 
 def solution(mesh):

time: 89.8 us -> 89.2 us (level)
    ppermute x1, waiting for transfers between devices: 2.34 us -> 0.41 us  [shards(): came = lax.ppermute(send, 'zh', [(0, 1), (1, 0), (2, 3), (3, 2)])]
    ppermute x1, waiting for transfers between devices: 0.01 us -> 1.29 us  [shards(): came = lax.ppermute(send, 'zh', [(0, 3), (3, 0), (1, 2), (2, 1)])]
    pallas_call x6 -> x8, Pallas kernels: 7.18 us -> 8.03 us  [call(): pl.pallas_call(kernel, out_shape=[jax.ShapeDtypeStruct(shape, kind) for s...]
  transfers between devices with their start and end apart: 14 -> 14, of which waited for: 6 -> 7; matrix products, arithmetic and copies ran while one was open for 2% -> 2% of each run, Pallas kernels for 2% -> 2%
where the time goes in v7:
time: 89.2 us; the launch traced here: 88.7 us
  starting transfers between devices  47.9 us (54%)
  waiting for transfers between devices  26.4 us (30%)
  Pallas kernels  8.03 us (9%)
  local copies, waits for them, and re-layouts  3.5 us (4%)
  other arithmetic  1.9 us (2%)
  between operations  0.97 us (1%)
    ppermute x10, starting transfers between devices, mp_move(): return lax.ppermute(value, ('sec', 'mp'), pairs)  23.7 us
    ppermute x10, waiting for transfers between devices, mp_move(): return lax.ppermute(value, ('sec', 'mp'), pairs)  18 us
    ppermute x1, starting transfers between devices, shards(): came = lax.ppermute(send, 'zh', [(0, 3), (3, 0), (1, 2), (2, 1)])  9.03 us
    ppermute x1, starting transfers between devices, shards(): came = lax.ppermute(send, 'zh', [(0, 1), (1, 0), (2, 3), (3, 2)])  8.8 us
    pallas_call x8, Pallas kernels, call(): pl.pallas_call(kernel, out_shape=[jax.ShapeDtypeStruct(shape, kind) for s...  8.03 us
    all_to_all x1, waiting for transfers between devices, shards(): partial = lax.all_to_all(partial, ('x', 'y'), 0, 0, tiled=True)  6.75 us
    all_to_all x1, starting transfers between devices, shards(): partial = lax.all_to_all(partial, ('x', 'y'), 0, 0, tiled=True)  5.04 us
    unnamed x15, local copies, waits for them, and re-layouts  3.35 us
  transfers between devices with their start and end apart: 14, of which 7 were waited for; matrix products, arithmetic and copies ran while one was open for 2% of the time, Pallas kernels for 2%

profile of v7, /device:TPU:1, one launch (start us, length us, event | category | flops | bytes accessed | tf_op | source)
XLA Modules:
  0.0 88.7 jit_solution(9273327291323000261)
XLA Ops:
  0.7 0.0 copy-start.1
  0.7 0.0 copy-start.2
  0.7 0.0 copy-start.3
  0.7 0.0 copy-start.4
  0.7 0.0 copy-start.5
  0.7 0.0 copy-start.6
  0.7 2.1 %copy.10 = bf16[112,8,2,512]{3,1,2,0:T(8,128)(2,1)S(1)} copy(bf16[112,8,2,512]{3,2,1,0:T(2,128)(2,1)} %bitcast.14) | data formatting | bytes 3670016
  2.8 0.1 reshape.138.order_ref
  3.0 0.0 copy-done.1
  3.0 0.0 copy-done.2
  3.0 0.0 copy-done.3
  3.0 2.8 %shard_map.86 = (bf16[512,1024]{1,0:T(8,128)(2,1)S(1)}, bf16[128,896]{1,0:T(8,128)(2,1)S(1)}, bf16[128,896]{1,0:T(8,128)(2,1)S(1)}, bf16[128,896]{1,0:T(8,128)(2...) custom-call(s32[1]{0:T(128)} %bitcast.1.sec_ref, ...), custom_call_target="tpu_custom_call" | custom-call | flops 1879048192 | bytes 4194304 | tf_op jit(solution)/shard_map/pallas_call | solution.py:202
  5.8 1.3 %collective-permute-start = (bf16[128,896]{1,0:T(8,128)(2,1)S(1)}, bf16[128,896]{1,0:T(8,128)(2,1)S(1)}, u32[]{:S(2)}, u32[]{:S(2)}) collective-permute-start(bf16[128,896]{1,0:T(8,128)(2,1)S(1)} %get-tuple-element.36), channel_id=1, source_target_pairs={{0,258},{1,259},{2,256},{3,257},{4,262},{5,263},{6,260},{7,261},{8... | collective-permute-start | bytes 688136 | tf_op jit(solution)/shard_map/enc_reduce/ppermute | solution.py:216
  7.1 1.3 %collective-permute-start.1 = (bf16[128,896]{1,0:T(8,128)(2,1)S(1)}, bf16[128,896]{1,0:T(8,128)(2,1)S(1)}, u32[]{:S(2)}, u32[]{:S(2)}) collective-permute-start(bf16[128,896]{1,0:T(8,128)(2,1)S(1)} %get-tuple-element.37), channel_id=1, source_target_pairs={{0,257},{1,258},{2,259},{3,256},{4,261},{5,262},{6,263},{7,260},{8... | collective-permute-start | bytes 688136 | tf_op jit(solution)/shard_map/enc_reduce/ppermute | solution.py:216
  8.4 1.3 %collective-permute-start.2 = (bf16[128,896]{1,0:T(8,128)(2,1)S(1)}, bf16[128,896]{1,0:T(8,128)(2,1)S(1)}, u32[]{:S(2)}, u32[]{:S(2)}) collective-permute-start(bf16[128,896]{1,0:T(8,128)(2,1)S(1)} %get-tuple-element.38), channel_id=1, source_target_pairs={{0,259},{1,256},{2,257},{3,258},{4,263},{5,260},{6,261},{7,262},{8... | collective-permute-start | bytes 688136 | tf_op jit(solution)/shard_map/enc_reduce/ppermute | solution.py:216
  9.7 1.3 %collective-permute-start.3 = (bf16[128,896]{1,0:T(8,128)(2,1)S(1)}, bf16[128,896]{1,0:T(8,128)(2,1)S(1)}, u32[]{:S(2)}, u32[]{:S(2)}) collective-permute-start(bf16[128,896]{1,0:T(8,128)(2,1)S(1)} %get-tuple-element.39), channel_id=1, source_target_pairs={{0,256},{1,257},{2,258},{3,259},{4,260},{5,261},{6,262},{7,263},{8... | collective-permute-start | bytes 688136 | tf_op jit(solution)/shard_map/enc_reduce/ppermute | solution.py:216
  11.0 10.1 %collective-permute-done.got0 = bf16[128,896]{1,0:T(8,128)(2,1)S(1)} collective-permute-done((bf16[128,896]{1,0:T(8,128)(2,1)S(1)}, bf16[128,896]{1,0:T(8,128)(2,1)S(1)}, u32[]{:S(2)}, u32[]{:S(2)}) %collective-permute-start) | collective-permute-done | bytes 229408 | tf_op jit(solution)/shard_map/enc_reduce/ppermute | solution.py:216
  21.1 0.0 collective-permute-done.1.got1
  21.1 2.1 %collective-permute-done.2.got2 = bf16[128,896]{1,0:T(8,128)(2,1)S(1)} collective-permute-done((bf16[128,896]{1,0:T(8,128)(2,1)S(1)}, bf16[128,896]{1,0:T(8,128)(2,1)S(1)}, u32[]{:S(2)}, u32[]{:S(2)}) %collective-permute-start.2) | collective-permute-done | bytes 229408 | tf_op jit(solution)/shard_map/enc_reduce/ppermute | solution.py:216
  23.2 0.0 collective-permute-done.3.got3
  23.3 0.5 shard_map.88
  23.8 2.5 %collective-permute-start.4 = (bf16[128,896]{1,0:T(8,128)(2,1)S(1)}, bf16[128,896]{1,0:T(8,128)(2,1)S(1)}, u32[]{:S(2)}, u32[]{:S(2)}) collective-permute-start(bf16[128,896]{1,0:T(8,128)(2,1)S(1)} %get-tuple-element.40.got0), channel_id=1, source_target_pairs={{256,257},{257,258},{258,259},{259,256},{260,261},{261,262},{262,2... | collective-permute-start | bytes 688136 | tf_op jit(solution)/shard_map/enc_gather/ppermute | solution.py:216
  26.2 5.1 %collective-permute-start.5 = (bf16[128,896]{1,0:T(8,128)(2,1)S(1)}, bf16[128,896]{1,0:T(8,128)(2,1)S(1)}, u32[]{:S(2)}, u32[]{:S(2)}) collective-permute-start(bf16[128,896]{1,0:T(8,128)(2,1)S(1)} %get-tuple-element.40.got0), channel_id=1, source_target_pairs={{256,258},{257,259},{258,256},{259,257},{260,262},{261,263},{262,2... | collective-permute-start | bytes 688136 | tf_op jit(solution)/shard_map/enc_gather/ppermute | solution.py:216
  31.3 1.9 %collective-permute-start.6 = (bf16[128,896]{1,0:T(8,128)(2,1)S(1)}, bf16[128,896]{1,0:T(8,128)(2,1)S(1)}, u32[]{:S(2)}, u32[]{:S(2)}) collective-permute-start(bf16[128,896]{1,0:T(8,128)(2,1)S(1)} %get-tuple-element.40.got0), channel_id=1, source_target_pairs={{256,259},{257,256},{258,257},{259,258},{260,263},{261,260},{262,2... | collective-permute-start | bytes 688136 | tf_op jit(solution)/shard_map/enc_gather/ppermute | solution.py:216
  33.3 1.2 %shard_map.87 = (bf16[16,56,1024]{2,1,0:T(8,128)(2,1)S(1)}, bf16[896,512]{1,0:T(8,128)(2,1)S(1)}) custom-call(s32[1]{0:T(128)} %bitcast.1.sec_ref, bf16[512,896]{1,0:T(8,128)(2,1)S(1)} %bitcast.13, bf16[896,1024]{1,0:T(8,128)(2,1)S(1)} %bitcast.10, bf16[512,1024]{1,0:T(8,128)(2,1)S(1)} %get-tuple-element.32.kv_grad_ref, s32[1,896]{1,0:T(1,128)S(1)} %reshape.138.order_ref), custom_call_target="tpu_custom_call" | custom-call | flops 2818572288 | bytes 4194304 | tf_op jit(solution)/shard_map/pallas_call | solution.py:202
  34.4 0.0 collective-permute-done.4.got1
  34.4 3.3 %collective-permute-done.5.got2 = bf16[128,896]{1,0:T(8,128)(2,1)S(1)} collective-permute-done((bf16[128,896]{1,0:T(8,128)(2,1)S(1)}, bf16[128,896]{1,0:T(8,128)(2,1)S(1)}, u32[]{:S(2)}, u32[]{:S(2)}) %collective-permute-start.5) | collective-permute-done | bytes 229408 | tf_op jit(solution)/shard_map/enc_gather/ppermute | solution.py:216
  37.8 2.4 %collective-permute-done.6.got3 = bf16[128,896]{1,0:T(8,128)(2,1)S(1)} collective-permute-done((bf16[128,896]{1,0:T(8,128)(2,1)S(1)}, bf16[128,896]{1,0:T(8,128)(2,1)S(1)}, u32[]{:S(2)}, u32[]{:S(2)}) %collective-permute-start.6) | collective-permute-done | bytes 229408 | tf_op jit(solution)/shard_map/enc_gather/ppermute | solution.py:216
  40.2 1.8 %shard_map.89 = (bf16[16,56,1024]{2,1,0:T(8,128)(2,1)S(1)}, bf16[512,512]{1,0:T(8,128)(2,1)S(1)}) custom-call(s32[1]{0:T(128)} %bitcast.1.sec_ref, s32[1]{0:T(128)} %bitcast.2.mp_ref, bf16[512,896]{1,0:T(8,128)(2,1)S(1)} %get-tuple-element.31.ordered_ref, bf16[896,512]{1,0:T(8,128)(2,1)S(1)} %get-tuple-element.33.down_ref, ...), custom_call_target="tpu_custom_call", output_to_operand_aliasing={{0}: (10, {})} | custom-call | flops 1879048192 | bytes 4194304 | tf_op jit(solution)/shard_map/pallas_call | solution.py:202
  42.0 1.2 %copy-done = bf16[16,56,1024]{2,1,0:T(8,128)(2,1)} copy-done((bf16[16,56,1024]{2,1,0:T(8,128)(2,1)}, bf16[16,56,1024]{2,1,0:T(8,128)(2,1)S(1)}, u32[]{:S(2)}) %copy-start) | copy-done | bytes 1835032
  43.3 0.8 shard_map.90
  44.1 5.0 %all-to-all-start = ((bf16[16,56,1024]{2,1,0:T(8,128)(2,1)}), bf16[16,56,1024]{2,1,0:T(8,128)(2,1)S(1)}, u32[]{:S(2)}, u32[]{:S(2)}) async-start(bf16[16,56,1024]{2,1,0:T(8,128)(2,1)} %copy-done), calls=%async_computation | async-start | bytes 3670016 | tf_op jit(solution)/shard_map/exchange/all_to_all | solution.py:304
  49.1 1.3 %collective-permute-start.8 = (bf16[128,896]{1,0:T(8,128)(2,1)S(1)}, bf16[128,896]{1,0:T(8,128)(2,1)S(1)}, u32[]{:S(2)}, u32[]{:S(2)}) collective-permute-start(bf16[128,896]{1,0:T(8,128)(2,1)S(1)} %get-tuple-element.50), channel_id=1, source_target_pairs={{256,0},{257,1},{258,2},{259,3},{260,4},{261,5},{262,6},{263,7},{2... | collective-permute-start | bytes 688136 | tf_op jit(solution)/shard_map/enc_out/ppermute | solution.py:283
  50.4 3.8 %collective-permute-start.10 = (bf16[128,896]{1,0:T(8,128)(2,1)S(1)}, bf16[128,896]{1,0:T(8,128)(2,1)S(1)}, u32[]{:S(2)}, u32[]{:S(2)}) collective-permute-start(bf16[128,896]{1,0:T(8,128)(2,1)S(1)} %get-tuple-element.52), channel_id=1, source_target_pairs={{256,257},{257,258},{258,259},{259,256},{260,261},{261,262},{262,2... | collective-permute-start | bytes 688136 | tf_op jit(solution)/shard_map/in_reduce/ppermute | solution.py:216
  54.2 3.3 %collective-permute-start.11 = (bf16[128,896]{1,0:T(8,128)(2,1)S(1)}, bf16[128,896]{1,0:T(8,128)(2,1)}, u32[]{:S(2)}, u32[]{:S(2)}) collective-permute-start(bf16[128,896]{1,0:T(8,128)(2,1)S(1)} %get-tuple-element.53), channel_id=1, source_target_pairs={{256,259},{257,256},{258,257},{259,258},{260,263},{261,260},{262,2... | collective-permute-start | bytes 688136 | tf_op jit(solution)/shard_map/in_reduce/ppermute | solution.py:216
  57.5 2.0 %collective-permute-start.9 = (bf16[128,896]{1,0:T(8,128)(2,1)S(1)}, bf16[128,896]{1,0:T(8,128)(2,1)}, u32[]{:S(2)}, u32[]{:S(2)}) collective-permute-start(bf16[128,896]{1,0:T(8,128)(2,1)S(1)} %get-tuple-element.51), channel_id=1, source_target_pairs={{256,258},{257,259},{258,256},{259,257},{260,262},{261,263},{262,2... | collective-permute-start | bytes 688136 | tf_op jit(solution)/shard_map/in_reduce/ppermute | solution.py:216
  59.6 6.7 %all-to-all-done.piece_ref = bf16[16,56,1024]{2,1,0:T(8,128)(2,1)S(1)} async-done(((bf16[16,56,1024]{2,1,0:T(8,128)(2,1)}), bf16[16,56,1024]{2,1,0:T(8,128)(2,1)S(1)}, u32[]{:S(2)}, u32[]{:S(2)}) %all-to-all-start) | async-done | bytes 1835040 | tf_op jit(solution)/shard_map/exchange/all_to_all | solution.py:304
  66.3 0.3 shard_map.91
  66.6 8.8 %collective-permute-start.7 = (bf16[32,1024]{1,0:T(8,128)(2,1)S(1)}, bf16[32,1024]{1,0:T(8,128)(2,1)S(1)}, u32[]{:S(2)}, u32[]{:S(2)}) collective-permute-start(bf16[32,1024]{1,0:T(8,128)(2,1)S(1)} %get-tuple-element.49), channel_id=1, source_target_pairs={{0,16},{16,0},{32,48},{48,32},{1,17},{17,1},{33,49},{49,33},{2,18}... | collective-permute-start | bytes 196616 | tf_op jit(solution)/shard_map/zh_first/ppermute | solution.py:311
  75.4 0.0 collective-permute-done.8
  75.4 0.0 collective-permute-done.10
  75.4 0.0 collective-permute-done.11
  75.4 0.0 collective-permute-done.9
  75.4 1.9 %fusion.1 = bf16[1,128,896]{2,1,0:T(8,128)(2,1)} fusion(bf16[128,896]{1,0:T(8,128)(2,1)S(1)} %collective-permute-done.8, bf16[128,896]{1,0:T(8,128)(2,1)S(1)} %get-tuple-element.54, bf16[128,896]{1,0:T(8,128)(2,1)} %collective-permute-done.11, bf16[128,896]{1,0:T(8,128)(2,1)S(1)} %collective-permute-done.10, bf16[128,896]{1,0:T(8,128)(2,1)} %collective-permute-done.9, ...), kind=kLoop, calls=%fused_computation.2 | loop fusion | flops 1032192 | bytes 1376257 | tf_op jit(solution)/shard_map/broadcast_in_dim | solution.py:312
  77.3 0.4 collective-permute-done.7.came_ref
  77.8 9.0 %collective-permute-start.12 = (bf16[16,1024]{1,0:T(8,128)(2,1)S(1)}, bf16[16,1024]{1,0:T(8,128)(2,1)S(1)}, u32[]{:S(2)}, u32[]{:S(2)}) collective-permute-start(bf16[16,1024]{1,0:T(8,128)(2,1)S(1)} %get-tuple-element.59), channel_id=1, source_target_pairs={{0,48},{48,0},{16,32},{32,16},{1,49},{49,1},{17,33},{33,17},{2,50}... | collective-permute-start | bytes 98312 | tf_op jit(solution)/shard_map/zh_second/ppermute | solution.py:315
  86.8 1.3 %collective-permute-done.12.came_ref = bf16[16,1024]{1,0:T(8,128)(2,1)S(1)} collective-permute-done((bf16[16,1024]{1,0:T(8,128)(2,1)S(1)}, bf16[16,1024]{1,0:T(8,128)(2,1)S(1)}, u32[]{:S(2)}, u32[]{:S(2)}) %collective-permute-start.12) | collective-permute-done | bytes 32800 | tf_op jit(solution)/shard_map/zh_second/ppermute | solution.py:315
  88.1 0.6 shard_map.93
  (6 shorter events, 0.0 us)
Async XLA Ops:
  0.7 2.3 %copy-start.1 = (bf16[1,512,896]{2,1,0:T(8,128)(2,1)S(1)}, bf16[1,512,896]{2,1,0:T(8,128)(2,1)}, u32[]{:S(2)}) copy-start(bf16[1,512,896]{2,1,0:T(8,128)(2,1)} %param.7) | copy-start | bytes 2752516
  0.7 2.3 %copy-start.2 = (bf16[128,512]{1,0:T(8,128)(2,1)S(1)}, bf16[128,512]{1,0:T(8,128)(2,1)}, u32[]{:S(2)}) copy-start(bf16[128,512]{1,0:T(8,128)(2,1)} %query_ref.1) | copy-start | bytes 393220
  0.7 2.3 %copy-start.3 = (bf16[128,512]{1,0:T(8,128)(2,1)S(1)}, bf16[128,512]{1,0:T(8,128)(2,1)}, u32[]{:S(2)}) copy-start(bf16[128,512]{1,0:T(8,128)(2,1)} %grad_ref.1) | copy-start | bytes 393220
  0.7 2.3 %copy-start.4 = (f32[4,128]{1,0:T(4,128)S(1)}, f32[4,128]{1,0:T(4,128)}, u32[]{:S(2)}) copy-start(f32[4,128]{1,0:T(4,128)} %lse_ref.1) | copy-start | bytes 6148
  0.7 2.3 %copy-start.5 = (f32[4,128]{1,0:T(4,128)S(1)}, f32[4,128]{1,0:T(4,128)}, u32[]{:S(2)}) copy-start(f32[4,128]{1,0:T(4,128)} %delta_ref.1) | copy-start | bytes 6148
  0.7 2.3 %copy-start.6 = (s32[2,2]{1,0:T(2,128)S(1)}, s32[2,2]{1,0:T(2,128)}, u32[]{:S(2)}) copy-start(s32[2,2]{1,0:T(2,128)} %span_ref.1) | copy-start | bytes 52
  5.8 15.3 %collective-permute-start = (bf16[128,896]{1,0:T(8,128)(2,1)S(1)}, bf16[128,896]{1,0:T(8,128)(2,1)S(1)}, u32[]{:S(2)}, u32[]{:S(2)}) collective-permute-start(bf16[128,896]{1,0:T(8,128)(2,1)S(1)} %get-tuple-element.36), channel_id=1, source_target_pairs={{0,258},{1,259},{2,256},{3,257},{4,262},{5,263},{6,260},{7,261},{8... | collective-permute-start | bytes 688136 | tf_op jit(solution)/shard_map/enc_reduce/ppermute | solution.py:216
  7.1 14.0 %collective-permute-start.1 = (bf16[128,896]{1,0:T(8,128)(2,1)S(1)}, bf16[128,896]{1,0:T(8,128)(2,1)S(1)}, u32[]{:S(2)}, u32[]{:S(2)}) collective-permute-start(bf16[128,896]{1,0:T(8,128)(2,1)S(1)} %get-tuple-element.37), channel_id=1, source_target_pairs={{0,257},{1,258},{2,259},{3,256},{4,261},{5,262},{6,263},{7,260},{8... | collective-permute-start | bytes 688136 | tf_op jit(solution)/shard_map/enc_reduce/ppermute | solution.py:216
  8.4 14.8 %collective-permute-start.2 = (bf16[128,896]{1,0:T(8,128)(2,1)S(1)}, bf16[128,896]{1,0:T(8,128)(2,1)S(1)}, u32[]{:S(2)}, u32[]{:S(2)}) collective-permute-start(bf16[128,896]{1,0:T(8,128)(2,1)S(1)} %get-tuple-element.38), channel_id=1, source_target_pairs={{0,259},{1,256},{2,257},{3,258},{4,263},{5,260},{6,261},{7,262},{8... | collective-permute-start | bytes 688136 | tf_op jit(solution)/shard_map/enc_reduce/ppermute | solution.py:216
  9.7 13.5 %collective-permute-start.3 = (bf16[128,896]{1,0:T(8,128)(2,1)S(1)}, bf16[128,896]{1,0:T(8,128)(2,1)S(1)}, u32[]{:S(2)}, u32[]{:S(2)}) collective-permute-start(bf16[128,896]{1,0:T(8,128)(2,1)S(1)} %get-tuple-element.39), channel_id=1, source_target_pairs={{0,256},{1,257},{2,258},{3,259},{4,260},{5,261},{6,262},{7,263},{8... | collective-permute-start | bytes 688136 | tf_op jit(solution)/shard_map/enc_reduce/ppermute | solution.py:216
  23.8 10.7 %collective-permute-start.4 = (bf16[128,896]{1,0:T(8,128)(2,1)S(1)}, bf16[128,896]{1,0:T(8,128)(2,1)S(1)}, u32[]{:S(2)}, u32[]{:S(2)}) collective-permute-start(bf16[128,896]{1,0:T(8,128)(2,1)S(1)} %get-tuple-element.40.got0), channel_id=1, source_target_pairs={{256,257},{257,258},{258,259},{259,256},{260,261},{261,262},{262,2... | collective-permute-start | bytes 688136 | tf_op jit(solution)/shard_map/enc_gather/ppermute | solution.py:216
  26.2 11.5 %collective-permute-start.5 = (bf16[128,896]{1,0:T(8,128)(2,1)S(1)}, bf16[128,896]{1,0:T(8,128)(2,1)S(1)}, u32[]{:S(2)}, u32[]{:S(2)}) collective-permute-start(bf16[128,896]{1,0:T(8,128)(2,1)S(1)} %get-tuple-element.40.got0), channel_id=1, source_target_pairs={{256,258},{257,259},{258,256},{259,257},{260,262},{261,263},{262,2... | collective-permute-start | bytes 688136 | tf_op jit(solution)/shard_map/enc_gather/ppermute | solution.py:216
  31.3 8.9 %collective-permute-start.6 = (bf16[128,896]{1,0:T(8,128)(2,1)S(1)}, bf16[128,896]{1,0:T(8,128)(2,1)S(1)}, u32[]{:S(2)}, u32[]{:S(2)}) collective-permute-start(bf16[128,896]{1,0:T(8,128)(2,1)S(1)} %get-tuple-element.40.got0), channel_id=1, source_target_pairs={{256,259},{257,256},{258,257},{259,258},{260,263},{261,260},{262,2... | collective-permute-start | bytes 688136 | tf_op jit(solution)/shard_map/enc_gather/ppermute | solution.py:216
  42.0 1.3 %copy-start = (bf16[16,56,1024]{2,1,0:T(8,128)(2,1)}, bf16[16,56,1024]{2,1,0:T(8,128)(2,1)S(1)}, u32[]{:S(2)}) copy-start(bf16[16,56,1024]{2,1,0:T(8,128)(2,1)S(1)} %get-tuple-element.48) | copy-start | bytes 5505028
  44.1 22.2 %all-to-all-start = ((bf16[16,56,1024]{2,1,0:T(8,128)(2,1)}), bf16[16,56,1024]{2,1,0:T(8,128)(2,1)S(1)}, u32[]{:S(2)}, u32[]{:S(2)}) async-start(bf16[16,56,1024]{2,1,0:T(8,128)(2,1)} %copy-done), calls=%async_computation | async-start | bytes 3670016 | tf_op jit(solution)/shard_map/exchange/all_to_all | solution.py:304
  49.1 26.3 %collective-permute-start.8 = (bf16[128,896]{1,0:T(8,128)(2,1)S(1)}, bf16[128,896]{1,0:T(8,128)(2,1)S(1)}, u32[]{:S(2)}, u32[]{:S(2)}) collective-permute-start(bf16[128,896]{1,0:T(8,128)(2,1)S(1)} %get-tuple-element.50), channel_id=1, source_target_pairs={{256,0},{257,1},{258,2},{259,3},{260,4},{261,5},{262,6},{263,7},{2... | collective-permute-start | bytes 688136 | tf_op jit(solution)/shard_map/enc_out/ppermute | solution.py:283
  50.4 25.0 %collective-permute-start.10 = (bf16[128,896]{1,0:T(8,128)(2,1)S(1)}, bf16[128,896]{1,0:T(8,128)(2,1)S(1)}, u32[]{:S(2)}, u32[]{:S(2)}) collective-permute-start(bf16[128,896]{1,0:T(8,128)(2,1)S(1)} %get-tuple-element.52), channel_id=1, source_target_pairs={{256,257},{257,258},{258,259},{259,256},{260,261},{261,262},{262,2... | collective-permute-start | bytes 688136 | tf_op jit(solution)/shard_map/in_reduce/ppermute | solution.py:216
  54.2 21.2 %collective-permute-start.11 = (bf16[128,896]{1,0:T(8,128)(2,1)S(1)}, bf16[128,896]{1,0:T(8,128)(2,1)}, u32[]{:S(2)}, u32[]{:S(2)}) collective-permute-start(bf16[128,896]{1,0:T(8,128)(2,1)S(1)} %get-tuple-element.53), channel_id=1, source_target_pairs={{256,259},{257,256},{258,257},{259,258},{260,263},{261,260},{262,2... | collective-permute-start | bytes 688136 | tf_op jit(solution)/shard_map/in_reduce/ppermute | solution.py:216
  57.5 17.9 %collective-permute-start.9 = (bf16[128,896]{1,0:T(8,128)(2,1)S(1)}, bf16[128,896]{1,0:T(8,128)(2,1)}, u32[]{:S(2)}, u32[]{:S(2)}) collective-permute-start(bf16[128,896]{1,0:T(8,128)(2,1)S(1)} %get-tuple-element.51), channel_id=1, source_target_pairs={{256,258},{257,259},{258,256},{259,257},{260,262},{261,263},{262,2... | collective-permute-start | bytes 688136 | tf_op jit(solution)/shard_map/in_reduce/ppermute | solution.py:216
  66.6 11.1 %collective-permute-start.7 = (bf16[32,1024]{1,0:T(8,128)(2,1)S(1)}, bf16[32,1024]{1,0:T(8,128)(2,1)S(1)}, u32[]{:S(2)}, u32[]{:S(2)}) collective-permute-start(bf16[32,1024]{1,0:T(8,128)(2,1)S(1)} %get-tuple-element.49), channel_id=1, source_target_pairs={{0,16},{16,0},{32,48},{48,32},{1,17},{17,1},{33,49},{49,33},{2,18}... | collective-permute-start | bytes 196616 | tf_op jit(solution)/shard_map/zh_first/ppermute | solution.py:311
  77.8 10.3 %collective-permute-start.12 = (bf16[16,1024]{1,0:T(8,128)(2,1)S(1)}, bf16[16,1024]{1,0:T(8,128)(2,1)S(1)}, u32[]{:S(2)}, u32[]{:S(2)}) collective-permute-start(bf16[16,1024]{1,0:T(8,128)(2,1)S(1)} %get-tuple-element.59), channel_id=1, source_target_pairs={{0,48},{48,0},{16,32},{32,16},{1,49},{49,1},{17,33},{33,17},{2,50}... | collective-permute-start | bytes 98312 | tf_op jit(solution)/shard_map/zh_second/ppermute | solution.py:315

commit v8 on v6

--- a/solution.py
+++ b/solution.py
@@ -11,6 +11,7 @@
 NEIGH = 128
 BLOCKS = 4
 N_MP = 4
+EARLY = (0, 2, 3)
 OUTER = (0, 3)
 INNER = (1, 2)
 SIDE = 4
@@ -126,21 +127,46 @@
         ordered_ref[...] = mm(share, places(order_ref)).astype(BF16)
 
 
-def encoder_kernel(sec_ref, mp_ref, ordered_ref, weight_ref, down_ref, hidden_ref, slope_ref, got0, got1, got2, got3, keep_ref,
-                   partial_ref, part0, part1, part2, part3, pre_grad_ref, arrived_ref, part_ref):
-    del keep_ref
+def early_kernel(sec_ref, mp_ref, ordered_ref, down_ref, hidden_ref, slope_ref, got0, got1, got2, sum_ref, pre_grad_ref):
     @on_section(sec_ref, 1)
     def work():
         half = hidden_ref.shape[1]
-        for step, got in enumerate((got0, got3, got2, got1)):
-            arrived_ref[block_rows(lax.rem(mp_ref[0] + step, N_MP)), :] = got[...]
-        arrived = arrived_ref[...]
-        store_chunks(partial_ref, mm(arrived, hidden_ref[...], TN), half)
-        pre_grad_ref[...] = (mm(arrived, down_ref[...]) * slope_ref[...]).astype(BF16)
-        store_chunks(partial_ref, mm(ordered_ref[...], pre_grad_ref[...], TN))
+        blocks = [block_rows(lax.rem(mp_ref[0] + step, N_MP)) for step in EARLY]
+
+        def pick(ref):
+            return jnp.concatenate([ref[rows, :] for rows in blocks], axis=0)
+
+        arrived = jnp.concatenate([got0[...], got2[...], got1[...]], axis=0)
+        sum_ref[:, half:] = mm(arrived, pick(hidden_ref), TN)
+        pre_grad = (mm(arrived, down_ref[...]) * pick(slope_ref)).astype(BF16)
+        sum_ref[:, :half] = mm(pick(ordered_ref), pre_grad, TN)
+        pre_grad_ref[...] = pre_grad
+
+
+def late_kernel(sec_ref, mp_ref, ordered_ref, weight_ref, down_ref, hidden_ref, slope_ref, got3, sum_ref, early_ref,
+                keep_ref, partial_ref, part0, part1, part2, part3, pre_grad_ref, part_ref, stage0, stage1, sems):
+    del keep_ref
+    @on_section(sec_ref, 1)
+    def work():
+        half = hidden_ref.shape[1]
+        rows = block_rows(lax.rem(mp_ref[0] + 1, N_MP))
+        arrived = got3[...]
+        store_chunks(stage1, sum_ref[:, half:] + mm(arrived, hidden_ref[rows, :], TN))
+        copy1 = pltpu.make_async_copy(stage1, partial_ref.at[:, :, pl.ds(half, half)], sems.at[1])
+        copy1.start()
+        pre_grad = (mm(arrived, down_ref[...]) * slope_ref[rows, :]).astype(BF16)
+        store_chunks(stage0, sum_ref[:, :half] + mm(ordered_ref[rows, :], pre_grad, TN))
+        copy0 = pltpu.make_async_copy(stage0, partial_ref.at[:, :, pl.ds(0, half)], sems.at[0])
+        copy0.start()
+        pre_grad_ref[rows, :] = pre_grad
+        for index, step in enumerate(EARLY):
+            block = block_rows(lax.rem(mp_ref[0] + step, N_MP))
+            pre_grad_ref[block, :] = early_ref[index * NEIGH:(index + 1) * NEIGH, :]
         part_ref[...] = mm(pre_grad_ref[...], weight_ref[:, :half], NT).astype(BF16)
         for step, part in enumerate((part0, part1, part2, part3)):
             part[...] = part_ref[block_rows(lax.rem(mp_ref[0] + step, N_MP)), :]
+        copy1.wait()
+        copy0.wait()
 
 
 def sum_kernel(zh_ref, piece_ref, keep_ref, send_ref, total_ref):
@@ -177,6 +203,13 @@
     send_ref[...] = jnp.where(upper, lower_block, upper_block).astype(BF16)
 
 
+def last_kernel(own_ref, came_ref, out_ref):
+    share, half = out_ref.shape[1], out_ref.shape[3]
+    total = (own_ref[...] + came_ref[...].astype(F32)) * (1.0 / (SIDE * SIDE * SIDE))
+    for column in range(2):
+        out_ref[0, :, column, :] = total[:share, column * half:(column + 1) * half]
+
+
 def vmem():
     return pl.BlockSpec(memory_space=pltpu.VMEM)
 
@@ -185,12 +218,13 @@
     return pl.BlockSpec(memory_space=pltpu.SMEM)
 
 
-def call(kernel, outs, args, scalars=0, scratch=(), flops=0, alias=None):
+def call(kernel, outs, args, scalars=0, scratch=(), flops=0, alias=None, far_in=None, far_out=None):
+    far = pl.BlockSpec(memory_space=pl.ANY)
     return pl.pallas_call(
         kernel,
         out_shape=[jax.ShapeDtypeStruct(shape, kind) for shape, kind in outs],
-        in_specs=[smem()] * scalars + [vmem()] * (len(args) - scalars),
-        out_specs=[vmem()] * len(outs),
+        in_specs=[smem() if i < scalars else far if i == far_in else vmem() for i in range(len(args))],
+        out_specs=[far if i == far_out else vmem() for i in range(len(outs))],
         scratch_shapes=list(scratch),
         input_output_aliases=alias or {},
         compiler_params=pltpu.CompilerParams(vmem_limit_bytes=VMEM_LIMIT),
@@ -269,14 +303,24 @@
     with jax.named_scope("enc_out"):
         enc_share = lax.ppermute(enc_share, "sec", [(1, 0)])
 
+    sums, early = call(
+        early_kernel,
+        [((width, 2 * half), F32), ((3 * quarter, half), BF16)],
+        (sec, mp, ordered_rows, down, hidden, slope, *got[:3]),
+        scalars=2,
+        flops=3 * cols_flops,
+    )
+    stage = pltpu.VMEM((pieces, chunk, half), BF16)
     partial, *in_parts = call(
-        encoder_kernel,
+        late_kernel,
         [piece_out] + part_outs,
-        (sec, mp, ordered_rows, weights, down, hidden, slope, *got, partial),
+        (sec, mp, ordered_rows, weights, down, hidden, slope, got[3], sums, early, partial),
         scalars=2,
-        scratch=[pltpu.VMEM((local_rows, half), BF16), part_scratch, part_scratch],
-        flops=4 * cols_flops,
-        alias={11: 0},
+        scratch=[pltpu.VMEM((local_rows, half), BF16), part_scratch, stage, stage, pltpu.SemaphoreType.DMA((2,))],
+        flops=2 * cols_flops,
+        alias={10: 0},
+        far_in=10,
+        far_out=0,
     )
     with jax.named_scope("exchange"):
         partial = lax.all_to_all(partial, ("x", "y"), 0, 0, tiled=True)
@@ -287,12 +331,12 @@
     keep, send = call(sum_kernel, [(pair_shape, F32), (pair_shape, BF16)], (zh, partial), scalars=1, scratch=[sum_scratch])
     with jax.named_scope("zh_first"):
         came = lax.ppermute(send, "zh", [(0, 1), (1, 0), (2, 3), (3, 2)])
+    came, row_part = lax.optimization_barrier((came, jnp.where(is_decoder, enc_share, in_share)[None]))
     own, send = call(halve_kernel, [(block_shape, F32), (block_shape, BF16)], (zh, keep, came), scalars=1)
     with jax.named_scope("zh_second"):
         came = lax.ppermute(send, "zh", [(0, 3), (3, 0), (1, 2), (2, 1)])
-    total = own + came.astype(F32)
-    weight_part = (total[:share] / (SIDE * SIDE * SIDE)).reshape(1, share, 2, half)
-    return (jnp.where(is_decoder, enc_share, in_share)[None], weight_part)
+    (weight_part,) = call(last_kernel, [((1, share, 2, half), F32)], (own, came))
+    return (row_part, weight_part)
 
 
 def solution(mesh):

time: 89.8 us -> 89.1 us (level)
  waiting for transfers between devices: 27 us -> 24 us
  Pallas kernels: 7.18 us -> 9.3 us
  starting transfers between devices: 48 us -> 48.9 us
    pallas_call x6 -> x8, Pallas kernels: 7.18 us -> 9.3 us  [call(): pl.pallas_call(kernel, out_shape=[jax.ShapeDtypeStruct(shape, kind) for s...]
    ppermute x10, waiting for transfers between devices: 18 us -> 16.2 us  [mp_move(): return lax.ppermute(value, ('sec', 'mp'), pairs)]
    ppermute x1, waiting for transfers between devices: 2.34 us -> 0.64 us  [shards(): came = lax.ppermute(send, 'zh', [(0, 1), (1, 0), (2, 3), (3, 2)])]
    ppermute x1, waiting for transfers between devices: 0.01 us -> 1.29 us  [shards(): came = lax.ppermute(send, 'zh', [(0, 3), (3, 0), (1, 2), (2, 1)])]
    all_to_all x1, starting transfers between devices: 5 us -> 5.91 us  [shards(): partial = lax.all_to_all(partial, ('x', 'y'), 0, 0, tiled=True)]
  transfers between devices with their start and end apart: 14 -> 14, of which waited for: 6 -> 7; matrix products, arithmetic and copies ran while one was open for 2% -> 2% of each run, Pallas kernels for 2% -> 3%
where the time goes in v8:
time: 89.1 us; the launch traced here: 88.6 us
  starting transfers between devices  48.9 us (55%)
  waiting for transfers between devices  24 us (27%)
  Pallas kernels  9.3 us (10%)
  local copies, waits for them, and re-layouts  3.5 us (4%)
  other arithmetic  1.9 us (2%)
  between operations  0.96 us (1%)
    ppermute x10, starting transfers between devices, mp_move(): return lax.ppermute(value, ('sec', 'mp'), pairs)  24.6 us
    ppermute x10, waiting for transfers between devices, mp_move(): return lax.ppermute(value, ('sec', 'mp'), pairs)  16.2 us
    pallas_call x8, Pallas kernels, call(): pl.pallas_call(kernel, out_shape=[jax.ShapeDtypeStruct(shape, kind) for s...  9.3 us
    ppermute x1, starting transfers between devices, shards(): came = lax.ppermute(send, 'zh', [(0, 1), (1, 0), (2, 3), (3, 2)])  8.8 us
    ppermute x1, starting transfers between devices, shards(): came = lax.ppermute(send, 'zh', [(0, 3), (3, 0), (1, 2), (2, 1)])  8.33 us
    all_to_all x1, starting transfers between devices, shards(): partial = lax.all_to_all(partial, ('x', 'y'), 0, 0, tiled=True)  5.91 us
    all_to_all x1, waiting for transfers between devices, shards(): partial = lax.all_to_all(partial, ('x', 'y'), 0, 0, tiled=True)  5.87 us
    unnamed x15, local copies, waits for them, and re-layouts  3.35 us
  transfers between devices with their start and end apart: 14, of which 7 were waited for; matrix products, arithmetic and copies ran while one was open for 2% of the time, Pallas kernels for 3%

profile of v8, /device:TPU:1, one launch (start us, length us, event | category | flops | bytes accessed | tf_op | source)
XLA Modules:
  0.0 88.6 jit_solution(17847437001206920189)
XLA Ops:
  0.7 0.0 copy-start.1
  0.7 0.0 copy-start.2
  0.7 0.0 copy-start.3
  0.7 0.0 copy-start.4
  0.7 0.0 copy-start.5
  0.7 0.0 copy-start.6
  0.7 2.1 %copy.10 = bf16[112,8,2,512]{3,1,2,0:T(8,128)(2,1)S(1)} copy(bf16[112,8,2,512]{3,2,1,0:T(2,128)(2,1)} %bitcast.14) | data formatting | bytes 3670016
  2.8 0.1 reshape.138.order_ref
  3.0 0.0 copy-done.1
  3.0 0.0 copy-done.2
  3.0 0.0 copy-done.3
  3.0 2.8 %shard_map.86 = (bf16[512,1024]{1,0:T(8,128)(2,1)S(1)}, bf16[128,896]{1,0:T(8,128)(2,1)S(1)}, bf16[128,896]{1,0:T(8,128)(2,1)S(1)}, bf16[128,896]{1,0:T(8,128)(2...) custom-call(s32[1]{0:T(128)} %bitcast.1.sec_ref, ...), custom_call_target="tpu_custom_call" | custom-call | flops 1879048192 | bytes 4194304 | tf_op jit(solution)/shard_map/pallas_call | solution.py:223
  5.8 1.3 %collective-permute-start = (bf16[128,896]{1,0:T(8,128)(2,1)S(1)}, bf16[128,896]{1,0:T(8,128)(2,1)S(1)}, u32[]{:S(2)}, u32[]{:S(2)}) collective-permute-start(bf16[128,896]{1,0:T(8,128)(2,1)S(1)} %get-tuple-element.32), channel_id=1, source_target_pairs={{0,258},{1,259},{2,256},{3,257},{4,262},{5,263},{6,260},{7,261},{8... | collective-permute-start | bytes 688136 | tf_op jit(solution)/shard_map/enc_reduce/ppermute | solution.py:237
  7.1 1.3 %collective-permute-start.1 = (bf16[128,896]{1,0:T(8,128)(2,1)S(1)}, bf16[128,896]{1,0:T(8,128)(2,1)S(1)}, u32[]{:S(2)}, u32[]{:S(2)}) collective-permute-start(bf16[128,896]{1,0:T(8,128)(2,1)S(1)} %get-tuple-element.33), channel_id=1, source_target_pairs={{0,257},{1,258},{2,259},{3,256},{4,261},{5,262},{6,263},{7,260},{8... | collective-permute-start | bytes 688136 | tf_op jit(solution)/shard_map/enc_reduce/ppermute | solution.py:237
  8.4 1.3 %collective-permute-start.2 = (bf16[128,896]{1,0:T(8,128)(2,1)S(1)}, bf16[128,896]{1,0:T(8,128)(2,1)S(1)}, u32[]{:S(2)}, u32[]{:S(2)}) collective-permute-start(bf16[128,896]{1,0:T(8,128)(2,1)S(1)} %get-tuple-element.34), channel_id=1, source_target_pairs={{0,259},{1,256},{2,257},{3,258},{4,263},{5,260},{6,261},{7,262},{8... | collective-permute-start | bytes 688136 | tf_op jit(solution)/shard_map/enc_reduce/ppermute | solution.py:237
  9.7 1.3 %collective-permute-start.3 = (bf16[128,896]{1,0:T(8,128)(2,1)S(1)}, bf16[128,896]{1,0:T(8,128)(2,1)S(1)}, u32[]{:S(2)}, u32[]{:S(2)}) collective-permute-start(bf16[128,896]{1,0:T(8,128)(2,1)S(1)} %get-tuple-element.35), channel_id=1, source_target_pairs={{0,256},{1,257},{2,258},{3,259},{4,260},{5,261},{6,262},{7,263},{8... | collective-permute-start | bytes 688136 | tf_op jit(solution)/shard_map/enc_reduce/ppermute | solution.py:237
  11.0 10.1 %collective-permute-done.got0 = bf16[128,896]{1,0:T(8,128)(2,1)S(1)} collective-permute-done((bf16[128,896]{1,0:T(8,128)(2,1)S(1)}, bf16[128,896]{1,0:T(8,128)(2,1)S(1)}, u32[]{:S(2)}, u32[]{:S(2)}) %collective-permute-start) | collective-permute-done | bytes 229408 | tf_op jit(solution)/shard_map/enc_reduce/ppermute | solution.py:237
  21.1 0.0 collective-permute-done.1.got1
  21.1 2.1 %collective-permute-done.2.got2 = bf16[128,896]{1,0:T(8,128)(2,1)S(1)} collective-permute-done((bf16[128,896]{1,0:T(8,128)(2,1)S(1)}, bf16[128,896]{1,0:T(8,128)(2,1)S(1)}, u32[]{:S(2)}, u32[]{:S(2)}) %collective-permute-start.2) | collective-permute-done | bytes 229408 | tf_op jit(solution)/shard_map/enc_reduce/ppermute | solution.py:237
  23.2 0.0 collective-permute-done.3.got3
  23.3 0.5 shard_map.88
  23.8 2.5 %collective-permute-start.5 = (bf16[128,896]{1,0:T(8,128)(2,1)S(1)}, bf16[128,896]{1,0:T(8,128)(2,1)S(1)}, u32[]{:S(2)}, u32[]{:S(2)}) collective-permute-start(bf16[128,896]{1,0:T(8,128)(2,1)S(1)} %get-tuple-element.36.got0), channel_id=1, source_target_pairs={{256,257},{257,258},{258,259},{259,256},{260,261},{261,262},{262,2... | collective-permute-start | bytes 688136 | tf_op jit(solution)/shard_map/enc_gather/ppermute | solution.py:237
  26.2 5.1 %collective-permute-start.6 = (bf16[128,896]{1,0:T(8,128)(2,1)S(1)}, bf16[128,896]{1,0:T(8,128)(2,1)S(1)}, u32[]{:S(2)}, u32[]{:S(2)}) collective-permute-start(bf16[128,896]{1,0:T(8,128)(2,1)S(1)} %get-tuple-element.36.got0), channel_id=1, source_target_pairs={{256,258},{257,259},{258,256},{259,257},{260,262},{261,263},{262,2... | collective-permute-start | bytes 688136 | tf_op jit(solution)/shard_map/enc_gather/ppermute | solution.py:237
  31.3 1.9 %collective-permute-start.4 = (bf16[128,896]{1,0:T(8,128)(2,1)S(1)}, bf16[128,896]{1,0:T(8,128)(2,1)S(1)}, u32[]{:S(2)}, u32[]{:S(2)}) collective-permute-start(bf16[128,896]{1,0:T(8,128)(2,1)S(1)} %get-tuple-element.36.got0), channel_id=1, source_target_pairs={{256,259},{257,256},{258,257},{259,258},{260,263},{261,260},{262,2... | collective-permute-start | bytes 688136 | tf_op jit(solution)/shard_map/enc_gather/ppermute | solution.py:237
  33.3 1.2 %shard_map.87 = (bf16[16,56,1024]{2,1,0:T(8,128)(2,1)S(1)}, bf16[896,512]{1,0:T(8,128)(2,1)S(1)}) custom-call(s32[1]{0:T(128)} %bitcast.1.sec_ref, bf16[512,896]{1,0:T(8,128)(2,1)S(1)} %bitcast.13, bf16[896,1024]{1,0:T(8,128)(2,1)S(1)} %bitcast.10, bf16[512,1024]{1,0:T(8,128)(2,1)S(1)} %get-tuple-element.28.kv_grad_ref, s32[1,896]{1,0:T(1,128)S(1)} %reshape.138.order_ref), custom_call_target="tpu_custom_call" | custom-call | flops 2818572288 | bytes 4194304 | tf_op jit(solution)/shard_map/pallas_call | solution.py:223
  34.4 0.0 collective-permute-done.5.got1
  34.4 3.3 %collective-permute-done.6.got2 = bf16[128,896]{1,0:T(8,128)(2,1)S(1)} collective-permute-done((bf16[128,896]{1,0:T(8,128)(2,1)S(1)}, bf16[128,896]{1,0:T(8,128)(2,1)S(1)}, u32[]{:S(2)}, u32[]{:S(2)}) %collective-permute-start.6) | collective-permute-done | bytes 229408 | tf_op jit(solution)/shard_map/enc_gather/ppermute | solution.py:237
  37.8 1.7 %shard_map.89 = (f32[896,1024]{1,0:T(8,128)S(1)}, bf16[384,512]{1,0:T(8,128)(2,1)S(1)}) custom-call(s32[1]{0:T(128)} %bitcast.1.sec_ref, s32[1]{0:T(128)} %bitcast.2.mp_ref, bf16[512,896]{1,0:T(8,128)(2,1)S(1)} %get-tuple-element.27.ordered_ref, bf16[896,512]{1,0:T(8,128)(2,1)S(1)} %get-tuple-element.29.down_ref, ...), custom_call_target="tpu_custom_call" | custom-call | flops 1409286144 | bytes 4194304 | tf_op jit(solution)/shard_map/pallas_call | solution.py:223
  39.4 0.7 collective-permute-done.4.got3
  40.1 2.2 %shard_map.90 = (bf16[16,56,1024]{2,1,0:T(8,128)(2,1)S(1)}, bf16[128,896]{1,0:T(8,128)(2,1)S(1)}, bf16[128,896]{1,0:T(8,128)(2,1)S(1)}, bf16[128,896]{1,0:T(8,128)(2,1)S(1)}, bf16[128,896]{1,0:T(8,128)(2,1)S(1)}) custom-call(s32[1]{0:T(128)} %bitcast.1.sec_ref, s32[1]{0:T(128)} %bitcast.2.mp_ref, ...), custom_call_target="tpu_custom_call", output_to_operand_aliasing={{0}: (10, {})} | custom-call | flops 939524096 | bytes 4194304 | tf_op jit(solution)/shard_map/pallas_call | solution.py:223
  42.4 1.2 %copy-done = bf16[16,56,1024]{2,1,0:T(8,128)(2,1)} copy-done((bf16[16,56,1024]{2,1,0:T(8,128)(2,1)}, bf16[16,56,1024]{2,1,0:T(8,128)(2,1)S(1)}, u32[]{:S(2)}) %copy-start) | copy-done | bytes 1835032
  43.6 5.9 %all-to-all-start = ((bf16[16,56,1024]{2,1,0:T(8,128)(2,1)}), bf16[16,56,1024]{2,1,0:T(8,128)(2,1)S(1)}, u32[]{:S(2)}, u32[]{:S(2)}) async-start(bf16[16,56,1024]{2,1,0:T(8,128)(2,1)} %copy-done), calls=%async_computation | async-start | bytes 3670016 | tf_op jit(solution)/shard_map/exchange/all_to_all | solution.py:326
  49.5 1.3 %collective-permute-start.8 = (bf16[128,896]{1,0:T(8,128)(2,1)S(1)}, bf16[128,896]{1,0:T(8,128)(2,1)S(1)}, u32[]{:S(2)}, u32[]{:S(2)}) collective-permute-start(bf16[128,896]{1,0:T(8,128)(2,1)S(1)} %get-tuple-element.42), channel_id=1, source_target_pairs={{256,0},{257,1},{258,2},{259,3},{260,4},{261,5},{262,6},{263,7},{2... | collective-permute-start | bytes 688136 | tf_op jit(solution)/shard_map/enc_out/ppermute | solution.py:304
  50.8 3.1 %collective-permute-start.10 = (bf16[128,896]{1,0:T(8,128)(2,1)S(1)}, bf16[128,896]{1,0:T(8,128)(2,1)S(1)}, u32[]{:S(2)}, u32[]{:S(2)}) collective-permute-start(bf16[128,896]{1,0:T(8,128)(2,1)S(1)} %get-tuple-element.44), channel_id=1, source_target_pairs={{256,257},{257,258},{258,259},{259,256},{260,261},{261,262},{262,2... | collective-permute-start | bytes 688136 | tf_op jit(solution)/shard_map/in_reduce/ppermute | solution.py:237
  53.9 4.7 %collective-permute-start.11 = (bf16[128,896]{1,0:T(8,128)(2,1)S(1)}, bf16[128,896]{1,0:T(8,128)(2,1)}, u32[]{:S(2)}, u32[]{:S(2)}) collective-permute-start(bf16[128,896]{1,0:T(8,128)(2,1)S(1)} %get-tuple-element.45), channel_id=1, source_target_pairs={{256,259},{257,256},{258,257},{259,258},{260,263},{261,260},{262,2... | collective-permute-start | bytes 688136 | tf_op jit(solution)/shard_map/in_reduce/ppermute | solution.py:237
  58.6 2.2 %collective-permute-start.9 = (bf16[128,896]{1,0:T(8,128)(2,1)S(1)}, bf16[128,896]{1,0:T(8,128)(2,1)}, u32[]{:S(2)}, u32[]{:S(2)}) collective-permute-start(bf16[128,896]{1,0:T(8,128)(2,1)S(1)} %get-tuple-element.43), channel_id=1, source_target_pairs={{256,258},{257,259},{258,256},{259,257},{260,262},{261,263},{262,2... | collective-permute-start | bytes 688136 | tf_op jit(solution)/shard_map/in_reduce/ppermute | solution.py:237
  60.8 5.9 %all-to-all-done.piece_ref = bf16[16,56,1024]{2,1,0:T(8,128)(2,1)S(1)} async-done(((bf16[16,56,1024]{2,1,0:T(8,128)(2,1)}), bf16[16,56,1024]{2,1,0:T(8,128)(2,1)S(1)}, u32[]{:S(2)}, u32[]{:S(2)}) %all-to-all-start) | async-done | bytes 1835040 | tf_op jit(solution)/shard_map/exchange/all_to_all | solution.py:326
  66.7 0.3 shard_map.91
  67.0 8.8 %collective-permute-start.7 = (bf16[32,1024]{1,0:T(8,128)(2,1)S(1)}, bf16[32,1024]{1,0:T(8,128)(2,1)S(1)}, u32[]{:S(2)}, u32[]{:S(2)}) collective-permute-start(bf16[32,1024]{1,0:T(8,128)(2,1)S(1)} %get-tuple-element.41), channel_id=1, source_target_pairs={{0,16},{16,0},{32,48},{48,32},{1,17},{17,1},{33,49},{49,33},{2,18}... | collective-permute-start | bytes 196616 | tf_op jit(solution)/shard_map/zh_first/ppermute | solution.py:333
  75.8 0.0 collective-permute-done.8
  75.8 0.0 collective-permute-done.10
  75.8 0.0 collective-permute-done.11
  75.8 0.0 collective-permute-done.9
  75.8 1.9 %fusion.1 = bf16[1,128,896]{2,1,0:T(8,128)(2,1)} fusion(bf16[128,896]{1,0:T(8,128)(2,1)S(1)} %collective-permute-done.8, bf16[128,896]{1,0:T(8,128)(2,1)S(1)} %get-tuple-element.46, bf16[128,896]{1,0:T(8,128)(2,1)} %collective-permute-done.11, bf16[128,896]{1,0:T(8,128)(2,1)S(1)} %collective-permute-done.10, bf16[128,896]{1,0:T(8,128)(2,1)} %collective-permute-done.9, ...), kind=kLoop, calls=%fused_computation.2 | loop fusion | flops 1032192 | bytes 1376257 | tf_op jit(solution)/shard_map/broadcast_in_dim | solution.py:334
  77.7 0.6 collective-permute-done.7.came_ref
  78.4 8.3 %collective-permute-start.12 = (bf16[16,1024]{1,0:T(8,128)(2,1)S(1)}, bf16[16,1024]{1,0:T(8,128)(2,1)S(1)}, u32[]{:S(2)}, u32[]{:S(2)}) collective-permute-start(bf16[16,1024]{1,0:T(8,128)(2,1)S(1)} %get-tuple-element.51), channel_id=1, source_target_pairs={{0,48},{48,0},{16,32},{32,16},{1,49},{49,1},{17,33},{33,17},{2,50}... | collective-permute-start | bytes 98312 | tf_op jit(solution)/shard_map/zh_second/ppermute | solution.py:337
  86.7 1.3 %collective-permute-done.12.came_ref = bf16[16,1024]{1,0:T(8,128)(2,1)S(1)} collective-permute-done((bf16[16,1024]{1,0:T(8,128)(2,1)S(1)}, bf16[16,1024]{1,0:T(8,128)(2,1)S(1)}, u32[]{:S(2)}, u32[]{:S(2)}) %collective-permute-start.12) | collective-permute-done | bytes 32800 | tf_op jit(solution)/shard_map/zh_second/ppermute | solution.py:337
  88.0 0.6 shard_map.93
  (6 shorter events, 0.0 us)
Async XLA Ops:
  0.7 2.3 %copy-start.1 = (bf16[1,512,896]{2,1,0:T(8,128)(2,1)S(1)}, bf16[1,512,896]{2,1,0:T(8,128)(2,1)}, u32[]{:S(2)}) copy-start(bf16[1,512,896]{2,1,0:T(8,128)(2,1)} %param.7) | copy-start | bytes 2752516
  0.7 2.3 %copy-start.2 = (bf16[128,512]{1,0:T(8,128)(2,1)S(1)}, bf16[128,512]{1,0:T(8,128)(2,1)}, u32[]{:S(2)}) copy-start(bf16[128,512]{1,0:T(8,128)(2,1)} %query_ref.1) | copy-start | bytes 393220
  0.7 2.3 %copy-start.3 = (bf16[128,512]{1,0:T(8,128)(2,1)S(1)}, bf16[128,512]{1,0:T(8,128)(2,1)}, u32[]{:S(2)}) copy-start(bf16[128,512]{1,0:T(8,128)(2,1)} %grad_ref.1) | copy-start | bytes 393220
  0.7 2.3 %copy-start.4 = (f32[4,128]{1,0:T(4,128)S(1)}, f32[4,128]{1,0:T(4,128)}, u32[]{:S(2)}) copy-start(f32[4,128]{1,0:T(4,128)} %lse_ref.1) | copy-start | bytes 6148
  0.7 2.3 %copy-start.5 = (f32[4,128]{1,0:T(4,128)S(1)}, f32[4,128]{1,0:T(4,128)}, u32[]{:S(2)}) copy-start(f32[4,128]{1,0:T(4,128)} %delta_ref.1) | copy-start | bytes 6148
  0.7 2.3 %copy-start.6 = (s32[2,2]{1,0:T(2,128)S(1)}, s32[2,2]{1,0:T(2,128)}, u32[]{:S(2)}) copy-start(s32[2,2]{1,0:T(2,128)} %span_ref.1) | copy-start | bytes 52
  5.8 15.3 %collective-permute-start = (bf16[128,896]{1,0:T(8,128)(2,1)S(1)}, bf16[128,896]{1,0:T(8,128)(2,1)S(1)}, u32[]{:S(2)}, u32[]{:S(2)}) collective-permute-start(bf16[128,896]{1,0:T(8,128)(2,1)S(1)} %get-tuple-element.32), channel_id=1, source_target_pairs={{0,258},{1,259},{2,256},{3,257},{4,262},{5,263},{6,260},{7,261},{8... | collective-permute-start | bytes 688136 | tf_op jit(solution)/shard_map/enc_reduce/ppermute | solution.py:237
  7.1 14.0 %collective-permute-start.1 = (bf16[128,896]{1,0:T(8,128)(2,1)S(1)}, bf16[128,896]{1,0:T(8,128)(2,1)S(1)}, u32[]{:S(2)}, u32[]{:S(2)}) collective-permute-start(bf16[128,896]{1,0:T(8,128)(2,1)S(1)} %get-tuple-element.33), channel_id=1, source_target_pairs={{0,257},{1,258},{2,259},{3,256},{4,261},{5,262},{6,263},{7,260},{8... | collective-permute-start | bytes 688136 | tf_op jit(solution)/shard_map/enc_reduce/ppermute | solution.py:237
  8.4 14.8 %collective-permute-start.2 = (bf16[128,896]{1,0:T(8,128)(2,1)S(1)}, bf16[128,896]{1,0:T(8,128)(2,1)S(1)}, u32[]{:S(2)}, u32[]{:S(2)}) collective-permute-start(bf16[128,896]{1,0:T(8,128)(2,1)S(1)} %get-tuple-element.34), channel_id=1, source_target_pairs={{0,259},{1,256},{2,257},{3,258},{4,263},{5,260},{6,261},{7,262},{8... | collective-permute-start | bytes 688136 | tf_op jit(solution)/shard_map/enc_reduce/ppermute | solution.py:237
  9.7 13.5 %collective-permute-start.3 = (bf16[128,896]{1,0:T(8,128)(2,1)S(1)}, bf16[128,896]{1,0:T(8,128)(2,1)S(1)}, u32[]{:S(2)}, u32[]{:S(2)}) collective-permute-start(bf16[128,896]{1,0:T(8,128)(2,1)S(1)} %get-tuple-element.35), channel_id=1, source_target_pairs={{0,256},{1,257},{2,258},{3,259},{4,260},{5,261},{6,262},{7,263},{8... | collective-permute-start | bytes 688136 | tf_op jit(solution)/shard_map/enc_reduce/ppermute | solution.py:237
  23.8 10.7 %collective-permute-start.5 = (bf16[128,896]{1,0:T(8,128)(2,1)S(1)}, bf16[128,896]{1,0:T(8,128)(2,1)S(1)}, u32[]{:S(2)}, u32[]{:S(2)}) collective-permute-start(bf16[128,896]{1,0:T(8,128)(2,1)S(1)} %get-tuple-element.36.got0), channel_id=1, source_target_pairs={{256,257},{257,258},{258,259},{259,256},{260,261},{261,262},{262,2... | collective-permute-start | bytes 688136 | tf_op jit(solution)/shard_map/enc_gather/ppermute | solution.py:237
  26.2 11.5 %collective-permute-start.6 = (bf16[128,896]{1,0:T(8,128)(2,1)S(1)}, bf16[128,896]{1,0:T(8,128)(2,1)S(1)}, u32[]{:S(2)}, u32[]{:S(2)}) collective-permute-start(bf16[128,896]{1,0:T(8,128)(2,1)S(1)} %get-tuple-element.36.got0), channel_id=1, source_target_pairs={{256,258},{257,259},{258,256},{259,257},{260,262},{261,263},{262,2... | collective-permute-start | bytes 688136 | tf_op jit(solution)/shard_map/enc_gather/ppermute | solution.py:237
  31.3 8.8 %collective-permute-start.4 = (bf16[128,896]{1,0:T(8,128)(2,1)S(1)}, bf16[128,896]{1,0:T(8,128)(2,1)S(1)}, u32[]{:S(2)}, u32[]{:S(2)}) collective-permute-start(bf16[128,896]{1,0:T(8,128)(2,1)S(1)} %get-tuple-element.36.got0), channel_id=1, source_target_pairs={{256,259},{257,256},{258,257},{259,258},{260,263},{261,260},{262,2... | collective-permute-start | bytes 688136 | tf_op jit(solution)/shard_map/enc_gather/ppermute | solution.py:237
  42.3 1.3 %copy-start = (bf16[16,56,1024]{2,1,0:T(8,128)(2,1)}, bf16[16,56,1024]{2,1,0:T(8,128)(2,1)S(1)}, u32[]{:S(2)}) copy-start(bf16[16,56,1024]{2,1,0:T(8,128)(2,1)S(1)} %get-tuple-element.40) | copy-start | bytes 5505028
  43.6 23.1 %all-to-all-start = ((bf16[16,56,1024]{2,1,0:T(8,128)(2,1)}), bf16[16,56,1024]{2,1,0:T(8,128)(2,1)S(1)}, u32[]{:S(2)}, u32[]{:S(2)}) async-start(bf16[16,56,1024]{2,1,0:T(8,128)(2,1)} %copy-done), calls=%async_computation | async-start | bytes 3670016 | tf_op jit(solution)/shard_map/exchange/all_to_all | solution.py:326
  49.5 26.3 %collective-permute-start.8 = (bf16[128,896]{1,0:T(8,128)(2,1)S(1)}, bf16[128,896]{1,0:T(8,128)(2,1)S(1)}, u32[]{:S(2)}, u32[]{:S(2)}) collective-permute-start(bf16[128,896]{1,0:T(8,128)(2,1)S(1)} %get-tuple-element.42), channel_id=1, source_target_pairs={{256,0},{257,1},{258,2},{259,3},{260,4},{261,5},{262,6},{263,7},{2... | collective-permute-start | bytes 688136 | tf_op jit(solution)/shard_map/enc_out/ppermute | solution.py:304
  50.8 25.0 %collective-permute-start.10 = (bf16[128,896]{1,0:T(8,128)(2,1)S(1)}, bf16[128,896]{1,0:T(8,128)(2,1)S(1)}, u32[]{:S(2)}, u32[]{:S(2)}) collective-permute-start(bf16[128,896]{1,0:T(8,128)(2,1)S(1)} %get-tuple-element.44), channel_id=1, source_target_pairs={{256,257},{257,258},{258,259},{259,256},{260,261},{261,262},{262,2... | collective-permute-start | bytes 688136 | tf_op jit(solution)/shard_map/in_reduce/ppermute | solution.py:237
  53.9 21.9 %collective-permute-start.11 = (bf16[128,896]{1,0:T(8,128)(2,1)S(1)}, bf16[128,896]{1,0:T(8,128)(2,1)}, u32[]{:S(2)}, u32[]{:S(2)}) collective-permute-start(bf16[128,896]{1,0:T(8,128)(2,1)S(1)} %get-tuple-element.45), channel_id=1, source_target_pairs={{256,259},{257,256},{258,257},{259,258},{260,263},{261,260},{262,2... | collective-permute-start | bytes 688136 | tf_op jit(solution)/shard_map/in_reduce/ppermute | solution.py:237
  58.6 17.2 %collective-permute-start.9 = (bf16[128,896]{1,0:T(8,128)(2,1)S(1)}, bf16[128,896]{1,0:T(8,128)(2,1)}, u32[]{:S(2)}, u32[]{:S(2)}) collective-permute-start(bf16[128,896]{1,0:T(8,128)(2,1)S(1)} %get-tuple-element.43), channel_id=1, source_target_pairs={{256,258},{257,259},{258,256},{259,257},{260,262},{261,263},{262,2... | collective-permute-start | bytes 688136 | tf_op jit(solution)/shard_map/in_reduce/ppermute | solution.py:237
  67.0 11.4 %collective-permute-start.7 = (bf16[32,1024]{1,0:T(8,128)(2,1)S(1)}, bf16[32,1024]{1,0:T(8,128)(2,1)S(1)}, u32[]{:S(2)}, u32[]{:S(2)}) collective-permute-start(bf16[32,1024]{1,0:T(8,128)(2,1)S(1)} %get-tuple-element.41), channel_id=1, source_target_pairs={{0,16},{16,0},{32,48},{48,32},{1,17},{17,1},{33,49},{49,33},{2,18}... | collective-permute-start | bytes 196616 | tf_op jit(solution)/shard_map/zh_first/ppermute | solution.py:333
  78.4 9.6 %collective-permute-start.12 = (bf16[16,1024]{1,0:T(8,128)(2,1)S(1)}, bf16[16,1024]{1,0:T(8,128)(2,1)S(1)}, u32[]{:S(2)}, u32[]{:S(2)}) collective-permute-start(bf16[16,1024]{1,0:T(8,128)(2,1)S(1)} %get-tuple-element.51), channel_id=1, source_target_pairs={{0,48},{48,0},{16,32},{32,16},{1,49},{49,1},{17,33},{33,17},{2,50}... | collective-permute-start | bytes 98312 | tf_op jit(solution)/shard_map/zh_second/ppermute | solution.py:337
